TPU v7x, 512 devices: a whole 4x4x16 slice. The times are simulated.
512 devices in a mesh: tile: 32 (over y, z_hi, core), mem: 16 (over x, z_lo).
Axes of the slice: x: 4, y: 4, z: 16 (z_hi: 4, z_lo: 4; z = z_hi * 4 + z_lo), core: 2. Of those that a mesh axis runs over, the one named last changes fastest.
Arguments:
- alpha: float32 [64, 4, 512, 512], P('mem', None, 'tile'), may hold values from -6 to 6
- perturbs: bfloat16 [64, 4, 512, 512], P('mem', None, 'tile'), may hold values from -6 to 6
- diff_x: float32 [64], P('mem'), may hold values from 0.04 to 0.24
- diff_y: float32 [64], P('mem'), may hold values from 0.04 to 0.24
- land_mask: int32 [512, 512], P('tile'), may hold values 0 or 1
- obs_tile: int32 [131072, 1], P(('tile', 'mem')), may hold values from 0 to 31; in each aligned block of 256 rows (0 to 255, 256 to 511, ...) at most 16 rows name the same one
- obs_row: int32 [131072], P(('tile', 'mem')), may hold values from 0 to 14
- obs_col: int32 [131072], P(('tile', 'mem')), may hold values from 0 to 510
- obs_lev: int32 [131072], P(('tile', 'mem')), may hold values from 0 to 3
- obs_weights: float32 [4, 131072], P(None, ('tile', 'mem')), may hold values from 0.1 to 1
- obs_value: float32 [131072], P(('tile', 'mem')), may hold values from -6 to 6
- obs_rinv: float32 [131072], P(('tile', 'mem')), may hold values from 1 to 16
Outputs:
- grad: float32 [64, 4, 512, 512], P('mem', None, 'tile')
- hofx: float32 [131072], P(('tile', 'mem'))
Inputs may be any that keep to these rules, and one draw needn't show every extreme that they name: `obs_tile`: among the 256 observations of one device (aligned blocks of rows) no tile is named more than 16 times, a bound that some block reaches.
All inputs are finite; a program needn't handle non-finite values. No bound on the sum of `land_mask` on one device may be relied on, other than what follows from the above.
Results may differ from a plain program's by a relative error of at most 0.00055.
Values sent between devices are 32-bit elements; how exact they have to be, the bound alone decides.
No kernel may reach another device: no remote copies, remote signals or barrier semaphores. Data moves between devices by JAX's collectives and lax.ppermute only.
A program may use at most 64 MiB of HBM per device.

v0:
```python
import jax
import jax.numpy as jnp
from jax import lax
from jax.sharding import PartitionSpec as P

STEPS = 8


def extended_2(block, sides, width):
    for axis, dim in sides:
        count = lax.axis_size(axis)
        forward = [(i, i + 1) for i in range(count - 1)]
        backward = [(target, source) for source, target in forward]
        low = lax.ppermute(
            lax.slice_in_dim(block, block.shape[dim] - width, None, axis=dim), axis, forward
        )
        high = lax.ppermute(lax.slice_in_dim(block, 0, width, axis=dim), axis, backward)
        block = jnp.concatenate([low, block, high], axis=dim)
    return block


def stencil(extended, rate_x, rate_y):
    core = extended[:, :, 1:-1]
    padded = jnp.pad(core, ((0, 0), (0, 0), (0, 0), (1, 1)))
    across = padded[..., 2:] + padded[..., :-2] - 2.0 * core
    along = extended[:, :, 2:] + extended[:, :, :-2] - 2.0 * core
    return core + rate_x * across + rate_y * along


def smooth(field, rate_x, rate_y):
    for step in range(STEPS):
        extended = extended_2(field, (("tile", 2),), 1)
        field = stencil(extended, rate_x, rate_y)
    return field


def corner_index(ints, rows, cols):
    base = (ints[2] * rows + ints[0]) * cols + ints[1]
    return (base, base + 1, base + cols, base + cols + 1)


def interpolate(field, ints, floats):
    levels, rows, cols = field.shape
    flat = field.reshape(-1)
    corners = corner_index(ints, rows, cols)
    result = floats[0] * flat[corners[0]]
    for k in range(1, 4):
        result = result + floats[k] * flat[corners[k]]
    return result


def spread(shape, ints, floats, dep):
    levels, rows, cols = shape
    corners = corner_index(ints, rows, cols)
    adjoint = jnp.zeros((levels * rows * cols,), jnp.float32)
    for k in range(4):
        adjoint = adjoint.at[corners[k]].add(floats[k] * dep)
    return adjoint.reshape(shape)


def on_device(
    alpha,
    perturbs,
    diff_x,
    diff_y,
    land_mask,
    obs_tile,
    obs_row,
    obs_col,
    obs_lev,
    obs_weights,
    obs_value,
    obs_rinv,
):
    land = land_mask.astype(jnp.float32)[None, None]
    rate_x = diff_x[:, None, None, None]
    rate_y = diff_y[:, None, None, None]
    factor = (lax.axis_size("mem") * alpha.shape[0] - 1) ** (-0.5)
    shape = alpha.shape[1:]
    local = land * smooth(land * alpha, rate_x, rate_y)
    partial_value = jnp.sum(perturbs * local, axis=0)
    tiles = lax.axis_size("tile")
    count = obs_row.shape[0]
    slots = 2 * count // tiles
    target = obs_tile[:, 0]
    onehot = (target[:, None] == jnp.arange(tiles, dtype=jnp.int32)[None]).astype(jnp.int32)
    before = jnp.cumsum(onehot, axis=0) - onehot
    place = jnp.sum(before * onehot, axis=1)
    where = target * slots + place
    int_rows = jnp.stack([obs_row, obs_col, obs_lev, jnp.ones_like(obs_row)])
    float_rows = jnp.concatenate([obs_weights, obs_value[None], obs_rinv[None]], axis=0)
    int_send = (
        jnp.zeros((4, tiles * slots), jnp.int32).at[:, where].set(int_rows).reshape(4, tiles, slots)
    )
    float_send = (
        jnp.zeros((6, tiles * slots), jnp.float32)
        .at[:, where]
        .set(float_rows)
        .reshape(6, tiles, slots)
    )
    int_recv, float_recv = (
        lax.all_to_all(int_send, "tile", split_axis=1, concat_axis=1, tiled=True),
        lax.all_to_all(float_send, "tile", split_axis=1, concat_axis=1, tiled=True),
    )
    incr = factor * lax.psum(partial_value, "mem")
    ints = int_recv.reshape(4, -1)
    floats = float_recv.reshape(6, -1)
    hofx_slots = interpolate(incr, ints, floats)
    dep = ints[3].astype(jnp.float32) * floats[5] * (hofx_slots - floats[4])
    adjoint = lax.psum(spread(shape, ints, floats, dep), "mem")
    returned = lax.all_to_all(
        hofx_slots.reshape(tiles, slots), "tile", split_axis=0, concat_axis=0, tiled=True
    )
    hofx = returned.reshape(-1)[where]
    source = perturbs * adjoint[None]
    grad = alpha + factor * land * smooth(land * source, rate_x, rate_y)
    return (grad, hofx)


def solution(mesh):
    return jax.shard_map(
        on_device,
        mesh=mesh,
        in_specs=(
            P("mem", None, "tile", None),
            P("mem", None, "tile", None),
            P("mem"),
            P("mem"),
            P("tile", None),
            P(("tile", "mem"), None),
            P(("tile", "mem")),
            P(("tile", "mem")),
            P(("tile", "mem")),
            P(None, ("tile", "mem")),
            P(("tile", "mem")),
            P(("tile", "mem")),
        ),
        out_specs=(P("mem", None, "tile", None), P(("tile", "mem"))),
        check_vma=False,
    )
```

profile of v0, /device:TPU:1, one launch (start us, length us, event | category | flops | bytes accessed | tf_op | source)
XLA Modules:
  0.0 628.3 jit_solution(14111333681414554375)
XLA Ops:
  9.1 8.8 %collective-permute-start = (f32[4,4,1,512]{3,2,1,0:T(1,128)S(1)}, f32[4,4,1,512]{3,2,1,0:T(1,128)S(1)}, u32[]{:S(2)}, u32[]{:S(2)}) collective-permute-start(f32[4,4,1,512]{3,2,1,0:T(1,128)S(1)} %get-tuple-element.37), channel_id=1, source_target_pairs={{16,0},{32,16},{48,32},{64,48},{80,64},{96,80},{112,96},{128,112},... | collective-permute-start | bytes 98312 | tf_op jit(solution)/shard_map/ppermute | solution.py:17
  17.9 3.3 collective-permute-start.1
  26.5 16.3 %all-to-all-start = ((s32[4,32,16]{2,0,1:T(4,128)}), s32[4,32,16]{2,0,1:T(4,128)S(1)}, u32[]{:S(2)}, u32[]{:S(2)}) async-start(s32[4,32,16]{2,0,1:T(4,128)} %copy.27), calls=%async_computation | async-start | bytes 131072 | tf_op jit(solution)/shard_map/all_to_all | solution.py:102
  45.6 7.3 %collective-permute-start.3 = (f32[4,4,1,512]{3,2,1,0:T(1,128)S(1)}, f32[4,4,1,512]{3,2,1,0:T(1,128)S(1)}, u32[]{:S(2)}, u32[]{:S(2)}) collective-permute-start(f32[4,4,1,512]{3,2,1,0:T(1,128)S(1)} %get-tuple-element.36), channel_id=1, source_target_pairs={{0,16},{16,32},{32,48},{48,64},{64,80},{80,96},{96,112},{112,128},... | collective-permute-start | bytes 98312 | tf_op jit(solution)/shard_map/ppermute | solution.py:14
  58.5 7.5 %collective-permute-start.5 = (f32[4,4,1,512]{3,2,1,0:T(1,128)S(1)}, f32[4,4,1,512]{3,2,1,0:T(1,128)S(1)}, u32[]{:S(2)}, u32[]{:S(2)}) collective-permute-start(f32[4,4,1,512]{3,2,1,0:T(1,128)S(1)} %get-tuple-element.34), channel_id=1, source_target_pairs={{0,16},{16,32},{32,48},{48,64},{64,80},{80,96},{96,112},{112,128},... | collective-permute-start | bytes 98312 | tf_op jit(solution)/shard_map/ppermute | solution.py:14
  66.1 14.4 %all-to-all-start.1 = ((f32[6,32,16]{2,0,1:T(8,128)}), f32[6,32,16]{2,0,1:T(8,128)S(1)}, u32[]{:S(2)}, u32[]{:S(2)}) async-start(f32[6,32,16]{2,0,1:T(8,128)} %copy.29), calls=%async_computation.1 | async-start | bytes 262144 | tf_op jit(solution)/shard_map/all_to_all | solution.py:103
  83.4 7.3 %collective-permute-start.7 = (f32[4,4,1,512]{3,2,1,0:T(1,128)S(1)}, f32[4,4,1,512]{3,2,1,0:T(1,128)S(1)}, u32[]{:S(2)}, u32[]{:S(2)}) collective-permute-start(f32[4,4,1,512]{3,2,1,0:T(1,128)S(1)} %get-tuple-element.32), channel_id=1, source_target_pairs={{0,16},{16,32},{32,48},{48,64},{64,80},{80,96},{96,112},{112,128},... | collective-permute-start | bytes 98312 | tf_op jit(solution)/shard_map/ppermute | solution.py:14
  95.4 7.5 %collective-permute-start.9 = (f32[4,4,1,512]{3,2,1,0:T(1,128)S(1)}, f32[4,4,1,512]{3,2,1,0:T(1,128)S(1)}, u32[]{:S(2)}, u32[]{:S(2)}) collective-permute-start(f32[4,4,1,512]{3,2,1,0:T(1,128)S(1)} %get-tuple-element.30), channel_id=1, source_target_pairs={{0,16},{16,32},{32,48},{48,64},{64,80},{80,96},{96,112},{112,128},... | collective-permute-start | bytes 98312 | tf_op jit(solution)/shard_map/ppermute | solution.py:14
  106.5 8.1 %collective-permute-start.11 = (f32[4,4,1,512]{3,2,1,0:T(1,128)S(1)}, f32[4,4,1,512]{3,2,1,0:T(1,128)S(1)}, u32[]{:S(2)}, u32[]{:S(2)}) collective-permute-start(f32[4,4,1,512]{3,2,1,0:T(1,128)S(1)} %get-tuple-element.28), channel_id=1, source_target_pairs={{0,16},{16,32},{32,48},{48,64},{64,80},{80,96},{96,112},{112,128},... | collective-permute-start | bytes 98312 | tf_op jit(solution)/shard_map/ppermute | solution.py:14
  118.2 8.1 %collective-permute-start.13 = (f32[4,4,1,512]{3,2,1,0:T(1,128)S(1)}, f32[4,4,1,512]{3,2,1,0:T(1,128)S(1)}, u32[]{:S(2)}, u32[]{:S(2)}) collective-permute-start(f32[4,4,1,512]{3,2,1,0:T(1,128)S(1)} %get-tuple-element.26), channel_id=1, source_target_pairs={{0,16},{16,32},{32,48},{48,64},{64,80},{80,96},{96,112},{112,128},... | collective-permute-start | bytes 98312 | tf_op jit(solution)/shard_map/ppermute | solution.py:14
  129.9 8.1 %collective-permute-start.15 = (f32[4,4,1,512]{3,2,1,0:T(1,128)S(1)}, f32[4,4,1,512]{3,2,1,0:T(1,128)S(1)}, u32[]{:S(2)}, u32[]{:S(2)}) collective-permute-start(f32[4,4,1,512]{3,2,1,0:T(1,128)S(1)} %get-tuple-element.24), channel_id=1, source_target_pairs={{0,16},{16,32},{32,48},{48,64},{64,80},{80,96},{96,112},{112,128},... | collective-permute-start | bytes 98312 | tf_op jit(solution)/shard_map/ppermute | solution.py:14
  141.2 161.8 %all-reduce.19.cloned.1.call-done = f32[4,16,512]{2,1,0:T(8,128)} async-done(((f32[4,16,512]{2,1,0:T(8,128)}), f32[4,16,512]{2,1,0:T(8,128)}) %all-reduce.19.cloned.1.call-update) | async-done | bytes 131088 | tf_op jit(solution)/shard_map/psum | solution.py:105
  304.0 3.1 gather_fusion
  307.1 3.1 gather_fusion.1
  310.3 3.1 gather_fusion.2
  313.4 3.1 gather_fusion.3
  316.6 3.4 scatter_custom_fusion.2
  320.0 3.6 scatter_fusion
  323.6 3.6 scatter_fusion.1
  327.1 3.6 scatter_fusion.2
  331.4 168.0 %all-reduce.21.cloned.1.call-done = f32[4,16,512]{2,1,0:T(8,128)} async-done(((f32[4,16,512]{2,1,0:T(8,128)}), f32[4,16,512]{2,1,0:T(8,128)}) %all-reduce.21.cloned.1.call-update) | async-done | bytes 131088 | tf_op jit(solution)/shard_map/psum | solution.py:110
  500.4 13.4 %collective-permute-start.16 = (f32[4,4,1,512]{3,2,1,0:T(1,128)S(1)}, f32[4,4,1,512]{3,2,1,0:T(1,128)S(1)}, u32[]{:S(2)}, u32[]{:S(2)}) collective-permute-start(f32[4,4,1,512]{3,2,1,0:T(1,128)S(1)} %get-tuple-element.21), channel_id=1, source_target_pairs={{16,0},{32,16},{48,32},{64,48},{80,64},{96,80},{112,96},{128,112},... | collective-permute-start | bytes 98312 | tf_op jit(solution)/shard_map/ppermute | solution.py:17
  513.8 7.1 %collective-permute-start.17 = (f32[4,4,1,512]{3,2,1,0:T(1,128)S(1)}, f32[4,4,1,512]{3,2,1,0:T(1,128)S(1)}, u32[]{:S(2)}, u32[]{:S(2)}) collective-permute-start(f32[4,4,1,512]{3,2,1,0:T(1,128)S(1)} %get-tuple-element.22), channel_id=1, source_target_pairs={{0,16},{16,32},{32,48},{48,64},{64,80},{80,96},{96,112},{112,128},... | collective-permute-start | bytes 98312 | tf_op jit(solution)/shard_map/ppermute | solution.py:14
  524.4 8.2 %collective-permute-start.19 = (f32[4,4,1,512]{3,2,1,0:T(1,128)S(1)}, f32[4,4,1,512]{3,2,1,0:T(1,128)S(1)}, u32[]{:S(2)}, u32[]{:S(2)}) collective-permute-start(f32[4,4,1,512]{3,2,1,0:T(1,128)S(1)} %get-tuple-element.20), channel_id=1, source_target_pairs={{0,16},{16,32},{32,48},{48,64},{64,80},{80,96},{96,112},{112,128},... | collective-permute-start | bytes 98312 | tf_op jit(solution)/shard_map/ppermute | solution.py:14
  536.2 8.1 %collective-permute-start.21 = (f32[4,4,1,512]{3,2,1,0:T(1,128)S(1)}, f32[4,4,1,512]{3,2,1,0:T(1,128)S(1)}, u32[]{:S(2)}, u32[]{:S(2)}) collective-permute-start(f32[4,4,1,512]{3,2,1,0:T(1,128)S(1)} %get-tuple-element.18), channel_id=1, source_target_pairs={{0,16},{16,32},{32,48},{48,64},{64,80},{80,96},{96,112},{112,128},... | collective-permute-start | bytes 98312 | tf_op jit(solution)/shard_map/ppermute | solution.py:14
  547.9 8.1 %collective-permute-start.23 = (f32[4,4,1,512]{3,2,1,0:T(1,128)S(1)}, f32[4,4,1,512]{3,2,1,0:T(1,128)S(1)}, u32[]{:S(2)}, u32[]{:S(2)}) collective-permute-start(f32[4,4,1,512]{3,2,1,0:T(1,128)S(1)} %get-tuple-element.16), channel_id=1, source_target_pairs={{0,16},{16,32},{32,48},{48,64},{64,80},{80,96},{96,112},{112,128},... | collective-permute-start | bytes 98312 | tf_op jit(solution)/shard_map/ppermute | solution.py:14
  559.6 8.1 %collective-permute-start.25 = (f32[4,4,1,512]{3,2,1,0:T(1,128)S(1)}, f32[4,4,1,512]{3,2,1,0:T(1,128)S(1)}, u32[]{:S(2)}, u32[]{:S(2)}) collective-permute-start(f32[4,4,1,512]{3,2,1,0:T(1,128)S(1)} %get-tuple-element.14), channel_id=1, source_target_pairs={{0,16},{16,32},{32,48},{48,64},{64,80},{80,96},{96,112},{112,128},... | collective-permute-start | bytes 98312 | tf_op jit(solution)/shard_map/ppermute | solution.py:14
  571.8 8.4 %collective-permute-start.27 = (f32[4,4,1,512]{3,2,1,0:T(1,128)S(1)}, f32[4,4,1,512]{3,2,1,0:T(1,128)S(1)}, u32[]{:S(2)}, u32[]{:S(2)}) collective-permute-start(f32[4,4,1,512]{3,2,1,0:T(1,128)S(1)} %get-tuple-element.12), channel_id=1, source_target_pairs={{0,16},{16,32},{32,48},{48,64},{64,80},{80,96},{96,112},{112,128},... | collective-permute-start | bytes 98312 | tf_op jit(solution)/shard_map/ppermute | solution.py:14
  583.7 8.9 %collective-permute-start.29 = (f32[4,4,1,512]{3,2,1,0:T(1,128)S(1)}, f32[4,4,1,512]{3,2,1,0:T(1,128)S(1)}, u32[]{:S(2)}, u32[]{:S(2)}) collective-permute-start(f32[4,4,1,512]{3,2,1,0:T(1,128)S(1)} %get-tuple-element.10), channel_id=1, source_target_pairs={{0,16},{16,32},{32,48},{48,64},{64,80},{80,96},{96,112},{112,128},... | collective-permute-start | bytes 98312 | tf_op jit(solution)/shard_map/ppermute | solution.py:14
  593.3 9.0 %all-to-all-start.2 = ((f32[32,1,16]{2,1,0:T(1,128)}), f32[32,1,16]{2,1,0:T(1,128)S(1)}, u32[]{:S(2)}, u32[]{:S(2)}) async-start(f32[32,1,16]{2,1,0:T(1,128)} %bitcast.22), calls=%async_computation.2 | async-start | bytes 32768 | tf_op jit(solution)/shard_map/all_to_all | solution.py:111
  605.1 7.3 %collective-permute-start.31 = (f32[4,4,1,512]{3,2,1,0:T(1,128)S(1)}, f32[4,4,1,512]{3,2,1,0:T(1,128)S(1)}, u32[]{:S(2)}, u32[]{:S(2)}) collective-permute-start(f32[4,4,1,512]{3,2,1,0:T(1,128)S(1)} %get-tuple-element.8), channel_id=1, source_target_pairs={{0,16},{16,32},{32,48},{48,64},{64,80},{80,96},{96,112},{112,128},... | collective-permute-start | bytes 98312 | tf_op jit(solution)/shard_map/ppermute | solution.py:14
  612.4 3.9 all-to-all-done.2
  (162 shorter events, 69.6 us)
Async XLA Ops:
  9.1 33.7 %collective-permute-start = (f32[4,4,1,512]{3,2,1,0:T(1,128)S(1)}, f32[4,4,1,512]{3,2,1,0:T(1,128)S(1)}, u32[]{:S(2)}, u32[]{:S(2)}) collective-permute-start(f32[4,4,1,512]{3,2,1,0:T(1,128)S(1)} %get-tuple-element.37), channel_id=1, source_target_pairs={{16,0},{32,16},{48,32},{64,48},{80,64},{96,80},{112,96},{128,112},... | collective-permute-start | bytes 98312 | tf_op jit(solution)/shard_map/ppermute | solution.py:17
  17.9 24.9 %collective-permute-start.1 = (f32[4,4,1,512]{3,2,1,0:T(1,128)S(1)}, f32[4,4,1,512]{3,2,1,0:T(1,128)S(1)}, u32[]{:S(2)}, u32[]{:S(2)}) collective-permute-start(f32[4,4,1,512]{3,2,1,0:T(1,128)S(1)} %get-tuple-element.38), channel_id=1, source_target_pairs={{0,16},{16,32},{32,48},{48,64},{64,80},{80,96},{96,112},{112,128},... | collective-permute-start | bytes 98312 | tf_op jit(solution)/shard_map/ppermute | solution.py:14
  26.5 39.6 %all-to-all-start = ((s32[4,32,16]{2,0,1:T(4,128)}), s32[4,32,16]{2,0,1:T(4,128)S(1)}, u32[]{:S(2)}, u32[]{:S(2)}) async-start(s32[4,32,16]{2,0,1:T(4,128)} %copy.27), calls=%async_computation | async-start | bytes 131072 | tf_op jit(solution)/shard_map/all_to_all | solution.py:102
  43.5 12.5 %collective-permute-start.2 = (f32[4,4,1,512]{3,2,1,0:T(1,128)S(1)}, f32[4,4,1,512]{3,2,1,0:T(1,128)S(1)}, u32[]{:S(2)}, u32[]{:S(2)}) collective-permute-start(f32[4,4,1,512]{3,2,1,0:T(1,128)S(1)} %get-tuple-element.35), channel_id=1, source_target_pairs={{16,0},{32,16},{48,32},{64,48},{80,64},{96,80},{112,96},{128,112},... | collective-permute-start | bytes 98312 | tf_op jit(solution)/shard_map/ppermute | solution.py:17
  45.6 10.3 %collective-permute-start.3 = (f32[4,4,1,512]{3,2,1,0:T(1,128)S(1)}, f32[4,4,1,512]{3,2,1,0:T(1,128)S(1)}, u32[]{:S(2)}, u32[]{:S(2)}) collective-permute-start(f32[4,4,1,512]{3,2,1,0:T(1,128)S(1)} %get-tuple-element.36), channel_id=1, source_target_pairs={{0,16},{16,32},{32,48},{48,64},{64,80},{80,96},{96,112},{112,128},... | collective-permute-start | bytes 98312 | tf_op jit(solution)/shard_map/ppermute | solution.py:14
  56.6 24.1 %collective-permute-start.4 = (f32[4,4,1,512]{3,2,1,0:T(1,128)S(1)}, f32[4,4,1,512]{3,2,1,0:T(1,128)S(1)}, u32[]{:S(2)}, u32[]{:S(2)}) collective-permute-start(f32[4,4,1,512]{3,2,1,0:T(1,128)S(1)} %get-tuple-element.33), channel_id=1, source_target_pairs={{16,0},{32,16},{48,32},{64,48},{80,64},{96,80},{112,96},{128,112},... | collective-permute-start | bytes 98312 | tf_op jit(solution)/shard_map/ppermute | solution.py:17
  58.5 22.2 %collective-permute-start.5 = (f32[4,4,1,512]{3,2,1,0:T(1,128)S(1)}, f32[4,4,1,512]{3,2,1,0:T(1,128)S(1)}, u32[]{:S(2)}, u32[]{:S(2)}) collective-permute-start(f32[4,4,1,512]{3,2,1,0:T(1,128)S(1)} %get-tuple-element.34), channel_id=1, source_target_pairs={{0,16},{16,32},{32,48},{48,64},{64,80},{80,96},{96,112},{112,128},... | collective-permute-start | bytes 98312 | tf_op jit(solution)/shard_map/ppermute | solution.py:14
  66.1 74.4 %all-to-all-start.1 = ((f32[6,32,16]{2,0,1:T(8,128)}), f32[6,32,16]{2,0,1:T(8,128)S(1)}, u32[]{:S(2)}, u32[]{:S(2)}) async-start(f32[6,32,16]{2,0,1:T(8,128)} %copy.29), calls=%async_computation.1 | async-start | bytes 262144 | tf_op jit(solution)/shard_map/all_to_all | solution.py:103
  80.4 222.5 %all-reduce.19.cloned.1.call-start = ((), (), s32[]{:S(2)}) async-start(), calls=%async_computation.3 | async-start | bytes 262144 | tf_op jit(solution)/shard_map/psum | solution.py:105
  81.3 11.6 %collective-permute-start.6 = (f32[4,4,1,512]{3,2,1,0:T(1,128)S(1)}, f32[4,4,1,512]{3,2,1,0:T(1,128)S(1)}, u32[]{:S(2)}, u32[]{:S(2)}) collective-permute-start(f32[4,4,1,512]{3,2,1,0:T(1,128)S(1)} %get-tuple-element.31), channel_id=1, source_target_pairs={{16,0},{32,16},{48,32},{64,48},{80,64},{96,80},{112,96},{128,112},... | collective-permute-start | bytes 98312 | tf_op jit(solution)/shard_map/ppermute | solution.py:17
  83.4 9.4 %collective-permute-start.7 = (f32[4,4,1,512]{3,2,1,0:T(1,128)S(1)}, f32[4,4,1,512]{3,2,1,0:T(1,128)S(1)}, u32[]{:S(2)}, u32[]{:S(2)}) collective-permute-start(f32[4,4,1,512]{3,2,1,0:T(1,128)S(1)} %get-tuple-element.32), channel_id=1, source_target_pairs={{0,16},{16,32},{32,48},{48,64},{64,80},{80,96},{96,112},{112,128},... | collective-permute-start | bytes 98312 | tf_op jit(solution)/shard_map/ppermute | solution.py:14
  93.5 10.2 %collective-permute-start.8 = (f32[4,4,1,512]{3,2,1,0:T(1,128)S(1)}, f32[4,4,1,512]{3,2,1,0:T(1,128)S(1)}, u32[]{:S(2)}, u32[]{:S(2)}) collective-permute-start(f32[4,4,1,512]{3,2,1,0:T(1,128)S(1)} %get-tuple-element.29), channel_id=1, source_target_pairs={{16,0},{32,16},{48,32},{64,48},{80,64},{96,80},{112,96},{128,112},... | collective-permute-start | bytes 98312 | tf_op jit(solution)/shard_map/ppermute | solution.py:17
  104.6 10.8 %collective-permute-start.10 = (f32[4,4,1,512]{3,2,1,0:T(1,128)S(1)}, f32[4,4,1,512]{3,2,1,0:T(1,128)S(1)}, u32[]{:S(2)}, u32[]{:S(2)}) collective-permute-start(f32[4,4,1,512]{3,2,1,0:T(1,128)S(1)} %get-tuple-element.27), channel_id=1, source_target_pairs={{16,0},{32,16},{48,32},{64,48},{80,64},{96,80},{112,96},{128,112},... | collective-permute-start | bytes 98312 | tf_op jit(solution)/shard_map/ppermute | solution.py:17
  106.5 9.1 %collective-permute-start.11 = (f32[4,4,1,512]{3,2,1,0:T(1,128)S(1)}, f32[4,4,1,512]{3,2,1,0:T(1,128)S(1)}, u32[]{:S(2)}, u32[]{:S(2)}) collective-permute-start(f32[4,4,1,512]{3,2,1,0:T(1,128)S(1)} %get-tuple-element.28), channel_id=1, source_target_pairs={{0,16},{16,32},{32,48},{48,64},{64,80},{80,96},{96,112},{112,128},... | collective-permute-start | bytes 98312 | tf_op jit(solution)/shard_map/ppermute | solution.py:14
  116.3 10.8 %collective-permute-start.12 = (f32[4,4,1,512]{3,2,1,0:T(1,128)S(1)}, f32[4,4,1,512]{3,2,1,0:T(1,128)S(1)}, u32[]{:S(2)}, u32[]{:S(2)}) collective-permute-start(f32[4,4,1,512]{3,2,1,0:T(1,128)S(1)} %get-tuple-element.25), channel_id=1, source_target_pairs={{16,0},{32,16},{48,32},{64,48},{80,64},{96,80},{112,96},{128,112},... | collective-permute-start | bytes 98312 | tf_op jit(solution)/shard_map/ppermute | solution.py:17
  118.2 9.1 %collective-permute-start.13 = (f32[4,4,1,512]{3,2,1,0:T(1,128)S(1)}, f32[4,4,1,512]{3,2,1,0:T(1,128)S(1)}, u32[]{:S(2)}, u32[]{:S(2)}) collective-permute-start(f32[4,4,1,512]{3,2,1,0:T(1,128)S(1)} %get-tuple-element.26), channel_id=1, source_target_pairs={{0,16},{16,32},{32,48},{48,64},{64,80},{80,96},{96,112},{112,128},... | collective-permute-start | bytes 98312 | tf_op jit(solution)/shard_map/ppermute | solution.py:14
  128.0 10.8 %collective-permute-start.14 = (f32[4,4,1,512]{3,2,1,0:T(1,128)S(1)}, f32[4,4,1,512]{3,2,1,0:T(1,128)S(1)}, u32[]{:S(2)}, u32[]{:S(2)}) collective-permute-start(f32[4,4,1,512]{3,2,1,0:T(1,128)S(1)} %get-tuple-element.23), channel_id=1, source_target_pairs={{16,0},{32,16},{48,32},{64,48},{80,64},{96,80},{112,96},{128,112},... | collective-permute-start | bytes 98312 | tf_op jit(solution)/shard_map/ppermute | solution.py:17
  140.3 359.1 %all-reduce.21.cloned.1.call-start = ((), (), s32[]{:S(2)}) async-start(), calls=%async_computation.4 | async-start | bytes 262144 | tf_op jit(solution)/shard_map/psum | solution.py:110
  500.4 20.5 %collective-permute-start.16 = (f32[4,4,1,512]{3,2,1,0:T(1,128)S(1)}, f32[4,4,1,512]{3,2,1,0:T(1,128)S(1)}, u32[]{:S(2)}, u32[]{:S(2)}) collective-permute-start(f32[4,4,1,512]{3,2,1,0:T(1,128)S(1)} %get-tuple-element.21), channel_id=1, source_target_pairs={{16,0},{32,16},{48,32},{64,48},{80,64},{96,80},{112,96},{128,112},... | collective-permute-start | bytes 98312 | tf_op jit(solution)/shard_map/ppermute | solution.py:17
  522.5 10.1 %collective-permute-start.18 = (f32[4,4,1,512]{3,2,1,0:T(1,128)S(1)}, f32[4,4,1,512]{3,2,1,0:T(1,128)S(1)}, u32[]{:S(2)}, u32[]{:S(2)}) collective-permute-start(f32[4,4,1,512]{3,2,1,0:T(1,128)S(1)} %get-tuple-element.19), channel_id=1, source_target_pairs={{16,0},{32,16},{48,32},{64,48},{80,64},{96,80},{112,96},{128,112},... | collective-permute-start | bytes 98312 | tf_op jit(solution)/shard_map/ppermute | solution.py:17
  524.4 9.2 %collective-permute-start.19 = (f32[4,4,1,512]{3,2,1,0:T(1,128)S(1)}, f32[4,4,1,512]{3,2,1,0:T(1,128)S(1)}, u32[]{:S(2)}, u32[]{:S(2)}) collective-permute-start(f32[4,4,1,512]{3,2,1,0:T(1,128)S(1)} %get-tuple-element.20), channel_id=1, source_target_pairs={{0,16},{16,32},{32,48},{48,64},{64,80},{80,96},{96,112},{112,128},... | collective-permute-start | bytes 98312 | tf_op jit(solution)/shard_map/ppermute | solution.py:14
  534.2 10.1 %collective-permute-start.20 = (f32[4,4,1,512]{3,2,1,0:T(1,128)S(1)}, f32[4,4,1,512]{3,2,1,0:T(1,128)S(1)}, u32[]{:S(2)}, u32[]{:S(2)}) collective-permute-start(f32[4,4,1,512]{3,2,1,0:T(1,128)S(1)} %get-tuple-element.17), channel_id=1, source_target_pairs={{16,0},{32,16},{48,32},{64,48},{80,64},{96,80},{112,96},{128,112},... | collective-permute-start | bytes 98312 | tf_op jit(solution)/shard_map/ppermute | solution.py:17
  545.9 10.1 %collective-permute-start.22 = (f32[4,4,1,512]{3,2,1,0:T(1,128)S(1)}, f32[4,4,1,512]{3,2,1,0:T(1,128)S(1)}, u32[]{:S(2)}, u32[]{:S(2)}) collective-permute-start(f32[4,4,1,512]{3,2,1,0:T(1,128)S(1)} %get-tuple-element.15), channel_id=1, source_target_pairs={{16,0},{32,16},{48,32},{64,48},{80,64},{96,80},{112,96},{128,112},... | collective-permute-start | bytes 98312 | tf_op jit(solution)/shard_map/ppermute | solution.py:17
  557.6 10.1 %collective-permute-start.24 = (f32[4,4,1,512]{3,2,1,0:T(1,128)S(1)}, f32[4,4,1,512]{3,2,1,0:T(1,128)S(1)}, u32[]{:S(2)}, u32[]{:S(2)}) collective-permute-start(f32[4,4,1,512]{3,2,1,0:T(1,128)S(1)} %get-tuple-element.13), channel_id=1, source_target_pairs={{16,0},{32,16},{48,32},{64,48},{80,64},{96,80},{112,96},{128,112},... | collective-permute-start | bytes 98312 | tf_op jit(solution)/shard_map/ppermute | solution.py:17
  559.6 9.7 %collective-permute-start.25 = (f32[4,4,1,512]{3,2,1,0:T(1,128)S(1)}, f32[4,4,1,512]{3,2,1,0:T(1,128)S(1)}, u32[]{:S(2)}, u32[]{:S(2)}) collective-permute-start(f32[4,4,1,512]{3,2,1,0:T(1,128)S(1)} %get-tuple-element.14), channel_id=1, source_target_pairs={{0,16},{16,32},{32,48},{48,64},{64,80},{80,96},{96,112},{112,128},... | collective-permute-start | bytes 98312 | tf_op jit(solution)/shard_map/ppermute | solution.py:14
  569.9 10.8 %collective-permute-start.26 = (f32[4,4,1,512]{3,2,1,0:T(1,128)S(1)}, f32[4,4,1,512]{3,2,1,0:T(1,128)S(1)}, u32[]{:S(2)}, u32[]{:S(2)}) collective-permute-start(f32[4,4,1,512]{3,2,1,0:T(1,128)S(1)} %get-tuple-element.11), channel_id=1, source_target_pairs={{16,0},{32,16},{48,32},{64,48},{80,64},{96,80},{112,96},{128,112},... | collective-permute-start | bytes 98312 | tf_op jit(solution)/shard_map/ppermute | solution.py:17
  571.8 9.4 %collective-permute-start.27 = (f32[4,4,1,512]{3,2,1,0:T(1,128)S(1)}, f32[4,4,1,512]{3,2,1,0:T(1,128)S(1)}, u32[]{:S(2)}, u32[]{:S(2)}) collective-permute-start(f32[4,4,1,512]{3,2,1,0:T(1,128)S(1)} %get-tuple-element.12), channel_id=1, source_target_pairs={{0,16},{16,32},{32,48},{48,64},{64,80},{80,96},{96,112},{112,128},... | collective-permute-start | bytes 98312 | tf_op jit(solution)/shard_map/ppermute | solution.py:14
  581.8 20.5 %collective-permute-start.28 = (f32[4,4,1,512]{3,2,1,0:T(1,128)S(1)}, f32[4,4,1,512]{3,2,1,0:T(1,128)S(1)}, u32[]{:S(2)}, u32[]{:S(2)}) collective-permute-start(f32[4,4,1,512]{3,2,1,0:T(1,128)S(1)} %get-tuple-element.9), channel_id=1, source_target_pairs={{16,0},{32,16},{48,32},{64,48},{80,64},{96,80},{112,96},{128,112},... | collective-permute-start | bytes 98312 | tf_op jit(solution)/shard_map/ppermute | solution.py:17
  583.7 18.6 %collective-permute-start.29 = (f32[4,4,1,512]{3,2,1,0:T(1,128)S(1)}, f32[4,4,1,512]{3,2,1,0:T(1,128)S(1)}, u32[]{:S(2)}, u32[]{:S(2)}) collective-permute-start(f32[4,4,1,512]{3,2,1,0:T(1,128)S(1)} %get-tuple-element.10), channel_id=1, source_target_pairs={{0,16},{16,32},{32,48},{48,64},{64,80},{80,96},{96,112},{112,128},... | collective-permute-start | bytes 98312 | tf_op jit(solution)/shard_map/ppermute | solution.py:14
  593.3 23.1 %all-to-all-start.2 = ((f32[32,1,16]{2,1,0:T(1,128)}), f32[32,1,16]{2,1,0:T(1,128)S(1)}, u32[]{:S(2)}, u32[]{:S(2)}) async-start(f32[32,1,16]{2,1,0:T(1,128)} %bitcast.22), calls=%async_computation.2 | async-start | bytes 32768 | tf_op jit(solution)/shard_map/all_to_all | solution.py:111
  602.9 17.2 %collective-permute-start.30 = (f32[4,4,1,512]{3,2,1,0:T(1,128)S(1)}, f32[4,4,1,512]{3,2,1,0:T(1,128)S(1)}, u32[]{:S(2)}, u32[]{:S(2)}) collective-permute-start(f32[4,4,1,512]{3,2,1,0:T(1,128)S(1)} %get-tuple-element.7), channel_id=1, source_target_pairs={{16,0},{32,16},{48,32},{64,48},{80,64},{96,80},{112,96},{128,112},... | collective-permute-start | bytes 98312 | tf_op jit(solution)/shard_map/ppermute | solution.py:17
  605.1 15.1 %collective-permute-start.31 = (f32[4,4,1,512]{3,2,1,0:T(1,128)S(1)}, f32[4,4,1,512]{3,2,1,0:T(1,128)S(1)}, u32[]{:S(2)}, u32[]{:S(2)}) collective-permute-start(f32[4,4,1,512]{3,2,1,0:T(1,128)S(1)} %get-tuple-element.8), channel_id=1, source_target_pairs={{0,16},{16,32},{32,48},{48,64},{64,80},{80,96},{96,112},{112,128},... | collective-permute-start | bytes 98312 | tf_op jit(solution)/shard_map/ppermute | solution.py:14
  (19 other events, 127.8 us)
Sparse Core Ops, SparseCore 0:
  140.4 162.5 all-reduce.18
  331.5 167.8 all-reduce.20
where the time goes:
time: 630 us; the launch traced here: 628 us
  waiting for transfers between devices  346 us (55%)
  starting transfers between devices  211 us (33%)
  other arithmetic  30.7 us (5%)
  local copies, waits for them, and re-layouts  25.6 us (4%)
  between operations  14.9 us (2%)
    psum x1, waiting for transfers between devices, on_device(): adjoint = lax.psum(spread(shape, ints, floats, dep), 'mem')  168 us
    psum x1, waiting for transfers between devices, on_device(): incr = factor * lax.psum(partial_value, 'mem')  162 us
    ppermute x16, starting transfers between devices, extended_2(): lax.ppermute(lax.slice_in_dim(block, block.shape[dim] - width, None, axis...  122 us
    ppermute x16, starting transfers between devices, extended_2(): lax.ppermute(lax.slice_in_dim(block, 0, width, axis=dim), axis, backward)  49.7 us
    all_to_all x1, starting transfers between devices, on_device(): lax.all_to_all(int_send, 'tile', split_axis=1, concat_axis=1, tiled=True)  16.3 us
    all_to_all x1, starting transfers between devices, on_device(): lax.all_to_all(float_send, 'tile', split_axis=1, concat_axis=1, tiled=True)  14.4 us
    scatter-add x4, other arithmetic, spread(): adjoint = adjoint.at[corners[k]].add(floats[k] * dep)  14.1 us
  transfers between devices with their start and end apart: 37, of which 18 were waited for; matrix products, arithmetic and copies ran while one was open for 3% of the time, Pallas kernels for 0%

commit v1 on v0

v1 whole, which is shorter than its diff:
```python
import functools
import math

import jax
import jax.numpy as jnp
from jax import lax
from jax.experimental import pallas as pl
from jax.experimental.pallas import tpu as pltpu
from jax.sharding import PartitionSpec as P

STEPS = 8
COMPS = 8
LANES = 128
HIGHEST = lax.Precision.HIGHEST
F32 = jnp.float32
BF16 = jnp.bfloat16


def iota(shape, dim):
    return lax.broadcasted_iota(jnp.int32, shape, dim)


def call(body, out_shape, in_specs=None, scratch=(), flops=0, moved=0, name=None):
    return pl.pallas_call(
        body,
        out_shape=out_shape,
        in_specs=in_specs,
        scratch_shapes=scratch,
        compiler_params=pltpu.CompilerParams(vmem_limit_bytes=48 * 2**20),
        cost_estimate=pl.CostEstimate(flops=flops, bytes_accessed=moved, transcendentals=0),
        name=name,
    )


VMEM = pl.BlockSpec(memory_space=pltpu.VMEM)
SMEM = pl.BlockSpec(memory_space=pltpu.SMEM)


def vmem(count):
    return [VMEM] * count


def ranks(tile_row):
    count = tile_row.shape[1]
    along = jnp.broadcast_to(tile_row, (count, count))
    down = along.T
    i, j = iota((count, count), 0), iota((count, count), 1)
    same = along == down
    column = jnp.sum(jnp.where(same & (j < i), 1.0, 0.0), axis=1, keepdims=True)
    row = jnp.sum(jnp.where(same & (i < j), 1.0, 0.0), axis=0, keepdims=True)
    return column, row


def pack_body(tiles, slots, tile_ref, data_ref, send_ref):
    tile_row = tile_ref[...]
    count = tile_row.shape[1]
    column, unused = ranks(tile_row)
    width = COMPS * slots
    expand = jnp.where(iota((COMPS, width), 1) // slots == iota((COMPS, width), 0), 1.0, 0.0)
    data = lax.dot_general(
        data_ref[...], expand, (((0,), (0,)), ((), ())), precision=HIGHEST, preferred_element_type=F32
    )
    slot = (iota((count, width), 1) % slots).astype(F32)
    data = jnp.where(column == slot, data, 0.0)
    choose = jnp.where(iota((tiles, count), 0).astype(F32) == tile_row, 1.0, 0.0)
    send_ref[...] = jnp.dot(choose, data, precision=HIGHEST, preferred_element_type=F32)


def unpack_body(tile_ref, back_ref, hofx_ref):
    tile_row = tile_ref[...]
    tiles, slots = back_ref.shape
    count = tile_row.shape[1]
    unused, row = ranks(tile_row)
    choose = jnp.where(iota((tiles, count), 0).astype(F32) == tile_row, 1.0, 0.0)
    found = lax.dot_general(
        back_ref[...], choose, (((0,), (0,)), ((), ())), precision=HIGHEST, preferred_element_type=F32
    )
    keep = iota((slots, count), 0).astype(F32) == row
    hofx_ref[...] = jnp.sum(jnp.where(keep, found, 0.0), axis=0, keepdims=True)


def rates(group, keep, rate_x_ref, rate_y_ref):
    first = iota((8, LANES), 0) < 4
    rx = jnp.where(first, rate_x_ref[2 * group], rate_x_ref[2 * group + 1])
    ry = jnp.where(first, rate_y_ref[2 * group], rate_y_ref[2 * group + 1])
    centre = 1.0 - 2.0 * rx - 2.0 * ry
    return [(centre * k, rx * k, ry * k) for k in keep]


def smooth_rows(work, rows, coefs, emit):
    total = rows + 2 * STEPS
    parts = work.shape[2] // LANES
    lane = iota((8, LANES), 1)
    at_left, at_right = lane == 0, lane == LANES - 1

    def load(r):
        return [work[r, :, j * LANES : (j + 1) * LANES] for j in range(parts)]

    for step in range(STEPS):
        before, here = load(step), load(step + 1)
        for r in range(step + 1, total - 1 - step):
            after = load(r + 1)
            centre, rx, ry = coefs[0 if r < STEPS else (2 if r >= STEPS + rows else 1)]
            right = [pltpu.roll(v, 1, 1) for v in here]
            left = [pltpu.roll(v, LANES - 1, 1) for v in here]
            new = []
            for j in range(parts):
                low = jnp.where(at_left, right[j - 1] if j > 0 else 0.0, right[j])
                high = jnp.where(at_right, left[j + 1] if j + 1 < parts else 0.0, left[j])
                new.append(centre * here[j] + rx * (low + high) + ry * (before[j] + after[j]))
            if step == STEPS - 1:
                emit(r - STEPS, new)
            else:
                for j in range(parts):
                    work[r, :, j * LANES : (j + 1) * LANES] = new[j]
            before, here = here, after


def tiled(x):
    columns = x.shape[-1]
    x = x.reshape(-1, 8, columns // LANES, LANES)
    return jnp.swapaxes(x, 1, 2).reshape(-1, LANES)


def untiled(x, shape):
    x = x.reshape(-1, shape[-1] // LANES, 8, LANES)
    return jnp.swapaxes(x, 1, 2).reshape(shape)


def at_fields(ref, group, r, j, parts):
    stride = ref.shape[0] // 16
    start = group * 8 * stride + (r // 8 * parts + j) * 8 + r % 8
    return pl.ds(start, 8, stride=stride)


def fields(ref, group, r, j, parts):
    return ref[at_fields(ref, group, r, j, parts), :]


def partial_body(rows, rate_x_ref, rate_y_ref, keep_ref, own_ref, low_ref, high_ref, members_ref, out_ref, work):
    parts = out_ref.shape[1] // LANES
    for group in range(2):
        for j in range(parts):
            lanes = slice(j * LANES, (j + 1) * LANES)
            for r in range(STEPS):
                work[r, :, lanes] = fields(low_ref, group, r, j, parts)
                work[rows + STEPS + r, :, lanes] = fields(high_ref, group, r, j, parts)
            for r in range(rows):
                work[STEPS + r, :, lanes] = fields(own_ref, group, r, j, parts)
        coefs = rates(group, (keep_ref[0], 1.0, keep_ref[1]), rate_x_ref, rate_y_ref)

        def emit(r, new, group=group):
            terms = [new[j] * fields(members_ref, group, r, j, parts) for j in range(parts)]
            if group == 0:
                for j in range(parts):
                    out_ref[r * 8 : r * 8 + 8, j * LANES : (j + 1) * LANES] = terms[j]
                return
            lane, half = iota((8, LANES), 1), iota((8, LANES), 0) < 4
            sums = []
            for j in range(parts):
                both = terms[j] + out_ref[r * 8 : r * 8 + 8, j * LANES : (j + 1) * LANES]
                sums.append(both + pltpu.roll(both, 4, 0))
            left = [pltpu.roll(v, LANES - 1, 1) for v in sums]
            for j in range(parts):
                later = left[j + 1] if j + 1 < parts else left[j]
                shifted = jnp.where(lane == LANES - 1, later, left[j])
                out_ref[r * 8 : r * 8 + 8, j * LANES : (j + 1) * LANES] = jnp.where(
                    half, sums[j], shifted
                )

        smooth_rows(work, rows, coefs, emit)


def grad_body(
    rows,
    factor,
    rate_x_ref,
    rate_y_ref,
    keep_ref,
    alpha_ref,
    land_ref,
    members_ref,
    members_low_ref,
    members_high_ref,
    adjoint_ref,
    adjoint_low_ref,
    adjoint_high_ref,
    out_ref,
    work,
):
    parts = land_ref.shape[1] // LANES

    def twice(ref, r, lanes):
        four = ref[r * 4 : r * 4 + 4, lanes]
        return jnp.concatenate([four, four], axis=0)

    for group in range(2):
        for j in range(parts):
            lanes = slice(j * LANES, (j + 1) * LANES)
            for r in range(STEPS):
                work[r, :, lanes] = fields(members_low_ref, group, r, j, parts) * twice(adjoint_low_ref, r, lanes)
                work[rows + STEPS + r, :, lanes] = fields(members_high_ref, group, r, j, parts) * twice(
                    adjoint_high_ref, r, lanes
                )
            for r in range(rows):
                work[STEPS + r, :, lanes] = (
                    fields(members_ref, group, r, j, parts) * adjoint_ref[r * 8 : r * 8 + 8, lanes]
                )
        coefs = rates(group, (keep_ref[0], 1.0, keep_ref[1]), rate_x_ref, rate_y_ref)

        def emit(r, new, group=group):
            for j in range(parts):
                lanes = slice(j * LANES, (j + 1) * LANES)
                land = jnp.broadcast_to(land_ref[r : r + 1, lanes], (8, LANES)) * factor
                value = fields(alpha_ref, group, r, j, parts) + land * new[j]
                out_ref[at_fields(out_ref, group, r, j, parts), :] = value

        smooth_rows(work, rows, coefs, emit)


def corner_terms(s, slots, comps, scale):
    def comp(k):
        return comps[k * slots + s : k * slots + s + 1, :]

    count = comps.shape[1]
    code = comp(1)
    level = code - 4.0 * jnp.floor(code * 0.25)
    row = jnp.floor(code * 0.25)
    sub = iota((8, count), 0).astype(F32)
    weights = [comp(2 + k) if scale is None else comp(2 + k) * scale for k in range(4)]
    left, right = sub == level, sub == level + 4.0
    lower = jnp.where(left, weights[0], jnp.where(right, weights[1], 0.0))
    upper = jnp.where(left, weights[2], jnp.where(right, weights[3], 0.0))
    return jnp.broadcast_to(row, (8, count)), lower, upper


def interpolate_body(rows, slots, raw_ref, field_ref, comps_ref, out_ref, pieces):
    comps_ref[...] = raw_ref[...].T
    columns = field_ref.shape[1]
    count = comps_ref.shape[1]
    field = field_ref[...]
    top = field.astype(BF16)
    pieces[: 8 * rows, :] = top
    pieces[8 * rows :, :] = (field - top.astype(F32)).astype(BF16)
    for s in range(slots):
        column = comps_ref[s : s + 1, :].astype(jnp.int32)
        hot = jnp.where(iota((columns, count), 0) == column, 1.0, 0.0).astype(BF16)
        found = jnp.dot(pieces[...], hot, preferred_element_type=F32)
        row, lower, upper = corner_terms(s, slots, comps_ref, None)
        total = jnp.zeros((8, count), F32)
        previous = None
        for g in range(rows):
            at = row == float(g)
            value = found[g * 8 : g * 8 + 8] + found[8 * (rows + g) : 8 * (rows + g) + 8]
            rest = 0.0 if previous is None else jnp.where(previous, upper, 0.0)
            total = total + jnp.where(at, lower, rest) * value
            previous = at
        out_ref[s : s + 1, :] = jnp.sum(total, axis=0, keepdims=True)


def spread_body(
    rows, slots, tiles, factor, me_ref, raw_ref, comps_ref, sums_ref, own_ref, low_ref, high_ref, back_ref, left, total
):
    columns = own_ref.shape[1]
    count = comps_ref.shape[1]
    hofx = sums_ref[0]
    for k in range(1, sums_ref.shape[0]):
        hofx = hofx + sums_ref[k]
    hofx = factor * hofx
    mine = iota((tiles, count), 1) == me_ref[0] * tiles + iota((tiles, count), 0)
    back_ref[...] = lax.dot_general(
        jnp.where(mine, 1.0, 0.0),
        hofx,
        (((1,), (1,)), ((), ())),
        precision=HIGHEST,
        preferred_element_type=F32,
    )
    value = comps_ref[6 * slots : 7 * slots, :]
    rinv = comps_ref[7 * slots : 8 * slots, :]
    dep = rinv * (hofx - value)
    for s in range(slots):
        row, lower, upper = corner_terms(s, slots, comps_ref, dep[s : s + 1, :])
        previous = None
        for g in range(rows):
            at = row == float(g)
            rest = 0.0 if previous is None else jnp.where(previous, upper, 0.0)
            term = jnp.where(at, lower, rest)
            top = term.astype(BF16)
            left[g * 8 : g * 8 + 8, :] = top
            left[8 * (rows + g) : 8 * (rows + g) + 8, :] = (term - top.astype(F32)).astype(BF16)
            previous = at
        column = raw_ref[:, s : s + 1].astype(jnp.int32)
        hot = jnp.where(iota((count, columns), 1) == column, 1.0, 0.0).astype(BF16)
        part = jnp.dot(left[...], hot, preferred_element_type=F32)
        if s == 0:
            total[...] = part
        else:
            total[...] += part
    lane, half = iota((8, columns), 1), iota((8, columns), 0) < 4
    for g in range(rows):
        both = total[g * 8 : g * 8 + 8, :] + total[8 * (rows + g) : 8 * (rows + g) + 8, :]
        moved = jnp.where(lane == 0, 0.0, pltpu.roll(pltpu.roll(both, 4, 0), 1, 1))
        four = both + moved
        own_ref[g * 8 : g * 8 + 8, :] = jnp.where(half, four, pltpu.roll(four, 4, 0))
        if g < STEPS:
            low_ref[g * 4 : g * 4 + 4, :] = four[:4]
        if g >= rows - STEPS:
            at = g - (rows - STEPS)
            high_ref[at * 4 : at * 4 + 4, :] = four[:4]


def on_device(
    alpha,
    perturbs,
    diff_x,
    diff_y,
    land_mask,
    obs_tile,
    obs_row,
    obs_col,
    obs_lev,
    obs_weights,
    obs_value,
    obs_rinv,
):
    members, levels, rows, columns = alpha.shape
    tiles, mems = lax.axis_size("tile"), lax.axis_size("mem")
    factor = (mems * members - 1) ** (-0.5)
    slots = 16
    inner = math.isqrt(mems)
    near = [[i * inner + j for j in range(inner)] for i in range(inner)]
    far = [[i * inner + j for i in range(inner)] for j in range(inner)]
    forward = [(i, i + 1) for i in range(tiles - 1)]
    backward = [(i + 1, i) for i in range(tiles - 1)]
    place = lax.axis_index("tile")
    keep = jnp.stack([place > 0, place < tiles - 1]).astype(F32)
    me = lax.axis_index("mem").astype(jnp.int32).reshape(1)
    flat = (members * levels * rows * columns // LANES, LANES)

    def exchange(low_rows, high_rows):
        return lax.ppermute(high_rows, "tile", forward), lax.ppermute(low_rows, "tile", backward)

    land = land_mask.astype(F32)
    own = land * alpha
    low, high = exchange(tiled(own[:, :, :STEPS]), tiled(own[:, :, rows - STEPS :]))
    own = tiled(own)

    tile_row = obs_tile.reshape(1, -1).astype(F32)
    data = jnp.concatenate(
        [
            obs_col.astype(F32)[None],
            (obs_row * levels + obs_lev).astype(F32)[None],
            obs_weights,
            obs_value[None],
            obs_rinv[None],
        ],
        axis=0,
    )
    width = COMPS * slots
    sent = call(
        functools.partial(pack_body, tiles, slots),
        jax.ShapeDtypeStruct((tiles, width), F32),
        vmem(2),
        name="pack",
    )(tile_row, data)
    routed = lax.all_to_all(sent, "tile", split_axis=0, concat_axis=0, tiled=True)
    raw = lax.all_to_all(
        jnp.broadcast_to(routed[None], (mems, tiles, width)), "mem", split_axis=0, concat_axis=0, tiled=True
    ).reshape(mems * tiles, width)

    masked = land * perturbs.astype(F32)
    members_low, members_high = exchange(tiled(masked[:, :, :STEPS]), tiled(masked[:, :, rows - STEPS :]))
    masked = tiled(masked)

    work = pltpu.VMEM((rows + 2 * STEPS, 8, columns), F32)
    partial = call(
        functools.partial(partial_body, rows),
        jax.ShapeDtypeStruct((8 * rows, columns), F32),
        [SMEM] * 3 + vmem(4),
        [work],
        flops=2 * 10**7,
        moved=2 * 10**6,
        name="partial",
    )(diff_x, diff_y, keep, own, low, high, masked)

    count = mems * tiles
    comps, found = call(
        functools.partial(interpolate_body, rows, slots),
        (jax.ShapeDtypeStruct((width, count), F32), jax.ShapeDtypeStruct((slots, count), F32)),
        vmem(2),
        [pltpu.VMEM((16 * rows, columns), BF16)],
        name="interpolate",
    )(raw, partial)

    def gather(x, groups):
        return lax.all_to_all(
            jnp.broadcast_to(x[None], (inner,) + x.shape),
            "mem",
            split_axis=0,
            concat_axis=0,
            axis_index_groups=groups,
            tiled=True,
        )

    sums = gather(jnp.sum(gather(found, near), axis=0), far)
    adjoint, adjoint_first, adjoint_last, back = call(
        functools.partial(spread_body, rows, slots, tiles, factor),
        (
            jax.ShapeDtypeStruct((8 * rows, columns), F32),
            jax.ShapeDtypeStruct((levels * STEPS, columns), F32),
            jax.ShapeDtypeStruct((levels * STEPS, columns), F32),
            jax.ShapeDtypeStruct((tiles, slots), F32),
        ),
        [SMEM] + vmem(3),
        [pltpu.VMEM((16 * rows, count), BF16), pltpu.VMEM((16 * rows, columns), F32)],
        name="spread",
    )(me, raw, comps, sums)
    adjoint_low, adjoint_high = exchange(adjoint_first, adjoint_last)
    returned = lax.all_to_all(back, "tile", split_axis=0, concat_axis=0, tiled=True)

    grad = call(
        functools.partial(grad_body, rows, factor),
        jax.ShapeDtypeStruct(flat, F32),
        [SMEM] * 3 + vmem(8),
        [work],
        flops=2 * 10**7,
        moved=2 * 10**6,
        name="grad",
    )(
        diff_x,
        diff_y,
        keep,
        tiled(alpha),
        land,
        masked,
        members_low,
        members_high,
        adjoint,
        adjoint_low,
        adjoint_high,
    )
    hofx = call(
        unpack_body,
        jax.ShapeDtypeStruct((1, tile_row.shape[1]), F32),
        vmem(2),
        name="unpack",
    )(tile_row, returned)
    return untiled(grad, alpha.shape), hofx.reshape(-1)


def solution(mesh):
    return jax.shard_map(
        on_device,
        mesh=mesh,
        in_specs=(
            P("mem", None, "tile", None),
            P("mem", None, "tile", None),
            P("mem"),
            P("mem"),
            P("tile", None),
            P(("tile", "mem"), None),
            P(("tile", "mem")),
            P(("tile", "mem")),
            P(("tile", "mem")),
            P(None, ("tile", "mem")),
            P(("tile", "mem")),
            P(("tile", "mem")),
        ),
        out_specs=(P("mem", None, "tile", None), P(("tile", "mem"))),
        check_vma=False,
    )
```

time: 630 us -> 139 us (0.22)
  waiting for transfers between devices: 346 us -> 18.8 us
  starting transfers between devices: 211 us -> 37.1 us
  blocking collectives: 0 us -> 58.3 us
  other arithmetic: 30.7 us -> 1.67 us
  local copies, waits for them, and re-layouts: 25.6 us -> 3.57 us
  Pallas kernels: 0 us -> 17.8 us
  between operations: 14.9 us -> 0.83 us
    psum x2 -> x0, waiting for transfers between devices: 330 us -> none  [the longest x1 168 us: on_device(): adjoint = lax.psum(spread(shape, ints, floats, dep), 'mem')]
    ppermute x32 -> x6, starting transfers between devices: 171 us -> 19.6 us  [the longest x3 13.9 us: exchange(): lax.ppermute(high_rows, 'tile', forward)]
    all_to_all x0 -> x2, blocking collectives: none -> 58.3 us  [the longest x1 33.4 us: on_device(): lax.all_to_all(sent, 'tile', split_axis=0, concat_axis=0, tiled=True)]
    all_to_all x3, starting transfers between devices: 39.6 us -> 17.5 us  [the longest x2 11.9 us: gather(): lax.all_to_all(jnp.broadcast_to(x[None], (inner,) + x.shape), 'mem', spli...]
    pallas_call x0 -> x6, Pallas kernels: none -> 17.8 us  [the longest x1 5.14 us: on_device(): call(functools.partial(grad_body, rows, factor), jax.ShapeDtypeStruct(fla...]
    gather x9 -> x0, local copies, waits for them, and re-layouts: 15.4 us -> none  [the longest x6 9.66 us: interpolate(): result = result + floats[k] * flat[corners[k]]]
    scatter-add x4 -> x0, other arithmetic: 14.1 us -> none  [spread(): adjoint = adjoint.at[corners[k]].add(floats[k] * dep)]
    add x17 -> x0, other arithmetic: 9.9 us -> none  [the longest x14 7.91 us: stencil(): return core + rate_x * across + rate_y * along]
  transfers between devices with their start and end apart: 37 -> 9, of which waited for: 18 -> 3; matrix products, arithmetic and copies ran while one was open for 3% -> 1% of each run, Pallas kernels for 0% -> 6%
where the time goes in v1:
time: 139 us; the launch traced here: 138 us
  blocking collectives  58.3 us (42%)
  starting transfers between devices  37.1 us (27%)
  waiting for transfers between devices  18.8 us (14%)
  Pallas kernels  17.8 us (13%)
  local copies, waits for them, and re-layouts  3.57 us (3%)
  other arithmetic  1.67 us (1%)
    all_to_all x1, blocking collectives, on_device(): lax.all_to_all(sent, 'tile', split_axis=0, concat_axis=0, tiled=True)  33.4 us
    all_to_all x1, blocking collectives, on_device(): lax.all_to_all(back, 'tile', split_axis=0, concat_axis=0, tiled=True)  24.9 us
    ppermute x3, starting transfers between devices, exchange(): lax.ppermute(high_rows, 'tile', forward)  13.9 us
    all_to_all x2, starting transfers between devices, gather(): lax.all_to_all(jnp.broadcast_to(x[None], (inner,) + x.shape), 'mem', spli...  11.9 us
    ppermute x3, waiting for transfers between devices, exchange(): lax.ppermute(low_rows, 'tile', backward)  11.2 us
    ppermute x3, starting transfers between devices, exchange(): lax.ppermute(low_rows, 'tile', backward)  5.76 us
    all_to_all x1, starting transfers between devices, on_device(): lax.all_to_all(jnp.broadcast_to(routed[None], (mems, tiles, width)), 'mem...  5.62 us
    all_to_all x2, waiting for transfers between devices, gather(): lax.all_to_all(jnp.broadcast_to(x[None], (inner,) + x.shape), 'mem', spli...  5.34 us
  transfers between devices with their start and end apart: 9, of which 3 were waited for; matrix products, arithmetic and copies ran while one was open for 1% of the time, Pallas kernels for 6%

profile of v1, /device:TPU:1, one launch (start us, length us, event | category | flops | bytes accessed | tf_op | source)
XLA Modules:
  0.0 138.1 jit_solution(14701527660150812564)
XLA Ops:
  0.6 0.7 convert_bitcast_fusion.tile_ref
  1.4 0.7 add_convert_fusion.1
  2.1 0.7 concatenate.3.data_ref
  2.8 0.6 pack.1
  3.4 33.4 %all_to_all.35 = f32[32,1,128]{2,1,0:T(1,128)S(1)} all-to-all(f32[32,1,128]{2,1,0:T(1,128)S(1)} %bitcast.66), channel_id=1, replica_groups=mesh['tile'=32,'mem'=16] {'tile'}, dimensions={0} | all-to-all | bytes 32768 | tf_op jit(solution)/shard_map/all_to_all | solution.py:366
  36.7 0.7 broadcast_in_dim.39
  37.5 5.6 %all-to-all-start.1 = ((f32[16,32,128]{2,1,0:T(8,128)}), f32[16,32,128]{2,1,0:T(8,128)S(1)}, u32[]{:S(2)}, u32[]{:S(2)}) async-start(f32[16,32,128]{2,1,0:T(8,128)} %broadcast_in_dim.39), calls=%async_computation.1 | async-start | bytes 524288 | tf_op jit(solution)/shard_map/all_to_all | solution.py:367
  43.1 0.1 broadcast_multiply_fusion
  43.3 0.1 fusion
  43.4 3.0 %collective-permute-start.2 = (f32[512,128]{1,0:T(8,128)S(1)}, f32[512,128]{1,0:T(8,128)S(1)}, u32[]{:S(2)}, u32[]{:S(2)}) collective-permute-start(f32[512,128]{1,0:T(8,128)S(1)} %bitcast.72), channel_id=1, source_target_pairs={{0,16},{16,32},{32,48},{48,64},{64,80},{80,96},{96,112},{112,128},... | collective-permute-start | bytes 786440 | tf_op jit(solution)/shard_map/ppermute | solution.py:341
  46.4 1.9 %collective-permute-start.3 = (f32[512,128]{1,0:T(8,128)S(1)}, f32[512,128]{1,0:T(8,128)S(1)}, u32[]{:S(2)}, u32[]{:S(2)}) collective-permute-start(f32[512,128]{1,0:T(8,128)S(1)} %bitcast.71), channel_id=1, source_target_pairs={{16,0},{32,16},{48,32},{64,48},{80,64},{96,80},{112,96},{128,112},... | collective-permute-start | bytes 786440 | tf_op jit(solution)/shard_map/ppermute | solution.py:341
  48.4 0.1 add_convert_fusion.keep_ref
  48.4 2.3 %collective-permute-done.2.low_ref = f32[512,128]{1,0:T(8,128)S(1)} collective-permute-done((f32[512,128]{1,0:T(8,128)S(1)}, f32[512,128]{1,0:T(8,128)S(1)}, u32[]{:S(2)}, u32[]{:S(2)}) %collective-permute-start.2) | collective-permute-done | bytes 262176 | tf_op jit(solution)/shard_map/ppermute | solution.py:341
  50.7 11.2 %collective-permute-done.3.high_ref = f32[512,128]{1,0:T(8,128)S(1)} collective-permute-done((f32[512,128]{1,0:T(8,128)S(1)}, f32[512,128]{1,0:T(8,128)S(1)}, u32[]{:S(2)}, u32[]{:S(2)}) %collective-permute-start.3) | collective-permute-done | bytes 262176 | tf_op jit(solution)/shard_map/ppermute | solution.py:341
  61.9 0.7 copy-done.1
  62.6 0.0 copy-done.2
  62.6 4.8 %partial.1.field_ref = f32[128,512]{1,0:T(8,128)S(1)} custom-call(f32[4]{0:T(128)S(1)} %copy-done.1, f32[4]{0:T(128)S(1)} %copy-done.2, f32[2]{0:T(128)S(1)} %add_convert_fusion.keep_ref, f32[1024,128]{1,0:T(8,128)S(1)} %bitcast.61, f32[512,128]{1,0:T(8,128)S(1)} %collective-permute-done.2.low_ref, f32[512,128]{1,0:T(8,128)S(1)} %collective-permute-done.3.high_ref, ...), custom_call_target="tpu_custom_call" | custom-call | flops 20000000 | bytes 2000000 | tf_op jit(solution)/shard_map/partial/pallas_call | solution.py:376
  67.4 3.4 %interpolate.1 = (f32[128,512]{1,0:T(8,128)S(1)}, f32[16,512]{1,0:T(8,128)S(1)}) custom-call(f32[512,128]{1,0:T(8,128)S(1)} %bitcast.62, f32[128,512]{1,0:T(8,128)S(1)} %partial.1.field_ref), custom_call_target="tpu_custom_call" | custom-call | tf_op jit(solution)/shard_map/interpolate/pallas_call | solution.py:387
  70.8 0.7 broadcast_in_dim.40
  71.5 6.1 %all-to-all-start.2 = ((f32[4,16,512]{2,1,0:T(8,128)}), f32[4,16,512]{2,1,0:T(8,128)S(1)}, u32[]{:S(2)}, u32[]{:S(2)}) async-start(f32[4,16,512]{2,1,0:T(8,128)} %broadcast_in_dim.40), calls=%async_computation.2 | async-start | bytes 262144 | tf_op jit(solution)/shard_map/all_to_all | solution.py:396
  77.6 3.2 %collective-permute-start = (f32[512,128]{1,0:T(8,128)S(1)}, f32[512,128]{1,0:T(8,128)S(1)}, u32[]{:S(2)}, u32[]{:S(2)}) collective-permute-start(f32[512,128]{1,0:T(8,128)S(1)} %bitcast.70), channel_id=1, source_target_pairs={{0,16},{16,32},{32,48},{48,64},{64,80},{80,96},{96,112},{112,128},... | collective-permute-start | bytes 786440 | tf_op jit(solution)/shard_map/ppermute | solution.py:341
  80.8 1.9 %collective-permute-start.1 = (f32[512,128]{1,0:T(8,128)S(1)}, f32[512,128]{1,0:T(8,128)S(1)}, u32[]{:S(2)}, u32[]{:S(2)}) collective-permute-start(f32[512,128]{1,0:T(8,128)S(1)} %bitcast.69), channel_id=1, source_target_pairs={{16,0},{32,16},{48,32},{64,48},{80,64},{96,80},{112,96},{128,112},... | collective-permute-start | bytes 786440 | tf_op jit(solution)/shard_map/ppermute | solution.py:341
  82.7 0.0 all-to-all-done.2
  82.8 0.7 broadcast_in_dim.41
  83.4 5.8 %all-to-all-start.3 = ((f32[4,16,512]{2,1,0:T(8,128)}), f32[4,16,512]{2,1,0:T(8,128)S(1)}, u32[]{:S(2)}, u32[]{:S(2)}) async-start(f32[4,16,512]{2,1,0:T(8,128)} %broadcast_in_dim.41), calls=%async_computation.3 | async-start | bytes 262144 | tf_op jit(solution)/shard_map/all_to_all | solution.py:396
  89.2 5.3 %all-to-all-done.3.sums_ref = f32[4,16,512]{2,1,0:T(8,128)S(1)} async-done(((f32[4,16,512]{2,1,0:T(8,128)}), f32[4,16,512]{2,1,0:T(8,128)S(1)}, u32[]{:S(2)}, u32[]{:S(2)}) %all-to-all-start.3) | async-done | bytes 131104 | tf_op jit(solution)/shard_map/all_to_all | solution.py:396
  94.5 3.2 %spread.1 = (f32[128,512]{1,0:T(8,128)S(1)}, f32[32,512]{1,0:T(8,128)S(1)}, f32[32,512]{1,0:T(8,128)S(1)}, f32[32,16]{1,0:T(8,128)S(1)}) custom-call(s32[1]{0:T(128)} %bitcast.14.me_ref, f32[512,128]{1,0:T(8,128)S(1)} %bitcast.63, f32[128,512]{1,0:T(8,128)S(1)} %get-tuple-element.8.comps_ref, f32[4,16,512]{2,1,0:T(8,128)S(1)} %all-to-all-done.3.sums_ref), custom_call_target="tpu_custom_call" | custom-call | tf_op jit(solution)/shard_map/spread/pallas_call | solution.py:406
  97.7 7.6 %collective-permute-start.4 = (f32[32,512]{1,0:T(8,128)S(1)}, f32[32,512]{1,0:T(8,128)S(1)}, u32[]{:S(2)}, u32[]{:S(2)}) collective-permute-start(f32[32,512]{1,0:T(8,128)S(1)} %get-tuple-element.11), channel_id=1, source_target_pairs={{0,16},{16,32},{32,48},{48,64},{64,80},{80,96},{96,112},{112,128},... | collective-permute-start | bytes 196616 | tf_op jit(solution)/shard_map/ppermute | solution.py:341
  105.3 1.9 %collective-permute-start.5 = (f32[32,512]{1,0:T(8,128)S(1)}, f32[32,512]{1,0:T(8,128)S(1)}, u32[]{:S(2)}, u32[]{:S(2)}) collective-permute-start(f32[32,512]{1,0:T(8,128)S(1)} %get-tuple-element.12), channel_id=1, source_target_pairs={{16,0},{32,16},{48,32},{64,48},{80,64},{96,80},{112,96},{128,112},... | collective-permute-start | bytes 196616 | tf_op jit(solution)/shard_map/ppermute | solution.py:341
  107.2 24.9 %all_to_all.36 = f32[32,1,16]{2,1,0:T(1,128)S(1)} all-to-all(f32[32,1,16]{2,1,0:T(1,128)S(1)} %bitcast.67), channel_id=1, replica_groups=mesh['tile'=32,'mem'=16] {'tile'}, dimensions={0} | all-to-all | bytes 4096 | tf_op jit(solution)/shard_map/all_to_all | solution.py:419
  132.2 0.8 unpack.1
  133.0 5.1 %grad.1 = f32[1024,128]{1,0:T(8,128)} custom-call(f32[4]{0:T(128)S(1)} %copy-done.1, f32[4]{0:T(128)S(1)} %copy-done.2, f32[2]{0:T(128)S(1)} %add_convert_fusion.keep_ref, f32[1024,128]{1,0:T(8,128)S(1)} %bitcast.64, f32[16,512]{1,0:T(8,128)S(1)} %convert_element_type.21.land_ref, f32[1024,128]{1,0:T(8,128)S(1)} %bitcast.60, ...), custom_call_target="tpu_custom_call" | custom-call | flops 20000000 | bytes 2000000 | tf_op jit(solution)/shard_map/grad/pallas_call | solution.py:421
  (18 shorter events, 0.1 us)
Async XLA Ops:
  0.6 0.8 copy-start.5
  0.6 42.5 %copy-start = (f32[4,4,16,512]{3,2,1,0:T(8,128)S(1)}, f32[4,4,16,512]{3,2,1,0:T(8,128)}, u32[]{:S(2)}) copy-start(f32[4,4,16,512]{3,2,1,0:T(8,128)} %param.12) | copy-start | bytes 1572868
  37.5 5.6 %copy-start.4 = (s32[16,512]{1,0:T(8,128)S(1)}, s32[16,512]{1,0:T(8,128)}, u32[]{:S(2)}) copy-start(s32[16,512]{1,0:T(8,128)} %param.16) | copy-start | bytes 98308
  37.5 5.7 %copy-start.3 = (bf16[4,4,16,512]{3,2,1,0:T(8,128)(2,1)S(1)}, bf16[4,4,16,512]{3,2,1,0:T(8,128)(2,1)}, u32[]{:S(2)}) copy-start(bf16[4,4,16,512]{3,2,1,0:T(8,128)(2,1)} %param.13) | copy-start | bytes 786436
  37.5 29.9 %all-to-all-start.1 = ((f32[16,32,128]{2,1,0:T(8,128)}), f32[16,32,128]{2,1,0:T(8,128)S(1)}, u32[]{:S(2)}, u32[]{:S(2)}) async-start(f32[16,32,128]{2,1,0:T(8,128)} %broadcast_in_dim.39), calls=%async_computation.1 | async-start | bytes 524288 | tf_op jit(solution)/shard_map/all_to_all | solution.py:367
  43.4 7.4 %collective-permute-start.2 = (f32[512,128]{1,0:T(8,128)S(1)}, f32[512,128]{1,0:T(8,128)S(1)}, u32[]{:S(2)}, u32[]{:S(2)}) collective-permute-start(f32[512,128]{1,0:T(8,128)S(1)} %bitcast.72), channel_id=1, source_target_pairs={{0,16},{16,32},{32,48},{48,64},{64,80},{80,96},{96,112},{112,128},... | collective-permute-start | bytes 786440 | tf_op jit(solution)/shard_map/ppermute | solution.py:341
  46.4 15.5 %collective-permute-start.3 = (f32[512,128]{1,0:T(8,128)S(1)}, f32[512,128]{1,0:T(8,128)S(1)}, u32[]{:S(2)}, u32[]{:S(2)}) collective-permute-start(f32[512,128]{1,0:T(8,128)S(1)} %bitcast.71), channel_id=1, source_target_pairs={{16,0},{32,16},{48,32},{64,48},{80,64},{96,80},{112,96},{128,112},... | collective-permute-start | bytes 786440 | tf_op jit(solution)/shard_map/ppermute | solution.py:341
  61.9 0.7 copy-start.1
  61.9 0.7 copy-start.2
  71.5 11.3 %all-to-all-start.2 = ((f32[4,16,512]{2,1,0:T(8,128)}), f32[4,16,512]{2,1,0:T(8,128)S(1)}, u32[]{:S(2)}, u32[]{:S(2)}) async-start(f32[4,16,512]{2,1,0:T(8,128)} %broadcast_in_dim.40), calls=%async_computation.2 | async-start | bytes 262144 | tf_op jit(solution)/shard_map/all_to_all | solution.py:396
  77.6 55.4 %collective-permute-start = (f32[512,128]{1,0:T(8,128)S(1)}, f32[512,128]{1,0:T(8,128)S(1)}, u32[]{:S(2)}, u32[]{:S(2)}) collective-permute-start(f32[512,128]{1,0:T(8,128)S(1)} %bitcast.70), channel_id=1, source_target_pairs={{0,16},{16,32},{32,48},{48,64},{64,80},{80,96},{96,112},{112,128},... | collective-permute-start | bytes 786440 | tf_op jit(solution)/shard_map/ppermute | solution.py:341
  80.8 52.1 %collective-permute-start.1 = (f32[512,128]{1,0:T(8,128)S(1)}, f32[512,128]{1,0:T(8,128)S(1)}, u32[]{:S(2)}, u32[]{:S(2)}) collective-permute-start(f32[512,128]{1,0:T(8,128)S(1)} %bitcast.69), channel_id=1, source_target_pairs={{16,0},{32,16},{48,32},{64,48},{80,64},{96,80},{112,96},{128,112},... | collective-permute-start | bytes 786440 | tf_op jit(solution)/shard_map/ppermute | solution.py:341
  83.4 11.1 %all-to-all-start.3 = ((f32[4,16,512]{2,1,0:T(8,128)}), f32[4,16,512]{2,1,0:T(8,128)S(1)}, u32[]{:S(2)}, u32[]{:S(2)}) async-start(f32[4,16,512]{2,1,0:T(8,128)} %broadcast_in_dim.41), calls=%async_computation.3 | async-start | bytes 262144 | tf_op jit(solution)/shard_map/all_to_all | solution.py:396
  97.7 35.3 %collective-permute-start.4 = (f32[32,512]{1,0:T(8,128)S(1)}, f32[32,512]{1,0:T(8,128)S(1)}, u32[]{:S(2)}, u32[]{:S(2)}) collective-permute-start(f32[32,512]{1,0:T(8,128)S(1)} %get-tuple-element.11), channel_id=1, source_target_pairs={{0,16},{16,32},{32,48},{48,64},{64,80},{80,96},{96,112},{112,128},... | collective-permute-start | bytes 196616 | tf_op jit(solution)/shard_map/ppermute | solution.py:341
  105.3 27.7 %collective-permute-start.5 = (f32[32,512]{1,0:T(8,128)S(1)}, f32[32,512]{1,0:T(8,128)S(1)}, u32[]{:S(2)}, u32[]{:S(2)}) collective-permute-start(f32[32,512]{1,0:T(8,128)S(1)} %get-tuple-element.12), channel_id=1, source_target_pairs={{16,0},{32,16},{48,32},{64,48},{80,64},{96,80},{112,96},{128,112},... | collective-permute-start | bytes 196616 | tf_op jit(solution)/shard_map/ppermute | solution.py:341

commit v2 on v1

--- a/solution.py
+++ b/solution.py
@@ -14,6 +14,8 @@
 HIGHEST = lax.Precision.HIGHEST
 F32 = jnp.float32
 BF16 = jnp.bfloat16
+PACK_FLOPS = 10**11
+PARTIAL_FLOPS = 10**11
 
 
 def iota(shape, dim):
@@ -51,8 +53,15 @@
     return column, row
 
 
-def pack_body(tiles, slots, tile_ref, data_ref, send_ref):
-    tile_row = tile_ref[...]
+def pack_body(
+    tiles, slots, levels, unused_ref, tile_ref, row_ref, col_ref, lev_ref, weights_ref, value_ref, rinv_ref, send_ref, data_ref
+):
+    tile_row = tile_ref[...].astype(F32)
+    data_ref[0:1, :] = col_ref[...].astype(F32)
+    data_ref[1:2, :] = (row_ref[...] * levels + lev_ref[...]).astype(F32)
+    data_ref[2:6, :] = weights_ref[...]
+    data_ref[6:7, :] = value_ref[...]
+    data_ref[7:8, :] = rinv_ref[...]
     count = tile_row.shape[1]
     column, unused = ranks(tile_row)
     width = COMPS * slots
@@ -67,7 +76,7 @@
 
 
 def unpack_body(tile_ref, back_ref, hofx_ref):
-    tile_row = tile_ref[...]
+    tile_row = tile_ref[...].astype(F32)
     tiles, slots = back_ref.shape
     count = tile_row.shape[1]
     unused, row = ranks(tile_row)
@@ -127,30 +136,62 @@
     return jnp.swapaxes(x, 1, 2).reshape(shape)
 
 
-def at_fields(ref, group, r, j, parts):
-    stride = ref.shape[0] // 16
-    start = group * 8 * stride + (r // 8 * parts + j) * 8 + r % 8
-    return pl.ds(start, 8, stride=stride)
-
-
-def fields(ref, group, r, j, parts):
-    return ref[at_fields(ref, group, r, j, parts), :]
-
-
-def partial_body(rows, rate_x_ref, rate_y_ref, keep_ref, own_ref, low_ref, high_ref, members_ref, out_ref, work):
+def at_fields(base, stride, group, r, j, parts):
+    return pl.ds(base + group * 8 * stride + (r // 8 * parts + j) * 8 + r % 8, 8, stride=stride)
+
+
+def odd_tile():
+    return lax.rem(lax.axis_index("tile"), 2)
+
+
+def keep_sides(tiles):
+    place = lax.axis_index("tile")
+    return jnp.where(place > 0, 1.0, 0.0), jnp.where(place < tiles - 1, 1.0, 0.0)
+
+
+def prep_body(alpha_ref, members_ref, land_ref, own_ref, masked_ref, far_ref, near_ref):
+    members, levels, rows, columns = members_ref.shape
+    parts = columns // LANES
+    size = rows * parts
+    count = members * levels
+    land = land_ref[...].astype(F32)
+    for f in range(count):
+        field = land * members_ref[f // levels, f % levels].astype(F32)
+        for k in range(rows // 8):
+            for j in range(parts):
+                at = f * size + (k * parts + j) * 8
+                mask = land[k * 8 : k * 8 + 8, j * LANES : (j + 1) * LANES]
+                own_ref[at : at + 8, :] = mask * alpha_ref[at : at + 8, :]
+                masked_ref[at : at + 8, :] = field[k * 8 : k * 8 + 8, j * LANES : (j + 1) * LANES]
+    brim = STEPS * parts
+    odd = odd_tile()
+    first = odd * (size - brim)
+    last = (1 - odd) * (size - brim)
+    for source, start in ((own_ref, 0), (masked_ref, count * brim)):
+        for f in range(count):
+            to = slice(start + f * brim, start + (f + 1) * brim)
+            far_ref[to, :] = source[pl.ds(pl.multiple_of(f * size + first, 8), brim), :]
+            near_ref[to, :] = source[pl.ds(pl.multiple_of(f * size + last, 8), brim), :]
+
+
+def partial_body(rows, tiles, rate_x_ref, rate_y_ref, own_ref, far_ref, near_ref, members_ref, out_ref, work):
     parts = out_ref.shape[1] // LANES
+    size, brim = rows * parts, STEPS * parts
+    odd = odd_tile()
+    far_at, near_at = odd * (rows + STEPS), (1 - odd) * (rows + STEPS)
+    below, above = keep_sides(tiles)
     for group in range(2):
         for j in range(parts):
             lanes = slice(j * LANES, (j + 1) * LANES)
             for r in range(STEPS):
-                work[r, :, lanes] = fields(low_ref, group, r, j, parts)
-                work[rows + STEPS + r, :, lanes] = fields(high_ref, group, r, j, parts)
+                work[far_at + r, :, lanes] = far_ref[at_fields(0, brim, group, r, j, parts), :]
+                work[near_at + r, :, lanes] = near_ref[at_fields(0, brim, group, r, j, parts), :]
             for r in range(rows):
-                work[STEPS + r, :, lanes] = fields(own_ref, group, r, j, parts)
-        coefs = rates(group, (keep_ref[0], 1.0, keep_ref[1]), rate_x_ref, rate_y_ref)
+                work[STEPS + r, :, lanes] = own_ref[at_fields(0, size, group, r, j, parts), :]
+        coefs = rates(group, (below, 1.0, above), rate_x_ref, rate_y_ref)
 
         def emit(r, new, group=group):
-            terms = [new[j] * fields(members_ref, group, r, j, parts) for j in range(parts)]
+            terms = [new[j] * members_ref[at_fields(0, size, group, r, j, parts), :] for j in range(parts)]
             if group == 0:
                 for j in range(parts):
                     out_ref[r * 8 : r * 8 + 8, j * LANES : (j + 1) * LANES] = terms[j]
@@ -173,22 +214,26 @@
 
 def grad_body(
     rows,
+    tiles,
     factor,
     rate_x_ref,
     rate_y_ref,
-    keep_ref,
     alpha_ref,
     land_ref,
     members_ref,
-    members_low_ref,
-    members_high_ref,
+    far_ref,
+    near_ref,
     adjoint_ref,
-    adjoint_low_ref,
-    adjoint_high_ref,
+    adjoint_far_ref,
+    adjoint_near_ref,
     out_ref,
     work,
 ):
     parts = land_ref.shape[1] // LANES
+    size, brim = rows * parts, STEPS * parts
+    odd = odd_tile()
+    far_at, near_at = odd * (rows + STEPS), (1 - odd) * (rows + STEPS)
+    below, above = keep_sides(tiles)
 
     def twice(ref, r, lanes):
         four = ref[r * 4 : r * 4 + 4, lanes]
@@ -198,22 +243,20 @@
         for j in range(parts):
             lanes = slice(j * LANES, (j + 1) * LANES)
             for r in range(STEPS):
-                work[r, :, lanes] = fields(members_low_ref, group, r, j, parts) * twice(adjoint_low_ref, r, lanes)
-                work[rows + STEPS + r, :, lanes] = fields(members_high_ref, group, r, j, parts) * twice(
-                    adjoint_high_ref, r, lanes
-                )
+                at = at_fields(16 * brim, brim, group, r, j, parts)
+                work[far_at + r, :, lanes] = far_ref[at, :] * twice(adjoint_far_ref, r, lanes)
+                work[near_at + r, :, lanes] = near_ref[at, :] * twice(adjoint_near_ref, r, lanes)
             for r in range(rows):
-                work[STEPS + r, :, lanes] = (
-                    fields(members_ref, group, r, j, parts) * adjoint_ref[r * 8 : r * 8 + 8, lanes]
-                )
-        coefs = rates(group, (keep_ref[0], 1.0, keep_ref[1]), rate_x_ref, rate_y_ref)
+                own = members_ref[at_fields(0, size, group, r, j, parts), :]
+                work[STEPS + r, :, lanes] = own * adjoint_ref[r * 8 : r * 8 + 8, lanes]
+        coefs = rates(group, (below, 1.0, above), rate_x_ref, rate_y_ref)
 
         def emit(r, new, group=group):
             for j in range(parts):
                 lanes = slice(j * LANES, (j + 1) * LANES)
-                land = jnp.broadcast_to(land_ref[r : r + 1, lanes], (8, LANES)) * factor
-                value = fields(alpha_ref, group, r, j, parts) + land * new[j]
-                out_ref[at_fields(out_ref, group, r, j, parts), :] = value
+                land = jnp.broadcast_to(land_ref[r : r + 1, lanes].astype(F32), (8, LANES)) * factor
+                at = at_fields(0, size, group, r, j, parts)
+                out_ref[at, :] = alpha_ref[at, :] + land * new[j]
 
         smooth_rows(work, rows, coefs, emit)
 
@@ -255,11 +298,21 @@
             rest = 0.0 if previous is None else jnp.where(previous, upper, 0.0)
             total = total + jnp.where(at, lower, rest) * value
             previous = at
-        out_ref[s : s + 1, :] = jnp.sum(total, axis=0, keepdims=True)
+        total = jnp.sum(total, axis=0, keepdims=True)
+        for k in range(out_ref.shape[0]):
+            out_ref[k, s : s + 1, :] = total
+
+
+def add_body(in_ref, out_ref):
+    total = in_ref[0]
+    for k in range(1, in_ref.shape[0]):
+        total = total + in_ref[k]
+    for k in range(out_ref.shape[0]):
+        out_ref[k] = total
 
 
 def spread_body(
-    rows, slots, tiles, factor, me_ref, raw_ref, comps_ref, sums_ref, own_ref, low_ref, high_ref, back_ref, left, total
+    rows, slots, tiles, factor, raw_ref, comps_ref, sums_ref, own_ref, far_ref, near_ref, back_ref, left, total
 ):
     columns = own_ref.shape[1]
     count = comps_ref.shape[1]
@@ -267,7 +320,7 @@
     for k in range(1, sums_ref.shape[0]):
         hofx = hofx + sums_ref[k]
     hofx = factor * hofx
-    mine = iota((tiles, count), 1) == me_ref[0] * tiles + iota((tiles, count), 0)
+    mine = iota((tiles, count), 1) == lax.axis_index("mem") * tiles + iota((tiles, count), 0)
     back_ref[...] = lax.dot_general(
         jnp.where(mine, 1.0, 0.0),
         hofx,
@@ -302,11 +355,11 @@
         moved = jnp.where(lane == 0, 0.0, pltpu.roll(pltpu.roll(both, 4, 0), 1, 1))
         four = both + moved
         own_ref[g * 8 : g * 8 + 8, :] = jnp.where(half, four, pltpu.roll(four, 4, 0))
-        if g < STEPS:
-            low_ref[g * 4 : g * 4 + 4, :] = four[:4]
-        if g >= rows - STEPS:
-            at = g - (rows - STEPS)
-            high_ref[at * 4 : at * 4 + 4, :] = four[:4]
+    odd = odd_tile()
+    first, last = odd * (rows - STEPS), (1 - odd) * (rows - STEPS)
+    for ref, start in ((far_ref, first), (near_ref, last)):
+        for r in range(STEPS):
+            ref[r * 4 : r * 4 + 4, :] = own_ref[pl.ds(pl.multiple_of((start + r) * 8, 8), 8), :][:4]
 
 
 def on_device(
@@ -328,120 +381,117 @@
     factor = (mems * members - 1) ** (-0.5)
     slots = 16
     inner = math.isqrt(mems)
-    near = [[i * inner + j for j in range(inner)] for i in range(inner)]
-    far = [[i * inner + j for i in range(inner)] for j in range(inner)]
-    forward = [(i, i + 1) for i in range(tiles - 1)]
-    backward = [(i + 1, i) for i in range(tiles - 1)]
-    place = lax.axis_index("tile")
-    keep = jnp.stack([place > 0, place < tiles - 1]).astype(F32)
-    me = lax.axis_index("mem").astype(jnp.int32).reshape(1)
-    flat = (members * levels * rows * columns // LANES, LANES)
-
-    def exchange(low_rows, high_rows):
-        return lax.ppermute(high_rows, "tile", forward), lax.ppermute(low_rows, "tile", backward)
-
-    land = land_mask.astype(F32)
-    own = land * alpha
-    low, high = exchange(tiled(own[:, :, :STEPS]), tiled(own[:, :, rows - STEPS :]))
-    own = tiled(own)
-
-    tile_row = obs_tile.reshape(1, -1).astype(F32)
-    data = jnp.concatenate(
-        [
-            obs_col.astype(F32)[None],
-            (obs_row * levels + obs_lev).astype(F32)[None],
-            obs_weights,
-            obs_value[None],
-            obs_rinv[None],
-        ],
-        axis=0,
-    )
+    near_group = [[i * inner + j for j in range(inner)] for i in range(inner)]
+    far_group = [[i * inner + j for i in range(inner)] for j in range(inner)]
+    pairs = [(i, i + 1) for i in range(0, tiles - 1, 2)]
+    near_pairs = pairs + [(b, a) for a, b in pairs]
+    pairs = [(i, i + 1) for i in range(1, tiles - 1, 2)]
+    far_pairs = pairs + [(b, a) for a, b in pairs]
+    size = members * levels * rows * columns // LANES
+    brim = members * levels * STEPS * columns // LANES
+
+    def exchange(far, near):
+        return lax.ppermute(far, "tile", far_pairs), lax.ppermute(near, "tile", near_pairs)
+
+    alpha_tiles = tiled(alpha)
+    own, masked, far, near = call(
+        prep_body,
+        (
+            jax.ShapeDtypeStruct((size, LANES), F32),
+            jax.ShapeDtypeStruct((size, LANES), F32),
+            jax.ShapeDtypeStruct((2 * brim, LANES), F32),
+            jax.ShapeDtypeStruct((2 * brim, LANES), F32),
+        ),
+        vmem(3),
+        name="prep",
+    )(alpha_tiles, perturbs, land_mask)
+    halo_far, halo_near = exchange(far, near)
+
+    count = obs_row.shape[0]
+    tile_row = obs_tile.reshape(1, count)
     width = COMPS * slots
     sent = call(
-        functools.partial(pack_body, tiles, slots),
+        functools.partial(pack_body, tiles, slots, levels),
         jax.ShapeDtypeStruct((tiles, width), F32),
-        vmem(2),
+        [pl.BlockSpec(memory_space=pl.ANY)] + vmem(7),
+        [pltpu.VMEM((COMPS, count), F32)],
+        flops=PACK_FLOPS,
         name="pack",
-    )(tile_row, data)
+    )(
+        far,
+        tile_row,
+        obs_row.reshape(1, count),
+        obs_col.reshape(1, count),
+        obs_lev.reshape(1, count),
+        obs_weights,
+        obs_value.reshape(1, count),
+        obs_rinv.reshape(1, count),
+    )
     routed = lax.all_to_all(sent, "tile", split_axis=0, concat_axis=0, tiled=True)
+    count = mems * tiles
     raw = lax.all_to_all(
         jnp.broadcast_to(routed[None], (mems, tiles, width)), "mem", split_axis=0, concat_axis=0, tiled=True
-    ).reshape(mems * tiles, width)
-
-    masked = land * perturbs.astype(F32)
-    members_low, members_high = exchange(tiled(masked[:, :, :STEPS]), tiled(masked[:, :, rows - STEPS :]))
-    masked = tiled(masked)
+    ).reshape(count, width)
 
     work = pltpu.VMEM((rows + 2 * STEPS, 8, columns), F32)
     partial = call(
-        functools.partial(partial_body, rows),
+        functools.partial(partial_body, rows, tiles),
         jax.ShapeDtypeStruct((8 * rows, columns), F32),
-        [SMEM] * 3 + vmem(4),
+        [SMEM] * 2 + vmem(4),
         [work],
-        flops=2 * 10**7,
-        moved=2 * 10**6,
+        flops=PARTIAL_FLOPS,
         name="partial",
-    )(diff_x, diff_y, keep, own, low, high, masked)
-
-    count = mems * tiles
+    )(diff_x, diff_y, own, halo_far, halo_near, masked)
+    copies = jax.ShapeDtypeStruct((inner, slots, count), F32)
     comps, found = call(
         functools.partial(interpolate_body, rows, slots),
-        (jax.ShapeDtypeStruct((width, count), F32), jax.ShapeDtypeStruct((slots, count), F32)),
+        (jax.ShapeDtypeStruct((width, count), F32), copies),
         vmem(2),
         [pltpu.VMEM((16 * rows, columns), BF16)],
         name="interpolate",
     )(raw, partial)
 
     def gather(x, groups):
-        return lax.all_to_all(
-            jnp.broadcast_to(x[None], (inner,) + x.shape),
-            "mem",
-            split_axis=0,
-            concat_axis=0,
-            axis_index_groups=groups,
-            tiled=True,
-        )
-
-    sums = gather(jnp.sum(gather(found, near), axis=0), far)
-    adjoint, adjoint_first, adjoint_last, back = call(
+        return lax.all_to_all(x, "mem", split_axis=0, concat_axis=0, axis_index_groups=groups, tiled=True)
+
+    sums = gather(call(add_body, copies, vmem(1), name="add")(gather(found, near_group)), far_group)
+    edge = jax.ShapeDtypeStruct((levels * STEPS, columns), F32)
+    adjoint, edge_far, edge_near, back = call(
         functools.partial(spread_body, rows, slots, tiles, factor),
         (
             jax.ShapeDtypeStruct((8 * rows, columns), F32),
-            jax.ShapeDtypeStruct((levels * STEPS, columns), F32),
-            jax.ShapeDtypeStruct((levels * STEPS, columns), F32),
+            edge,
+            edge,
             jax.ShapeDtypeStruct((tiles, slots), F32),
         ),
-        [SMEM] + vmem(3),
+        vmem(3),
         [pltpu.VMEM((16 * rows, count), BF16), pltpu.VMEM((16 * rows, columns), F32)],
         name="spread",
-    )(me, raw, comps, sums)
-    adjoint_low, adjoint_high = exchange(adjoint_first, adjoint_last)
+    )(raw, comps, sums)
+    adjoint_far, adjoint_near = exchange(edge_far, edge_near)
     returned = lax.all_to_all(back, "tile", split_axis=0, concat_axis=0, tiled=True)
 
     grad = call(
-        functools.partial(grad_body, rows, factor),
-        jax.ShapeDtypeStruct(flat, F32),
-        [SMEM] * 3 + vmem(8),
+        functools.partial(grad_body, rows, tiles, factor),
+        jax.ShapeDtypeStruct((size, LANES), F32),
+        [SMEM] * 2 + vmem(8),
         [work],
-        flops=2 * 10**7,
-        moved=2 * 10**6,
         name="grad",
     )(
         diff_x,
         diff_y,
-        keep,
-        tiled(alpha),
-        land,
+        alpha_tiles,
+        land_mask,
         masked,
-        members_low,
-        members_high,
+        halo_far,
+        halo_near,
         adjoint,
-        adjoint_low,
-        adjoint_high,
+        adjoint_far,
+        adjoint_near,
     )
     hofx = call(
         unpack_body,
-        jax.ShapeDtypeStruct((1, tile_row.shape[1]), F32),
+        jax.ShapeDtypeStruct((1, obs_row.shape[0]), F32),
         vmem(2),
         name="unpack",
     )(tile_row, returned)

time: 139 us -> 128 us (0.921)
  waiting for transfers between devices: 18.8 us -> 4 us
  blocking collectives: 58.3 us -> 70.8 us
  starting transfers between devices: 37.1 us -> 27.7 us
  other arithmetic: 1.67 us -> 0 us
  Pallas kernels: 17.8 us -> 19.3 us
    all_to_all x0 -> x2, blocking collectives: none -> 14.9 us  [gather(): lax.all_to_all(x, 'mem', split_axis=0, concat_axis=0, axis_index_groups=g...]
    ppermute x6 -> x4, waiting for transfers between devices: 13.5 us -> 0.01 us  [the longest x2 0.01 us: exchange(): lax.ppermute(near, 'tile', near_pairs)]
    all_to_all x2 -> x0, starting transfers between devices: 11.9 us -> none  [gather(): lax.all_to_all(jnp.broadcast_to(x[None], (inner,) + x.shape), 'mem', spli...]
    all_to_all x2 -> x0, waiting for transfers between devices: 5.34 us -> none  [gather(): lax.all_to_all(jnp.broadcast_to(x[None], (inner,) + x.shape), 'mem', spli...]
    all_to_all x1, waiting for transfers between devices: 0.01 us -> 3.99 us  [on_device(): lax.all_to_all(jnp.broadcast_to(routed[None], (mems, tiles, width)), 'mem...]
    unnamed x12 -> x28, local copies, waits for them, and re-layouts: 0.69 us -> 4.13 us
    all_to_all x1, blocking collectives: 24.9 us -> 21.8 us  [on_device(): lax.all_to_all(back, 'tile', split_axis=0, concat_axis=0, tiled=True)]
    ppermute x6 -> x4, starting transfers between devices: 19.6 us -> 22.3 us  [the longest x2 11.6 us: exchange(): lax.ppermute(far, 'tile', far_pairs)]
  transfers between devices with their start and end apart: 9 -> 5, of which waited for: 3 -> 1; matrix products, arithmetic and copies ran while one was open for 1% -> 1% of each run, Pallas kernels for 6% -> 5%
where the time goes in v2:
time: 128 us; the launch traced here: 127 us
  blocking collectives  70.8 us (55%)
  starting transfers between devices  27.7 us (22%)
  Pallas kernels  19.3 us (15%)
  local copies, waits for them, and re-layouts  4.86 us (4%)
  waiting for transfers between devices  4 us (3%)
    all_to_all x1, blocking collectives, on_device(): lax.all_to_all(sent, 'tile', split_axis=0, concat_axis=0, tiled=True)  34.1 us
    all_to_all x1, blocking collectives, on_device(): lax.all_to_all(back, 'tile', split_axis=0, concat_axis=0, tiled=True)  21.8 us
    all_to_all x2, blocking collectives, gather(): lax.all_to_all(x, 'mem', split_axis=0, concat_axis=0, axis_index_groups=g...  14.9 us
    ppermute x2, starting transfers between devices, exchange(): lax.ppermute(far, 'tile', far_pairs)  11.6 us
    ppermute x2, starting transfers between devices, exchange(): lax.ppermute(near, 'tile', near_pairs)  10.7 us
    all_to_all x1, starting transfers between devices, on_device(): lax.all_to_all(jnp.broadcast_to(routed[None], (mems, tiles, width)), 'mem...  5.39 us
    pallas_call x1, Pallas kernels, on_device(): call(functools.partial(grad_body, rows, tiles, factor), jax.ShapeDtypeStr...  5.38 us
    pallas_call x1, Pallas kernels, on_device(): call(functools.partial(partial_body, rows, tiles), jax.ShapeDtypeStruct((...  4.99 us
  transfers between devices with their start and end apart: 5, of which 1 were waited for; matrix products, arithmetic and copies ran while one was open for 1% of the time, Pallas kernels for 5%

profile of v2, /device:TPU:1, one launch (start us, length us, event | category | flops | bytes accessed | tf_op | source)
XLA Modules:
  0.0 127.4 jit_solution(18000360593248602169)
XLA Ops:
  0.6 1.0 copy-done
  1.7 0.9 copy-done.2
  2.6 0.8 copy-done.3
  3.4 0.9 prep.1
  4.3 8.8 %collective-permute-start.1 = (f32[1024,128]{1,0:T(8,128)}, f32[1024,128]{1,0:T(8,128)S(1)}, u32[]{:S(2)}, u32[]{:S(2)}) collective-permute-start(f32[1024,128]{1,0:T(8,128)} %get-tuple-element.14), channel_id=1, source_target_pairs={{0,16},{32,48},{64,80},{96,112},{128,144},{160,176},{192,208},{224... | collective-permute-start | bytes 1572872 | tf_op jit(solution)/shard_map/ppermute | solution.py:394
  13.1 3.3 %collective-permute-start = (f32[1024,128]{1,0:T(8,128)S(1)}, f32[1024,128]{1,0:T(8,128)S(1)}, u32[]{:S(2)}, u32[]{:S(2)}) collective-permute-start(f32[1024,128]{1,0:T(8,128)S(1)} %get-tuple-element.13.unused_ref), channel_id=1, source_target_pairs={{16,32},{48,64},{80,96},{112,128},{144,160},{176,192},{208,224},{2... | collective-permute-start | bytes 1572872 | tf_op jit(solution)/shard_map/ppermute | solution.py:394
  16.5 0.0 copy-start.11
  16.5 0.0 copy-start.12
  16.5 0.6 copy-done.9
  17.1 0.0 copy-done.10
  17.2 0.0 copy-done.11
  17.2 0.0 copy-done.12
  17.2 0.0 copy-done.13
  17.2 0.0 copy-done.8
  17.2 0.0 copy-done.5
  17.2 0.6 pack.1
  17.8 34.1 %all_to_all.35 = f32[32,1,128]{2,1,0:T(1,128)S(1)} all-to-all(f32[32,1,128]{2,1,0:T(1,128)S(1)} %bitcast.32), channel_id=1, replica_groups=mesh['tile'=32,'mem'=16] {'tile'}, dimensions={0} | all-to-all | bytes 32768 | tf_op jit(solution)/shard_map/all_to_all | solution.py:430
  51.9 0.7 broadcast_in_dim.9
  52.6 5.4 %all-to-all-start.1 = ((f32[16,32,128]{2,1,0:T(8,128)}), f32[16,32,128]{2,1,0:T(8,128)S(1)}, u32[]{:S(2)}, u32[]{:S(2)}) async-start(f32[16,32,128]{2,1,0:T(8,128)} %broadcast_in_dim.9), calls=%async_computation.1 | async-start | bytes 524288 | tf_op jit(solution)/shard_map/all_to_all | solution.py:432
  58.1 0.6 copy-done.6
  58.7 0.0 copy-done.7
  58.7 5.0 %partial.1.field_ref = f32[128,512]{1,0:T(8,128)S(1)} custom-call(f32[4]{0:T(128)S(1)} %copy-done.6, f32[4]{0:T(128)S(1)} %copy-done.7, f32[1024,128]{1,0:T(8,128)S(1)} %get-tuple-element.15.own_ref, f32[1024,128]{1,0:T(8,128)S(1)} %collective-permute-done.far_ref, f32[1024,128]{1,0:T(8,128)S(1)} %collective-permute-done.1.near_ref, ...), custom_call_target="tpu_custom_call" | custom-call | flops 99999997952 | tf_op jit(solution)/shard_map/partial/pallas_call | solution.py:437
  63.7 4.0 %all-to-all-done.1 = f32[16,32,128]{2,1,0:T(8,128)S(1)} async-done(((f32[16,32,128]{2,1,0:T(8,128)}), f32[16,32,128]{2,1,0:T(8,128)S(1)}, u32[]{:S(2)}, u32[]{:S(2)}) %all-to-all-start.1) | async-done | bytes 262176 | tf_op jit(solution)/shard_map/all_to_all | solution.py:432
  67.7 3.4 %interpolate.1 = (f32[128,512]{1,0:T(8,128)S(1)}, f32[4,16,512]{2,1,0:T(8,128)S(1)}) custom-call(f32[512,128]{1,0:T(8,128)S(1)} %bitcast.26, f32[128,512]{1,0:T(8,128)S(1)} %partial.1.field_ref), custom_call_target="tpu_custom_call" | custom-call | tf_op jit(solution)/shard_map/interpolate/pallas_call | solution.py:446
  71.1 7.2 %all_to_all.36.in_ref = f32[4,16,512]{2,1,0:T(8,128)S(1)} all-to-all(f32[4,16,512]{2,1,0:T(8,128)S(1)} %get-tuple-element.17), channel_id=1, replica_groups={{0,1,2,3},{4,5,6,7},{8,9,10,11},{12,13,14,15},{16,17,18,19},{20,21,22,2..., dimensions={0} | all-to-all | bytes 262144 | tf_op jit(solution)/shard_map/all_to_all | solution.py:455
  78.3 7.8 %all_to_all.37.sums_ref = f32[4,16,512]{2,1,0:T(8,128)S(1)} all-to-all(f32[4,16,512]{2,1,0:T(8,128)S(1)} %add.1), channel_id=1, replica_groups={{0,4,8,12},{1,5,9,13},{2,6,10,14},{3,7,11,15},{16,20,24,28},{17,21,25,2..., dimensions={0} | all-to-all | bytes 262144 | tf_op jit(solution)/shard_map/all_to_all | solution.py:455
  86.0 3.2 %spread.1 = (f32[128,512]{1,0:T(8,128)S(1)}, f32[32,512]{1,0:T(8,128)S(1)}, f32[32,512]{1,0:T(8,128)S(1)}, f32[32,16]{1,0:T(8,128)S(1)}) custom-call(f32[512,128]{1,0:T(8,128)S(1)} %bitcast.27, f32[128,512]{1,0:T(8,128)S(1)} %get-tuple-element.16.comps_ref, f32[4,16,512]{2,1,0:T(8,128)S(1)} %all_to_all.37.sums_ref), custom_call_target="tpu_custom_call" | custom-call | tf_op jit(solution)/shard_map/spread/pallas_call | solution.py:459
  89.3 8.3 %collective-permute-start.2 = (f32[32,512]{1,0:T(8,128)S(1)}, f32[32,512]{1,0:T(8,128)S(1)}, u32[]{:S(2)}, u32[]{:S(2)}) collective-permute-start(f32[32,512]{1,0:T(8,128)S(1)} %get-tuple-element.19), channel_id=1, source_target_pairs={{16,32},{48,64},{80,96},{112,128},{144,160},{176,192},{208,224},{2... | collective-permute-start | bytes 196616 | tf_op jit(solution)/shard_map/ppermute | solution.py:394
  97.5 1.9 %collective-permute-start.3 = (f32[32,512]{1,0:T(8,128)S(1)}, f32[32,512]{1,0:T(8,128)S(1)}, u32[]{:S(2)}, u32[]{:S(2)}) collective-permute-start(f32[32,512]{1,0:T(8,128)S(1)} %get-tuple-element.20), channel_id=1, source_target_pairs={{0,16},{32,48},{64,80},{96,112},{128,144},{160,176},{192,208},{224... | collective-permute-start | bytes 196616 | tf_op jit(solution)/shard_map/ppermute | solution.py:394
  99.5 21.8 %all_to_all.38 = f32[32,1,16]{2,1,0:T(1,128)S(1)} all-to-all(f32[32,1,16]{2,1,0:T(1,128)S(1)} %bitcast.31), channel_id=1, replica_groups=mesh['tile'=32,'mem'=16] {'tile'}, dimensions={0} | all-to-all | bytes 4096 | tf_op jit(solution)/shard_map/all_to_all | solution.py:472
  121.2 0.8 unpack.1
  122.0 5.4 %grad.1 = f32[1024,128]{1,0:T(8,128)} custom-call(f32[4]{0:T(128)S(1)} %copy-done.6, f32[4]{0:T(128)S(1)} %copy-done.7, f32[1024,128]{1,0:T(8,128)S(1)} %bitcast.29, s32[16,512]{1,0:T(8,128)S(1)} %copy-done.4, f32[1024,128]{1,0:T(8,128)S(1)} %get-tuple-element.12.members_ref, f32[1024,128]{1,0:T(8,128)S(1)} %collective-permute-done.far_ref, ...), custom_call_target="tpu_custom_call" | custom-call | tf_op jit(solution)/shard_map/grad/pallas_call | solution.py:474
  (19 shorter events, 0.1 us)
Async XLA Ops:
  0.6 1.0 copy-start
  1.7 0.9 copy-start.2
  2.6 0.8 copy-start.3
  4.3 53.7 %collective-permute-start.1 = (f32[1024,128]{1,0:T(8,128)}, f32[1024,128]{1,0:T(8,128)S(1)}, u32[]{:S(2)}, u32[]{:S(2)}) collective-permute-start(f32[1024,128]{1,0:T(8,128)} %get-tuple-element.14), channel_id=1, source_target_pairs={{0,16},{32,48},{64,80},{96,112},{128,144},{160,176},{192,208},{224... | collective-permute-start | bytes 1572872 | tf_op jit(solution)/shard_map/ppermute | solution.py:394
  13.1 44.9 %collective-permute-start = (f32[1024,128]{1,0:T(8,128)S(1)}, f32[1024,128]{1,0:T(8,128)S(1)}, u32[]{:S(2)}, u32[]{:S(2)}) collective-permute-start(f32[1024,128]{1,0:T(8,128)S(1)} %get-tuple-element.13.unused_ref), channel_id=1, source_target_pairs={{16,32},{48,64},{80,96},{112,128},{144,160},{176,192},{208,224},{2... | collective-permute-start | bytes 1572872 | tf_op jit(solution)/shard_map/ppermute | solution.py:394
  16.5 0.7 copy-start.9
  16.5 0.7 copy-start.10
  16.5 0.7 copy-start.11
  16.5 0.7 copy-start.12
  16.5 0.7 copy-start.13
  16.5 0.7 copy-start.8
  16.5 0.7 copy-start.5
  52.6 15.1 %all-to-all-start.1 = ((f32[16,32,128]{2,1,0:T(8,128)}), f32[16,32,128]{2,1,0:T(8,128)S(1)}, u32[]{:S(2)}, u32[]{:S(2)}) async-start(f32[16,32,128]{2,1,0:T(8,128)} %broadcast_in_dim.9), calls=%async_computation.1 | async-start | bytes 524288 | tf_op jit(solution)/shard_map/all_to_all | solution.py:432
  58.0 0.7 copy-start.6
  58.1 0.7 copy-start.7
  78.3 43.7 %copy-start.1 = (f32[4,4,16,512]{3,2,1,0:T(8,128)S(1)}, f32[4,4,16,512]{3,2,1,0:T(8,128)}, u32[]{:S(2)}) copy-start(f32[4,4,16,512]{3,2,1,0:T(8,128)} %param.12) | copy-start | bytes 1572868
  89.2 32.8 %copy-start.4 = (s32[16,512]{1,0:T(8,128)S(1)}, s32[16,512]{1,0:T(8,128)}, u32[]{:S(2)}) copy-start(s32[16,512]{1,0:T(8,128)} %land_ref.3) | copy-start | bytes 98308
  89.3 32.7 %collective-permute-start.2 = (f32[32,512]{1,0:T(8,128)S(1)}, f32[32,512]{1,0:T(8,128)S(1)}, u32[]{:S(2)}, u32[]{:S(2)}) collective-permute-start(f32[32,512]{1,0:T(8,128)S(1)} %get-tuple-element.19), channel_id=1, source_target_pairs={{16,32},{48,64},{80,96},{112,128},{144,160},{176,192},{208,224},{2... | collective-permute-start | bytes 196616 | tf_op jit(solution)/shard_map/ppermute | solution.py:394
  97.5 24.5 %collective-permute-start.3 = (f32[32,512]{1,0:T(8,128)S(1)}, f32[32,512]{1,0:T(8,128)S(1)}, u32[]{:S(2)}, u32[]{:S(2)}) collective-permute-start(f32[32,512]{1,0:T(8,128)S(1)} %get-tuple-element.20), channel_id=1, source_target_pairs={{0,16},{32,48},{64,80},{96,112},{128,144},{160,176},{192,208},{224... | collective-permute-start | bytes 196616 | tf_op jit(solution)/shard_map/ppermute | solution.py:394

commit v3 on v2

--- a/solution.py
+++ b/solution.py
@@ -1,5 +1,4 @@
 import functools
-import math
 
 import jax
 import jax.numpy as jnp
@@ -14,7 +13,7 @@
 HIGHEST = lax.Precision.HIGHEST
 F32 = jnp.float32
 BF16 = jnp.bfloat16
-PACK_FLOPS = 10**11
+COPY_FLOPS = 0
 PARTIAL_FLOPS = 10**11
 
 
@@ -36,6 +35,7 @@
 
 VMEM = pl.BlockSpec(memory_space=pltpu.VMEM)
 SMEM = pl.BlockSpec(memory_space=pltpu.SMEM)
+ANY = pl.BlockSpec(memory_space=pl.ANY)
 
 
 def vmem(count):
@@ -54,7 +54,7 @@
 
 
 def pack_body(
-    tiles, slots, levels, unused_ref, tile_ref, row_ref, col_ref, lev_ref, weights_ref, value_ref, rinv_ref, send_ref, data_ref
+    tiles, slots, levels, tile_ref, row_ref, col_ref, lev_ref, weights_ref, value_ref, rinv_ref, send_ref, data_ref
 ):
     tile_row = tile_ref[...].astype(F32)
     data_ref[0:1, :] = col_ref[...].astype(F32)
@@ -149,7 +149,7 @@
     return jnp.where(place > 0, 1.0, 0.0), jnp.where(place < tiles - 1, 1.0, 0.0)
 
 
-def prep_body(alpha_ref, members_ref, land_ref, own_ref, masked_ref, far_ref, near_ref):
+def prep_body(unused_ref, alpha_ref, members_ref, land_ref, own_ref, masked_ref, far_ref, far_members_ref, near_ref):
     members, levels, rows, columns = members_ref.shape
     parts = columns // LANES
     size = rows * parts
@@ -167,11 +167,12 @@
     odd = odd_tile()
     first = odd * (size - brim)
     last = (1 - odd) * (size - brim)
-    for source, start in ((own_ref, 0), (masked_ref, count * brim)):
+    for source, far, start in ((own_ref, far_ref, 0), (masked_ref, far_members_ref, count * brim)):
         for f in range(count):
-            to = slice(start + f * brim, start + (f + 1) * brim)
-            far_ref[to, :] = source[pl.ds(pl.multiple_of(f * size + first, 8), brim), :]
-            near_ref[to, :] = source[pl.ds(pl.multiple_of(f * size + last, 8), brim), :]
+            to = f * brim
+            far[to : to + brim, :] = source[pl.ds(pl.multiple_of(f * size + first, 8), brim), :]
+            to = start + f * brim
+            near_ref[to : to + brim, :] = source[pl.ds(pl.multiple_of(f * size + last, 8), brim), :]
 
 
 def partial_body(rows, tiles, rate_x_ref, rate_y_ref, own_ref, far_ref, near_ref, members_ref, out_ref, work):
@@ -243,8 +244,9 @@
         for j in range(parts):
             lanes = slice(j * LANES, (j + 1) * LANES)
             for r in range(STEPS):
+                at = at_fields(0, brim, group, r, j, parts)
+                work[far_at + r, :, lanes] = far_ref[at, :] * twice(adjoint_far_ref, r, lanes)
                 at = at_fields(16 * brim, brim, group, r, j, parts)
-                work[far_at + r, :, lanes] = far_ref[at, :] * twice(adjoint_far_ref, r, lanes)
                 work[near_at + r, :, lanes] = near_ref[at, :] * twice(adjoint_near_ref, r, lanes)
             for r in range(rows):
                 own = members_ref[at_fields(0, size, group, r, j, parts), :]
@@ -277,7 +279,7 @@
     return jnp.broadcast_to(row, (8, count)), lower, upper
 
 
-def interpolate_body(rows, slots, raw_ref, field_ref, comps_ref, out_ref, pieces):
+def interpolate_body(rows, slots, unused_ref, raw_ref, field_ref, comps_ref, out_ref, pieces, values):
     comps_ref[...] = raw_ref[...].T
     columns = field_ref.shape[1]
     count = comps_ref.shape[1]
@@ -298,17 +300,14 @@
             rest = 0.0 if previous is None else jnp.where(previous, upper, 0.0)
             total = total + jnp.where(at, lower, rest) * value
             previous = at
-        total = jnp.sum(total, axis=0, keepdims=True)
-        for k in range(out_ref.shape[0]):
-            out_ref[k, s : s + 1, :] = total
-
-
-def add_body(in_ref, out_ref):
-    total = in_ref[0]
-    for k in range(1, in_ref.shape[0]):
-        total = total + in_ref[k]
+        values[s : s + 1, :] = jnp.sum(total, axis=0, keepdims=True)
     for k in range(out_ref.shape[0]):
-        out_ref[k] = total
+        out_ref[k] = values[...]
+
+
+def copies_body(unused_ref, in_ref, out_ref):
+    for k in range(out_ref.shape[0]):
+        out_ref[k] = in_ref[...]
 
 
 def spread_body(
@@ -380,9 +379,6 @@
     tiles, mems = lax.axis_size("tile"), lax.axis_size("mem")
     factor = (mems * members - 1) ** (-0.5)
     slots = 16
-    inner = math.isqrt(mems)
-    near_group = [[i * inner + j for j in range(inner)] for i in range(inner)]
-    far_group = [[i * inner + j for i in range(inner)] for j in range(inner)]
     pairs = [(i, i + 1) for i in range(0, tiles - 1, 2)]
     near_pairs = pairs + [(b, a) for a, b in pairs]
     pairs = [(i, i + 1) for i in range(1, tiles - 1, 2)]
@@ -390,22 +386,11 @@
     size = members * levels * rows * columns // LANES
     brim = members * levels * STEPS * columns // LANES
 
-    def exchange(far, near):
-        return lax.ppermute(far, "tile", far_pairs), lax.ppermute(near, "tile", near_pairs)
-
-    alpha_tiles = tiled(alpha)
-    own, masked, far, near = call(
-        prep_body,
-        (
-            jax.ShapeDtypeStruct((size, LANES), F32),
-            jax.ShapeDtypeStruct((size, LANES), F32),
-            jax.ShapeDtypeStruct((2 * brim, LANES), F32),
-            jax.ShapeDtypeStruct((2 * brim, LANES), F32),
-        ),
-        vmem(3),
-        name="prep",
-    )(alpha_tiles, perturbs, land_mask)
-    halo_far, halo_near = exchange(far, near)
+    def to_far(x):
+        return lax.ppermute(x, "tile", far_pairs)
+
+    def to_near(x):
+        return lax.ppermute(x, "tile", near_pairs)
 
     count = obs_row.shape[0]
     tile_row = obs_tile.reshape(1, count)
@@ -413,12 +398,10 @@
     sent = call(
         functools.partial(pack_body, tiles, slots, levels),
         jax.ShapeDtypeStruct((tiles, width), F32),
-        [pl.BlockSpec(memory_space=pl.ANY)] + vmem(7),
+        vmem(7),
         [pltpu.VMEM((COMPS, count), F32)],
-        flops=PACK_FLOPS,
         name="pack",
     )(
-        far,
         tile_row,
         obs_row.reshape(1, count),
         obs_col.reshape(1, count),
@@ -428,10 +411,32 @@
         obs_rinv.reshape(1, count),
     )
     routed = lax.all_to_all(sent, "tile", split_axis=0, concat_axis=0, tiled=True)
+
+    alpha_tiles = tiled(alpha)
+    own, masked, far, far_members, near = call(
+        prep_body,
+        (
+            jax.ShapeDtypeStruct((size, LANES), F32),
+            jax.ShapeDtypeStruct((size, LANES), F32),
+            jax.ShapeDtypeStruct((brim, LANES), F32),
+            jax.ShapeDtypeStruct((brim, LANES), F32),
+            jax.ShapeDtypeStruct((2 * brim, LANES), F32),
+        ),
+        [ANY] + vmem(3),
+        name="prep",
+    )(routed, alpha_tiles, perturbs, land_mask)
+    halo_far, halo_near = to_far(far), to_near(near)
+
+    copied = call(
+        copies_body,
+        jax.ShapeDtypeStruct((mems, tiles, width), F32),
+        [ANY] + vmem(1),
+        flops=COPY_FLOPS,
+        name="copies",
+    )(far, routed)
     count = mems * tiles
-    raw = lax.all_to_all(
-        jnp.broadcast_to(routed[None], (mems, tiles, width)), "mem", split_axis=0, concat_axis=0, tiled=True
-    ).reshape(count, width)
+    raw = lax.all_to_all(copied, "mem", split_axis=0, concat_axis=0, tiled=True).reshape(count, width)
+    members_far = to_far(far_members)
 
     work = pltpu.VMEM((rows + 2 * STEPS, 8, columns), F32)
     partial = call(
@@ -442,19 +447,17 @@
         flops=PARTIAL_FLOPS,
         name="partial",
     )(diff_x, diff_y, own, halo_far, halo_near, masked)
-    copies = jax.ShapeDtypeStruct((inner, slots, count), F32)
     comps, found = call(
         functools.partial(interpolate_body, rows, slots),
-        (jax.ShapeDtypeStruct((width, count), F32), copies),
-        vmem(2),
-        [pltpu.VMEM((16 * rows, columns), BF16)],
+        (
+            jax.ShapeDtypeStruct((width, count), F32),
+            jax.ShapeDtypeStruct((mems, slots, count), F32),
+        ),
+        [ANY] + vmem(2),
+        [pltpu.VMEM((16 * rows, columns), BF16), pltpu.VMEM((slots, count), F32)],
         name="interpolate",
-    )(raw, partial)
-
-    def gather(x, groups):
-        return lax.all_to_all(x, "mem", split_axis=0, concat_axis=0, axis_index_groups=groups, tiled=True)
-
-    sums = gather(call(add_body, copies, vmem(1), name="add")(gather(found, near_group)), far_group)
+    )(members_far, raw, partial)
+    sums = lax.all_to_all(found, "mem", split_axis=0, concat_axis=0, tiled=True)
     edge = jax.ShapeDtypeStruct((levels * STEPS, columns), F32)
     adjoint, edge_far, edge_near, back = call(
         functools.partial(spread_body, rows, slots, tiles, factor),
@@ -468,7 +471,7 @@
         [pltpu.VMEM((16 * rows, count), BF16), pltpu.VMEM((16 * rows, columns), F32)],
         name="spread",
     )(raw, comps, sums)
-    adjoint_far, adjoint_near = exchange(edge_far, edge_near)
+    adjoint_far, adjoint_near = to_far(edge_far), to_near(edge_near)
     returned = lax.all_to_all(back, "tile", split_axis=0, concat_axis=0, tiled=True)
 
     grad = call(
@@ -483,7 +486,7 @@
         alpha_tiles,
         land_mask,
         masked,
-        halo_far,
+        members_far,
         halo_near,
         adjoint,
         adjoint_far,

time: 128 us -> 139 us (1.086)
  blocking collectives: 70.8 us -> 80.6 us
  waiting for transfers between devices: 4 us -> 5.73 us
  local copies, waits for them, and re-layouts: 4.86 us -> 3.39 us
    all_to_all x2 -> x1, blocking collectives: 14.9 us -> 24.6 us  [on_device(): sums = lax.all_to_all(found, 'mem', split_axis=0, concat_axis=0, tiled=True)]
    ppermute x4 -> x5, waiting for transfers between devices: 0.01 us -> 5.73 us  [the longest x3 5.73 us: to_far(): return lax.ppermute(x, 'tile', far_pairs)]
    all_to_all x1, waiting for transfers between devices: 3.99 us -> 0.01 us  [on_device(): lax.all_to_all(copied, 'mem', split_axis=0, concat_axis=0, tiled=True)]
    unnamed x28 -> x26, local copies, waits for them, and re-layouts: 4.13 us -> 3.39 us
    ppermute x4 -> x5, starting transfers between devices: 22.3 us -> 22.6 us  [the longest x3 18.2 us: to_far(): return lax.ppermute(x, 'tile', far_pairs)]
  transfers between devices with their start and end apart: 5 -> 6, of which waited for: 1 -> 2; matrix products, arithmetic and copies ran while one was open for 1% -> 0% of each run, Pallas kernels for 5% -> 5%
where the time goes in v3:
time: 139 us; the launch traced here: 138 us
  blocking collectives  80.6 us (58%)
  starting transfers between devices  28.1 us (20%)
  Pallas kernels  19.5 us (14%)
  waiting for transfers between devices  5.73 us (4%)
  local copies, waits for them, and re-layouts  3.39 us (2%)
    all_to_all x1, blocking collectives, on_device(): lax.all_to_all(sent, 'tile', split_axis=0, concat_axis=0, tiled=True)  33.4 us
    all_to_all x1, blocking collectives, on_device(): sums = lax.all_to_all(found, 'mem', split_axis=0, concat_axis=0, tiled=True)  24.6 us
    all_to_all x1, blocking collectives, on_device(): lax.all_to_all(back, 'tile', split_axis=0, concat_axis=0, tiled=True)  22.7 us
    ppermute x3, starting transfers between devices, to_far(): return lax.ppermute(x, 'tile', far_pairs)  18.2 us
    ppermute x3, waiting for transfers between devices, to_far(): return lax.ppermute(x, 'tile', far_pairs)  5.73 us
    all_to_all x1, starting transfers between devices, on_device(): lax.all_to_all(copied, 'mem', split_axis=0, concat_axis=0, tiled=True)  5.52 us
    pallas_call x1, Pallas kernels, on_device(): call(functools.partial(grad_body, rows, tiles, factor), jax.ShapeDtypeStr...  5.38 us
    pallas_call x1, Pallas kernels, on_device(): call(functools.partial(partial_body, rows, tiles), jax.ShapeDtypeStruct((...  5.01 us
  transfers between devices with their start and end apart: 6, of which 2 were waited for; matrix products, arithmetic and copies ran while one was open for 0% of the time, Pallas kernels for 5%

profile of v3, /device:TPU:1, one launch (start us, length us, event | category | flops | bytes accessed | tf_op | source)
XLA Modules:
  0.0 138.2 jit_solution(16127703705451843290)
XLA Ops:
  0.7 0.6 copy-done.10
  1.3 0.0 copy-done.8
  1.3 0.0 copy-done.9
  1.3 0.0 copy-done.4
  1.4 0.0 copy-done.6
  1.4 0.0 copy-done.7
  1.4 0.0 copy-done.5
  1.4 0.6 pack.1
  2.0 33.4 %all_to_all.32 = f32[32,1,128]{2,1,0:T(1,128)S(1)} all-to-all(f32[32,1,128]{2,1,0:T(1,128)S(1)} %bitcast.33), channel_id=1, replica_groups=mesh['tile'=32,'mem'=16] {'tile'}, dimensions={0} | all-to-all | bytes 32768 | tf_op jit(solution)/shard_map/all_to_all | solution.py:413
  35.3 1.0 copy-done
  36.4 0.9 copy-done.2
  37.3 0.2 prep.1
  37.5 2.5 %collective-permute-start.1 = (f32[1024,128]{1,0:T(8,128)S(1)}, f32[1024,128]{1,0:T(8,128)S(1)}, u32[]{:S(2)}, u32[]{:S(2)}) collective-permute-start(f32[1024,128]{1,0:T(8,128)S(1)} %get-tuple-element.15), channel_id=1, source_target_pairs={{0,16},{32,48},{64,80},{96,112},{128,144},{160,176},{192,208},{224... | collective-permute-start | bytes 1572872 | tf_op jit(solution)/shard_map/ppermute | solution.py:393
  40.0 2.1 %collective-permute-start.2 = (f32[512,128]{1,0:T(8,128)S(1)}, f32[512,128]{1,0:T(8,128)S(1)}, u32[]{:S(2)}, u32[]{:S(2)}) collective-permute-start(f32[512,128]{1,0:T(8,128)S(1)} %get-tuple-element.16.unused_ref), channel_id=1, source_target_pairs={{16,32},{48,64},{80,96},{112,128},{144,160},{176,192},{208,224},{2... | collective-permute-start | bytes 786440 | tf_op jit(solution)/shard_map/ppermute | solution.py:390
  42.1 0.7 copies.1
  42.9 5.5 %all-to-all-start.1 = ((f32[16,32,128]{2,1,0:T(8,128)}), f32[16,32,128]{2,1,0:T(8,128)S(1)}, u32[]{:S(2)}, u32[]{:S(2)}) async-start(f32[16,32,128]{2,1,0:T(8,128)} %copies.1), calls=%async_computation.1 | async-start | bytes 524288 | tf_op jit(solution)/shard_map/all_to_all | solution.py:438
  48.4 7.6 %collective-permute-start = (f32[512,128]{1,0:T(8,128)S(1)}, f32[512,128]{1,0:T(8,128)S(1)}, u32[]{:S(2)}, u32[]{:S(2)}) collective-permute-start(f32[512,128]{1,0:T(8,128)S(1)} %get-tuple-element.14), channel_id=1, source_target_pairs={{16,32},{48,64},{80,96},{112,128},{144,160},{176,192},{208,224},{2... | collective-permute-start | bytes 786440 | tf_op jit(solution)/shard_map/ppermute | solution.py:390
  56.0 2.6 %collective-permute-done.2.far_ref = f32[512,128]{1,0:T(8,128)S(1)} collective-permute-done((f32[512,128]{1,0:T(8,128)S(1)}, f32[512,128]{1,0:T(8,128)S(1)}, u32[]{:S(2)}, u32[]{:S(2)}) %collective-permute-start.2) | collective-permute-done | bytes 262176 | tf_op jit(solution)/shard_map/ppermute | solution.py:390
  58.6 0.0 collective-permute-done.1.near_ref
  58.6 0.7 copy-done.11
  59.3 0.0 copy-done.12
  59.3 5.0 %partial.1.field_ref = f32[128,512]{1,0:T(8,128)S(1)} custom-call(f32[4]{0:T(128)S(1)} %copy-done.11, f32[4]{0:T(128)S(1)} %copy-done.12, f32[1024,128]{1,0:T(8,128)S(1)} %get-tuple-element.17.own_ref, f32[512,128]{1,0:T(8,128)S(1)} %collective-permute-done.2.far_ref, f32[1024,128]{1,0:T(8,128)S(1)} %collective-permute-done.1.near_ref, ...), custom_call_target="tpu_custom_call" | custom-call | flops 99999997952 | tf_op jit(solution)/shard_map/partial/pallas_call | solution.py:442
  64.3 3.1 %collective-permute-done.unused_ref.far_ref = f32[512,128]{1,0:T(8,128)S(1)} collective-permute-done((f32[512,128]{1,0:T(8,128)S(1)}, f32[512,128]{1,0:T(8,128)S(1)}, u32[]{:S(2)}, u32[]{:S(2)}) %collective-permute-start) | collective-permute-done | bytes 262176 | tf_op jit(solution)/shard_map/ppermute | solution.py:390
  67.4 0.0 all-to-all-done.1
  67.5 3.4 %interpolate.1 = (f32[128,512]{1,0:T(8,128)S(1)}, f32[16,16,512]{2,1,0:T(8,128)S(1)}) custom-call(f32[512,128]{1,0:T(8,128)S(1)} %collective-permute-done.unused_ref.far_ref, f32[512,128]{1,0:T(8,128)S(1)} %bitcast.26, f32[128,512]{1,0:T(8,128)S(1)} %partial.1.field_ref), custom_call_target="tpu_custom_call" | custom-call | tf_op jit(solution)/shard_map/interpolate/pallas_call | solution.py:450
  70.8 24.6 %all_to_all.33.sums_ref = f32[16,16,512]{2,1,0:T(8,128)S(1)} all-to-all(f32[16,16,512]{2,1,0:T(8,128)S(1)} %get-tuple-element.19), channel_id=1, replica_groups=mesh['tile'=32,'mem'=16] {'mem'}, dimensions={0} | all-to-all | bytes 1048576 | tf_op jit(solution)/shard_map/all_to_all | solution.py:460
  95.5 3.5 %spread.1 = (f32[128,512]{1,0:T(8,128)S(1)}, f32[32,512]{1,0:T(8,128)S(1)}, f32[32,512]{1,0:T(8,128)S(1)}, f32[32,16]{1,0:T(8,128)S(1)}) custom-call(f32[512,128]{1,0:T(8,128)S(1)} %bitcast.27, f32[128,512]{1,0:T(8,128)S(1)} %get-tuple-element.18.comps_ref, f32[16,16,512]{2,1,0:T(8,128)S(1)} %all_to_all.33.sums_ref), custom_call_target="tpu_custom_call" | custom-call | tf_op jit(solution)/shard_map/spread/pallas_call | solution.py:462
  99.0 8.4 %collective-permute-start.3 = (f32[32,512]{1,0:T(8,128)S(1)}, f32[32,512]{1,0:T(8,128)S(1)}, u32[]{:S(2)}, u32[]{:S(2)}) collective-permute-start(f32[32,512]{1,0:T(8,128)S(1)} %get-tuple-element.21), channel_id=1, source_target_pairs={{16,32},{48,64},{80,96},{112,128},{144,160},{176,192},{208,224},{2... | collective-permute-start | bytes 196616 | tf_op jit(solution)/shard_map/ppermute | solution.py:390
  107.4 1.9 %collective-permute-start.4 = (f32[32,512]{1,0:T(8,128)S(1)}, f32[32,512]{1,0:T(8,128)S(1)}, u32[]{:S(2)}, u32[]{:S(2)}) collective-permute-start(f32[32,512]{1,0:T(8,128)S(1)} %get-tuple-element.22), channel_id=1, source_target_pairs={{0,16},{32,48},{64,80},{96,112},{128,144},{160,176},{192,208},{224... | collective-permute-start | bytes 196616 | tf_op jit(solution)/shard_map/ppermute | solution.py:393
  109.3 22.7 %all_to_all.34 = f32[32,1,16]{2,1,0:T(1,128)S(1)} all-to-all(f32[32,1,16]{2,1,0:T(1,128)S(1)} %bitcast.34), channel_id=1, replica_groups=mesh['tile'=32,'mem'=16] {'tile'}, dimensions={0} | all-to-all | bytes 4096 | tf_op jit(solution)/shard_map/all_to_all | solution.py:475
  132.0 0.8 unpack.1
  132.8 5.4 %grad.1 = f32[1024,128]{1,0:T(8,128)} custom-call(f32[4]{0:T(128)S(1)} %copy-done.11, f32[4]{0:T(128)S(1)} %copy-done.12, f32[1024,128]{1,0:T(8,128)S(1)} %bitcast.29, s32[16,512]{1,0:T(8,128)S(1)} %copy-done.3, f32[1024,128]{1,0:T(8,128)S(1)} %get-tuple-element.13.members_ref, f32[512,128]{1,0:T(8,128)S(1)} %collective-permute-done.unused_ref.far_ref, ...), custom_call_target="tpu_custom_call" | custom-call | tf_op jit(solution)/shard_map/grad/pallas_call | solution.py:477
  (17 shorter events, 0.0 us)
Async XLA Ops:
  0.6 0.7 copy-start.10
  0.6 0.7 copy-start.8
  0.7 0.7 copy-start.9
  0.7 0.7 copy-start.4
  0.7 0.7 copy-start.6
  0.7 0.7 copy-start.7
  0.7 0.7 copy-start.5
  1.4 33.9 %copy-start.3 = (s32[16,512]{1,0:T(8,128)S(1)}, s32[16,512]{1,0:T(8,128)}, u32[]{:S(2)}) copy-start(s32[16,512]{1,0:T(8,128)} %land_ref.3) | copy-start | bytes 98308
  35.3 1.0 copy-start
  36.4 0.9 copy-start.2
  37.5 21.1 %collective-permute-start.1 = (f32[1024,128]{1,0:T(8,128)S(1)}, f32[1024,128]{1,0:T(8,128)S(1)}, u32[]{:S(2)}, u32[]{:S(2)}) collective-permute-start(f32[1024,128]{1,0:T(8,128)S(1)} %get-tuple-element.15), channel_id=1, source_target_pairs={{0,16},{32,48},{64,80},{96,112},{128,144},{160,176},{192,208},{224... | collective-permute-start | bytes 1572872 | tf_op jit(solution)/shard_map/ppermute | solution.py:393
  40.0 18.6 %collective-permute-start.2 = (f32[512,128]{1,0:T(8,128)S(1)}, f32[512,128]{1,0:T(8,128)S(1)}, u32[]{:S(2)}, u32[]{:S(2)}) collective-permute-start(f32[512,128]{1,0:T(8,128)S(1)} %get-tuple-element.16.unused_ref), channel_id=1, source_target_pairs={{16,32},{48,64},{80,96},{112,128},{144,160},{176,192},{208,224},{2... | collective-permute-start | bytes 786440 | tf_op jit(solution)/shard_map/ppermute | solution.py:390
  42.9 24.6 %all-to-all-start.1 = ((f32[16,32,128]{2,1,0:T(8,128)}), f32[16,32,128]{2,1,0:T(8,128)S(1)}, u32[]{:S(2)}, u32[]{:S(2)}) async-start(f32[16,32,128]{2,1,0:T(8,128)} %copies.1), calls=%async_computation.1 | async-start | bytes 524288 | tf_op jit(solution)/shard_map/all_to_all | solution.py:438
  48.4 19.0 %collective-permute-start = (f32[512,128]{1,0:T(8,128)S(1)}, f32[512,128]{1,0:T(8,128)S(1)}, u32[]{:S(2)}, u32[]{:S(2)}) collective-permute-start(f32[512,128]{1,0:T(8,128)S(1)} %get-tuple-element.14), channel_id=1, source_target_pairs={{16,32},{48,64},{80,96},{112,128},{144,160},{176,192},{208,224},{2... | collective-permute-start | bytes 786440 | tf_op jit(solution)/shard_map/ppermute | solution.py:390
  58.6 0.7 copy-start.11
  58.6 0.7 copy-start.12
  95.5 37.3 %copy-start.1 = (f32[4,4,16,512]{3,2,1,0:T(8,128)S(1)}, f32[4,4,16,512]{3,2,1,0:T(8,128)}, u32[]{:S(2)}) copy-start(f32[4,4,16,512]{3,2,1,0:T(8,128)} %param.12) | copy-start | bytes 1572868
  99.0 33.8 %collective-permute-start.3 = (f32[32,512]{1,0:T(8,128)S(1)}, f32[32,512]{1,0:T(8,128)S(1)}, u32[]{:S(2)}, u32[]{:S(2)}) collective-permute-start(f32[32,512]{1,0:T(8,128)S(1)} %get-tuple-element.21), channel_id=1, source_target_pairs={{16,32},{48,64},{80,96},{112,128},{144,160},{176,192},{208,224},{2... | collective-permute-start | bytes 196616 | tf_op jit(solution)/shard_map/ppermute | solution.py:390
  107.4 25.4 %collective-permute-start.4 = (f32[32,512]{1,0:T(8,128)S(1)}, f32[32,512]{1,0:T(8,128)S(1)}, u32[]{:S(2)}, u32[]{:S(2)}) collective-permute-start(f32[32,512]{1,0:T(8,128)S(1)} %get-tuple-element.22), channel_id=1, source_target_pairs={{0,16},{32,48},{64,80},{96,112},{128,144},{160,176},{192,208},{224... | collective-permute-start | bytes 196616 | tf_op jit(solution)/shard_map/ppermute | solution.py:393

commit v4 on v2

--- a/solution.py
+++ b/solution.py
@@ -16,19 +16,20 @@
 BF16 = jnp.bfloat16
 PACK_FLOPS = 10**11
 PARTIAL_FLOPS = 10**11
+GRAD_FLOPS = 10**11
 
 
 def iota(shape, dim):
     return lax.broadcasted_iota(jnp.int32, shape, dim)
 
 
-def call(body, out_shape, in_specs=None, scratch=(), flops=0, moved=0, name=None):
+def call(body, out_shape, in_specs=None, scratch=(), flops=0, moved=0, name=None, mib=48):
     return pl.pallas_call(
         body,
         out_shape=out_shape,
         in_specs=in_specs,
         scratch_shapes=scratch,
-        compiler_params=pltpu.CompilerParams(vmem_limit_bytes=48 * 2**20),
+        compiler_params=pltpu.CompilerParams(vmem_limit_bytes=mib * 2**20),
         cost_estimate=pl.CostEstimate(flops=flops, bytes_accessed=moved, transcendentals=0),
         name=name,
     )
@@ -36,6 +37,7 @@
 
 VMEM = pl.BlockSpec(memory_space=pltpu.VMEM)
 SMEM = pl.BlockSpec(memory_space=pltpu.SMEM)
+ANY = pl.BlockSpec(memory_space=pl.ANY)
 
 
 def vmem(count):
@@ -75,7 +77,7 @@
     send_ref[...] = jnp.dot(choose, data, precision=HIGHEST, preferred_element_type=F32)
 
 
-def unpack_body(tile_ref, back_ref, hofx_ref):
+def unpack_body(unused_ref, tile_ref, back_ref, hofx_ref):
     tile_row = tile_ref[...].astype(F32)
     tiles, slots = back_ref.shape
     count = tile_row.shape[1]
@@ -149,7 +151,19 @@
     return jnp.where(place > 0, 1.0, 0.0), jnp.where(place < tiles - 1, 1.0, 0.0)
 
 
-def prep_body(alpha_ref, members_ref, land_ref, own_ref, masked_ref, far_ref, near_ref):
+def prep_body(
+    alpha_in, members_in, land_in, own_ref, masked_ref, far_ref, near_ref, alpha_ref, members_ref, land_ref, sems
+):
+    copies = [
+        pltpu.make_async_copy(source, target, sems.at[k])
+        for k, (source, target) in enumerate(
+            ((land_in, land_ref), (members_in, members_ref), (alpha_in, alpha_ref))
+        )
+    ]
+    for copy in copies:
+        copy.start()
+    for copy in copies:
+        copy.wait()
     members, levels, rows, columns = members_ref.shape
     parts = columns // LANES
     size = rows * parts
@@ -227,8 +241,10 @@
     adjoint_far_ref,
     adjoint_near_ref,
     out_ref,
+    token_ref,
     work,
 ):
+    token_ref[...] = jnp.zeros_like(token_ref)
     parts = land_ref.shape[1] // LANES
     size, brim = rows * parts, STEPS * parts
     odd = odd_tile()
@@ -301,6 +317,11 @@
         total = jnp.sum(total, axis=0, keepdims=True)
         for k in range(out_ref.shape[0]):
             out_ref[k, s : s + 1, :] = total
+
+
+def copies_body(unused_ref, in_ref, out_ref):
+    for k in range(out_ref.shape[0]):
+        out_ref[k] = in_ref[...]
 
 
 def add_body(in_ref, out_ref):
@@ -402,8 +423,15 @@
             jax.ShapeDtypeStruct((2 * brim, LANES), F32),
             jax.ShapeDtypeStruct((2 * brim, LANES), F32),
         ),
-        vmem(3),
+        [pl.BlockSpec(memory_space=pltpu.HBM)] * 3,
+        [
+            pltpu.VMEM(alpha_tiles.shape, F32),
+            pltpu.VMEM(perturbs.shape, perturbs.dtype),
+            pltpu.VMEM(land_mask.shape, land_mask.dtype),
+            pltpu.SemaphoreType.DMA((3,)),
+        ],
         name="prep",
+        mib=60,
     )(alpha_tiles, perturbs, land_mask)
     halo_far, halo_near = exchange(far, near)
 
@@ -413,7 +441,7 @@
     sent = call(
         functools.partial(pack_body, tiles, slots, levels),
         jax.ShapeDtypeStruct((tiles, width), F32),
-        [pl.BlockSpec(memory_space=pl.ANY)] + vmem(7),
+        [ANY] + vmem(7),
         [pltpu.VMEM((COMPS, count), F32)],
         flops=PACK_FLOPS,
         name="pack",
@@ -429,10 +457,6 @@
     )
     routed = lax.all_to_all(sent, "tile", split_axis=0, concat_axis=0, tiled=True)
     count = mems * tiles
-    raw = lax.all_to_all(
-        jnp.broadcast_to(routed[None], (mems, tiles, width)), "mem", split_axis=0, concat_axis=0, tiled=True
-    ).reshape(count, width)
-
     work = pltpu.VMEM((rows + 2 * STEPS, 8, columns), F32)
     partial = call(
         functools.partial(partial_body, rows, tiles),
@@ -442,6 +466,13 @@
         flops=PARTIAL_FLOPS,
         name="partial",
     )(diff_x, diff_y, own, halo_far, halo_near, masked)
+    copied = call(
+        copies_body,
+        jax.ShapeDtypeStruct((mems, tiles, width), F32),
+        [ANY] + vmem(1),
+        name="copies",
+    )(partial, routed)
+    raw = lax.all_to_all(copied, "mem", split_axis=0, concat_axis=0, tiled=True).reshape(count, width)
     copies = jax.ShapeDtypeStruct((inner, slots, count), F32)
     comps, found = call(
         functools.partial(interpolate_body, rows, slots),
@@ -471,11 +502,12 @@
     adjoint_far, adjoint_near = exchange(edge_far, edge_near)
     returned = lax.all_to_all(back, "tile", split_axis=0, concat_axis=0, tiled=True)
 
-    grad = call(
+    grad, token = call(
         functools.partial(grad_body, rows, tiles, factor),
-        jax.ShapeDtypeStruct((size, LANES), F32),
+        (jax.ShapeDtypeStruct((size, LANES), F32), jax.ShapeDtypeStruct((8, LANES), F32)),
         [SMEM] * 2 + vmem(8),
         [work],
+        flops=GRAD_FLOPS,
         name="grad",
     )(
         diff_x,
@@ -492,9 +524,9 @@
     hofx = call(
         unpack_body,
         jax.ShapeDtypeStruct((1, obs_row.shape[0]), F32),
-        vmem(2),
+        [ANY] + vmem(2),
         name="unpack",
-    )(tile_row, returned)
+    )(token, tile_row, returned)
     return untiled(grad, alpha.shape), hofx.reshape(-1)
 
 

time: 128 us -> 125 us (0.977)
  blocking collectives: 70.8 us -> 29.7 us
  starting transfers between devices: 27.7 us -> 47.2 us
  waiting for transfers between devices: 4 us -> 22.5 us
  Pallas kernels: 19.3 us -> 21.6 us
  local copies, waits for them, and re-layouts: 4.86 us -> 3.12 us
    all_to_all x2 -> x1, blocking collectives: 55.9 us -> 14.8 us  [on_device(): lax.all_to_all(copied, 'mem', split_axis=0, concat_axis=0, tiled=True)]
    all_to_all x1 -> x2, starting transfers between devices: 5.39 us -> 24.6 us  [the longest x1 13.2 us: on_device(): lax.all_to_all(sent, 'tile', split_axis=0, concat_axis=0, tiled=True)]
    ppermute x2, waiting for transfers between devices: 0.01 us -> 9.84 us  [exchange(): lax.ppermute(far, 'tile', far_pairs)]
    all_to_all x1 -> x2, waiting for transfers between devices: 3.99 us -> 12.6 us  [the longest x1 8.73 us: on_device(): lax.all_to_all(back, 'tile', split_axis=0, concat_axis=0, tiled=True)]
    pallas_call x1, Pallas kernels: 0.94 us -> 2.55 us  [on_device(): call(prep_body, (jax.ShapeDtypeStruct((size, LANES), F32), jax.ShapeDtype...]
    unnamed x28 -> x30, local copies, waits for them, and re-layouts: 4.13 us -> 3.12 us
    pallas_call x2 -> x3, Pallas kernels: 6.17 us -> 6.18 us  [the longest x1 5.38 us: on_device(): call(functools.partial(grad_body, rows, tiles, factor), (jax.ShapeDtypeSt...]
  transfers between devices with their start and end apart: 5 -> 6, of which waited for: 1 -> 3; matrix products, arithmetic and copies ran while one was open for 1% -> 0% of each run, Pallas kernels for 5% -> 9%
where the time goes in v4:
time: 125 us
  starting transfers between devices  47.2 us (38%)
  blocking collectives  29.7 us (24%)
  waiting for transfers between devices  22.5 us (18%)
  Pallas kernels  21.6 us (17%)
  local copies, waits for them, and re-layouts  3.12 us (2%)
    all_to_all x2, blocking collectives, gather(): lax.all_to_all(x, 'mem', split_axis=0, concat_axis=0, axis_index_groups=g...  14.9 us
    all_to_all x1, blocking collectives, on_device(): lax.all_to_all(copied, 'mem', split_axis=0, concat_axis=0, tiled=True)  14.8 us
    all_to_all x1, starting transfers between devices, on_device(): lax.all_to_all(sent, 'tile', split_axis=0, concat_axis=0, tiled=True)  13.2 us
    ppermute x2, starting transfers between devices, exchange(): lax.ppermute(far, 'tile', far_pairs)  11.7 us
    all_to_all x1, starting transfers between devices, on_device(): lax.all_to_all(back, 'tile', split_axis=0, concat_axis=0, tiled=True)  11.4 us
    ppermute x2, starting transfers between devices, exchange(): lax.ppermute(near, 'tile', near_pairs)  10.9 us
    ppermute x2, waiting for transfers between devices, exchange(): lax.ppermute(far, 'tile', far_pairs)  9.84 us
    all_to_all x1, waiting for transfers between devices, on_device(): lax.all_to_all(back, 'tile', split_axis=0, concat_axis=0, tiled=True)  8.73 us
  transfers between devices with their start and end apart: 6, of which 3 were waited for; matrix products, arithmetic and copies ran while one was open for 0% of the time, Pallas kernels for 9%

profile of v4, /device:TPU:1, one launch (start us, length us, event | category | flops | bytes accessed | tf_op | source)
XLA Modules:
  0.0 124.9 jit_solution(14956261060205798720)
XLA Ops:
  0.6 2.6 %prep.1 = (f32[1024,128]{1,0:T(8,128)}, f32[1024,128]{1,0:T(8,128)}, f32[1024,128]{1,0:T(8,128)}, f32[1024,128]{1,0:T(8,128)}) custom-call(f32[1024,128]{1,0:T(8,128)} %bitcast.28, bf16[4,4,16,512]{3,2,1,0:T(8,128)(2,1)} %members_in.1, s32[16,512]{1,0:T(8,128)} %land_ref.1), custom_call_target="tpu_custom_call" | custom-call | tf_op jit(solution)/shard_map/prep/pallas_call | solution.py:418
  3.2 8.8 %collective-permute-start.1 = (f32[1024,128]{1,0:T(8,128)}, f32[1024,128]{1,0:T(8,128)S(1)}, u32[]{:S(2)}, u32[]{:S(2)}) collective-permute-start(f32[1024,128]{1,0:T(8,128)} %get-tuple-element.16), channel_id=1, source_target_pairs={{0,16},{32,48},{64,80},{96,112},{128,144},{160,176},{192,208},{224... | collective-permute-start | bytes 1572872 | tf_op jit(solution)/shard_map/ppermute | solution.py:415
  12.0 3.3 %collective-permute-start = (f32[1024,128]{1,0:T(8,128)}, f32[1024,128]{1,0:T(8,128)S(1)}, u32[]{:S(2)}, u32[]{:S(2)}) collective-permute-start(f32[1024,128]{1,0:T(8,128)} %get-tuple-element.15.unused_ref), channel_id=1, source_target_pairs={{16,32},{48,64},{80,96},{112,128},{144,160},{176,192},{208,224},{2... | collective-permute-start | bytes 1572872 | tf_op jit(solution)/shard_map/ppermute | solution.py:415
  15.3 0.0 copy-start.8
  15.3 0.0 copy-start.9
  15.4 0.6 copy-done.8
  16.0 0.0 copy-done.9
  16.0 0.0 copy-done.10
  16.0 0.0 copy-done.11
  16.1 0.0 copy-done.12
  16.1 0.0 copy-done.7
  16.1 0.0 copy-done.2
  16.1 1.0 copy-done.6
  17.2 1.2 pack.1
  18.3 13.2 %all-to-all-start = ((f32[32,1,128]{2,1,0:T(1,128)}), f32[32,1,128]{2,1,0:T(1,128)S(1)}, u32[]{:S(2)}, u32[]{:S(2)}) async-start(f32[32,1,128]{2,1,0:T(1,128)} %bitcast.12), calls=%async_computation | async-start | bytes 32768 | tf_op jit(solution)/shard_map/all_to_all | solution.py:458
  31.5 9.8 %collective-permute-done.far_ref = f32[1024,128]{1,0:T(8,128)S(1)} collective-permute-done((f32[1024,128]{1,0:T(8,128)}, f32[1024,128]{1,0:T(8,128)S(1)}, u32[]{:S(2)}, u32[]{:S(2)}) %collective-permute-start) | collective-permute-done | bytes 524320 | tf_op jit(solution)/shard_map/ppermute | solution.py:415
  41.4 0.6 copy-done.13
  42.0 0.0 copy-done.14
  42.0 5.1 %partial.1.unused_ref.field_ref = f32[128,512]{1,0:T(8,128)S(1)} custom-call(f32[4]{0:T(128)S(1)} %copy-done.13, f32[4]{0:T(128)S(1)} %copy-done.14, f32[1024,128]{1,0:T(8,128)S(1)} %copy-done.5, f32[1024,128]{1,0:T(8,128)S(1)} %collective-permute-done.far_ref, f32[1024,128]{1,0:T(8,128)S(1)} %collective-permute-done.1.near_ref, f32[1024,128]{1,0:T(8,128)S(1)} %copy-done.4), custom_call_target="tpu_custom_call" | custom-call | flops 99999997952 | tf_op jit(solution)/shard_map/partial/pallas_call | solution.py:461
  47.1 3.9 %all-to-all-done = f32[32,1,128]{2,1,0:T(1,128)S(1)} async-done(((f32[32,1,128]{2,1,0:T(1,128)}), f32[32,1,128]{2,1,0:T(1,128)S(1)}, u32[]{:S(2)}, u32[]{:S(2)}) %all-to-all-start) | async-done | bytes 16416 | tf_op jit(solution)/shard_map/all_to_all | solution.py:458
  51.0 14.8 %all_to_all.37 = f32[16,32,128]{2,1,0:T(8,128)S(1)} all-to-all(f32[16,32,128]{2,1,0:T(8,128)S(1)} %copies.1), channel_id=1, replica_groups=mesh['tile'=32,'mem'=16] {'mem'}, dimensions={0} | all-to-all | bytes 524288 | tf_op jit(solution)/shard_map/all_to_all | solution.py:475
  65.8 3.4 %interpolate.1 = (f32[128,512]{1,0:T(8,128)S(1)}, f32[4,16,512]{2,1,0:T(8,128)S(1)}) custom-call(f32[512,128]{1,0:T(8,128)S(1)} %bitcast.26, f32[128,512]{1,0:T(8,128)S(1)} %partial.1.unused_ref.field_ref), custom_call_target="tpu_custom_call" | custom-call | tf_op jit(solution)/shard_map/interpolate/pallas_call | solution.py:477
  69.2 7.2 %all_to_all.38.in_ref = f32[4,16,512]{2,1,0:T(8,128)S(1)} all-to-all(f32[4,16,512]{2,1,0:T(8,128)S(1)} %get-tuple-element.19), channel_id=1, replica_groups={{0,1,2,3},{4,5,6,7},{8,9,10,11},{12,13,14,15},{16,17,18,19},{20,21,22,2..., dimensions={0} | all-to-all | bytes 262144 | tf_op jit(solution)/shard_map/all_to_all | solution.py:486
  76.3 7.7 %all_to_all.39.sums_ref = f32[4,16,512]{2,1,0:T(8,128)S(1)} all-to-all(f32[4,16,512]{2,1,0:T(8,128)S(1)} %add.1), channel_id=1, replica_groups={{0,4,8,12},{1,5,9,13},{2,6,10,14},{3,7,11,15},{16,20,24,28},{17,21,25,2..., dimensions={0} | all-to-all | bytes 262144 | tf_op jit(solution)/shard_map/all_to_all | solution.py:486
  84.1 3.2 %spread.1 = (f32[128,512]{1,0:T(8,128)S(1)}, f32[32,512]{1,0:T(8,128)S(1)}, f32[32,512]{1,0:T(8,128)S(1)}, f32[32,16]{1,0:T(8,128)}) custom-call(f32[512,128]{1,0:T(8,128)S(1)} %bitcast.27, f32[128,512]{1,0:T(8,128)S(1)} %get-tuple-element.18.comps_ref, f32[4,16,512]{2,1,0:T(8,128)S(1)} %all_to_all.39.sums_ref), custom_call_target="tpu_custom_call" | custom-call | tf_op jit(solution)/shard_map/spread/pallas_call | solution.py:490
  87.3 8.4 %collective-permute-start.2 = (f32[32,512]{1,0:T(8,128)S(1)}, f32[32,512]{1,0:T(8,128)S(1)}, u32[]{:S(2)}, u32[]{:S(2)}) collective-permute-start(f32[32,512]{1,0:T(8,128)S(1)} %get-tuple-element.21), channel_id=1, source_target_pairs={{16,32},{48,64},{80,96},{112,128},{144,160},{176,192},{208,224},{2... | collective-permute-start | bytes 196616 | tf_op jit(solution)/shard_map/ppermute | solution.py:415
  95.7 2.1 %collective-permute-start.3 = (f32[32,512]{1,0:T(8,128)S(1)}, f32[32,512]{1,0:T(8,128)S(1)}, u32[]{:S(2)}, u32[]{:S(2)}) collective-permute-start(f32[32,512]{1,0:T(8,128)S(1)} %get-tuple-element.22), channel_id=1, source_target_pairs={{0,16},{32,48},{64,80},{96,112},{128,144},{160,176},{192,208},{224... | collective-permute-start | bytes 196616 | tf_op jit(solution)/shard_map/ppermute | solution.py:415
  97.8 11.4 %all-to-all-start.4 = ((f32[32,1,16]{2,1,0:T(1,128)}), f32[32,1,16]{2,1,0:T(1,128)S(1)}, u32[]{:S(2)}, u32[]{:S(2)}) async-start(f32[32,1,16]{2,1,0:T(1,128)} %bitcast.19), calls=%async_computation.4 | async-start | bytes 32768 | tf_op jit(solution)/shard_map/all_to_all | solution.py:503
  109.3 5.4 %grad.1 = (f32[1024,128]{1,0:T(8,128)}, f32[8,128]{1,0:T(8,128)S(1)}) custom-call(f32[4]{0:T(128)S(1)} %copy-done.13, f32[4]{0:T(128)S(1)} %copy-done.14, f32[1024,128]{1,0:T(8,128)S(1)} %bitcast.29, s32[16,512]{1,0:T(8,128)S(1)} %copy-done.1, f32[1024,128]{1,0:T(8,128)S(1)} %copy-done.4, f32[1024,128]{1,0:T(8,128)S(1)} %collective-permute-done.far_ref, ...), custom_call_target="tpu_custom_call" | custom-call | flops 99999997952 | tf_op jit(solution)/shard_map/grad/pallas_call | solution.py:505
  114.7 8.7 %all-to-all-done.4 = f32[32,1,16]{2,1,0:T(1,128)S(1)} async-done(((f32[32,1,16]{2,1,0:T(1,128)}), f32[32,1,16]{2,1,0:T(1,128)S(1)}, u32[]{:S(2)}, u32[]{:S(2)}) %all-to-all-start.4) | async-done | bytes 2080 | tf_op jit(solution)/shard_map/all_to_all | solution.py:503
  123.4 0.7 copy-done.3
  124.1 0.8 unpack.1
  (22 shorter events, 0.1 us)
Async XLA Ops:
  3.2 28.3 %collective-permute-start.1 = (f32[1024,128]{1,0:T(8,128)}, f32[1024,128]{1,0:T(8,128)S(1)}, u32[]{:S(2)}, u32[]{:S(2)}) collective-permute-start(f32[1024,128]{1,0:T(8,128)} %get-tuple-element.16), channel_id=1, source_target_pairs={{0,16},{32,48},{64,80},{96,112},{128,144},{160,176},{192,208},{224... | collective-permute-start | bytes 1572872 | tf_op jit(solution)/shard_map/ppermute | solution.py:415
  12.0 29.4 %collective-permute-start = (f32[1024,128]{1,0:T(8,128)}, f32[1024,128]{1,0:T(8,128)S(1)}, u32[]{:S(2)}, u32[]{:S(2)}) collective-permute-start(f32[1024,128]{1,0:T(8,128)} %get-tuple-element.15.unused_ref), channel_id=1, source_target_pairs={{16,32},{48,64},{80,96},{112,128},{144,160},{176,192},{208,224},{2... | collective-permute-start | bytes 1572872 | tf_op jit(solution)/shard_map/ppermute | solution.py:415
  15.3 0.7 copy-start.8
  15.3 0.7 copy-start.9
  15.4 0.7 copy-start.10
  15.4 0.7 copy-start.11
  15.4 0.7 copy-start.12
  15.4 0.7 copy-start.7
  15.4 0.7 copy-start.2
  16.1 1.0 copy-start.6
  17.2 24.2 %copy-start.4 = (f32[1024,128]{1,0:T(8,128)S(1)}, f32[1024,128]{1,0:T(8,128)}, u32[]{:S(2)}) copy-start(f32[1024,128]{1,0:T(8,128)} %get-tuple-element.14.members_ref) | copy-start | bytes 1572868
  17.2 24.2 %copy-start.5 = (f32[1024,128]{1,0:T(8,128)S(1)}, f32[1024,128]{1,0:T(8,128)}, u32[]{:S(2)}) copy-start(f32[1024,128]{1,0:T(8,128)} %get-tuple-element.17.own_ref) | copy-start | bytes 1572868
  18.3 32.7 %all-to-all-start = ((f32[32,1,128]{2,1,0:T(1,128)}), f32[32,1,128]{2,1,0:T(1,128)S(1)}, u32[]{:S(2)}, u32[]{:S(2)}) async-start(f32[32,1,128]{2,1,0:T(1,128)} %bitcast.12), calls=%async_computation | async-start | bytes 32768 | tf_op jit(solution)/shard_map/all_to_all | solution.py:458
  41.4 0.7 copy-start.13
  41.4 0.7 copy-start.14
  76.3 33.0 %copy-start = (f32[4,4,16,512]{3,2,1,0:T(8,128)S(1)}, f32[4,4,16,512]{3,2,1,0:T(8,128)}, u32[]{:S(2)}) copy-start(f32[4,4,16,512]{3,2,1,0:T(8,128)} %param.12) | copy-start | bytes 1572868
  87.3 22.0 %copy-start.1 = (s32[16,512]{1,0:T(8,128)S(1)}, s32[16,512]{1,0:T(8,128)}, u32[]{:S(2)}) copy-start(s32[16,512]{1,0:T(8,128)} %land_ref.1) | copy-start | bytes 98308
  87.3 21.9 %collective-permute-start.2 = (f32[32,512]{1,0:T(8,128)S(1)}, f32[32,512]{1,0:T(8,128)S(1)}, u32[]{:S(2)}, u32[]{:S(2)}) collective-permute-start(f32[32,512]{1,0:T(8,128)S(1)} %get-tuple-element.21), channel_id=1, source_target_pairs={{16,32},{48,64},{80,96},{112,128},{144,160},{176,192},{208,224},{2... | collective-permute-start | bytes 196616 | tf_op jit(solution)/shard_map/ppermute | solution.py:415
  95.7 13.6 %collective-permute-start.3 = (f32[32,512]{1,0:T(8,128)S(1)}, f32[32,512]{1,0:T(8,128)S(1)}, u32[]{:S(2)}, u32[]{:S(2)}) collective-permute-start(f32[32,512]{1,0:T(8,128)S(1)} %get-tuple-element.22), channel_id=1, source_target_pairs={{0,16},{32,48},{64,80},{96,112},{128,144},{160,176},{192,208},{224... | collective-permute-start | bytes 196616 | tf_op jit(solution)/shard_map/ppermute | solution.py:415
  97.8 25.6 %all-to-all-start.4 = ((f32[32,1,16]{2,1,0:T(1,128)}), f32[32,1,16]{2,1,0:T(1,128)S(1)}, u32[]{:S(2)}, u32[]{:S(2)}) async-start(f32[32,1,16]{2,1,0:T(1,128)} %bitcast.19), calls=%async_computation.4 | async-start | bytes 32768 | tf_op jit(solution)/shard_map/all_to_all | solution.py:503
  123.4 0.7 copy-start.3

commit v5 on v4

--- a/solution.py
+++ b/solution.py
@@ -55,33 +55,25 @@
     return column, row
 
 
-def pack_body(
-    tiles, slots, levels, unused_ref, tile_ref, row_ref, col_ref, lev_ref, weights_ref, value_ref, rinv_ref, send_ref, data_ref
-):
-    tile_row = tile_ref[...].astype(F32)
-    data_ref[0:1, :] = col_ref[...].astype(F32)
-    data_ref[1:2, :] = (row_ref[...] * levels + lev_ref[...]).astype(F32)
-    data_ref[2:6, :] = weights_ref[...]
-    data_ref[6:7, :] = value_ref[...]
-    data_ref[7:8, :] = rinv_ref[...]
+def pack(tiles, slots, tile_row, data):
     count = tile_row.shape[1]
     column, unused = ranks(tile_row)
     width = COMPS * slots
     expand = jnp.where(iota((COMPS, width), 1) // slots == iota((COMPS, width), 0), 1.0, 0.0)
     data = lax.dot_general(
-        data_ref[...], expand, (((0,), (0,)), ((), ())), precision=HIGHEST, preferred_element_type=F32
+        data, expand, (((0,), (0,)), ((), ())), precision=HIGHEST, preferred_element_type=F32
     )
     slot = (iota((count, width), 1) % slots).astype(F32)
     data = jnp.where(column == slot, data, 0.0)
     choose = jnp.where(iota((tiles, count), 0).astype(F32) == tile_row, 1.0, 0.0)
-    send_ref[...] = jnp.dot(choose, data, precision=HIGHEST, preferred_element_type=F32)
-
-
-def unpack_body(unused_ref, tile_ref, back_ref, hofx_ref):
-    tile_row = tile_ref[...].astype(F32)
+    return jnp.dot(choose, data, precision=HIGHEST, preferred_element_type=F32)
+
+
+def unpack_body(unused_ref, info_ref, back_ref, hofx_ref):
+    tile_row = info_ref[0:1, :]
+    row = info_ref[1:2, :]
     tiles, slots = back_ref.shape
     count = tile_row.shape[1]
-    unused, row = ranks(tile_row)
     choose = jnp.where(iota((tiles, count), 0).astype(F32) == tile_row, 1.0, 0.0)
     found = lax.dot_general(
         back_ref[...], choose, (((0,), (0,)), ((), ())), precision=HIGHEST, preferred_element_type=F32
@@ -151,25 +143,64 @@
     return jnp.where(place > 0, 1.0, 0.0), jnp.where(place < tiles - 1, 1.0, 0.0)
 
 
-def prep_body(
-    alpha_in, members_in, land_in, own_ref, masked_ref, far_ref, near_ref, alpha_ref, members_ref, land_ref, sems
-):
+def prep_body(tiles, slots, levels, *refs):
+    sources, (far_ref, near_ref, sent_ref), buffers, (data_ref, sems) = (
+        refs[:10],
+        refs[10:13],
+        refs[13:23],
+        refs[23:],
+    )
     copies = [
         pltpu.make_async_copy(source, target, sems.at[k])
-        for k, (source, target) in enumerate(
-            ((land_in, land_ref), (members_in, members_ref), (alpha_in, alpha_ref))
-        )
+        for k, (source, target) in enumerate(zip(sources, buffers))
     ]
     for copy in copies:
         copy.start()
     for copy in copies:
         copy.wait()
+    alpha_ref, members_ref, land_ref, tile_ref, row_ref, col_ref, lev_ref, weights_ref, value_ref, rinv_ref = buffers
+    members, unused, rows, columns = members_ref.shape
+    parts = columns // LANES
+    size, brim = rows * parts, STEPS * parts
+    odd = odd_tile()
+    land = land_ref[...].astype(F32)
+    is_odd = jnp.broadcast_to(odd, (STEPS, columns)) == 1
+    land_first, land_last = land[:STEPS], land[rows - STEPS :]
+    land_far, land_near = jnp.where(is_odd, land_last, land_first), jnp.where(is_odd, land_first, land_last)
+    count = members * levels
+    for f in range(count):
+        field = members_ref[f // levels, f % levels].astype(F32)
+        first, last = field[:STEPS], field[rows - STEPS :]
+        for ref, mask, top, start in (
+            (far_ref, land_far, jnp.where(is_odd, last, first), odd * (size - brim)),
+            (near_ref, land_near, jnp.where(is_odd, first, last), (1 - odd) * (size - brim)),
+        ):
+            value = mask * top
+            for j in range(parts):
+                lanes = slice(j * LANES, (j + 1) * LANES)
+                at = pl.multiple_of(f * size + start + j * 8, 8)
+                ref[f * brim + j * 8 : f * brim + j * 8 + 8, :] = mask[:, lanes] * alpha_ref[pl.ds(at, 8), :]
+                at = (count + f) * brim + j * 8
+                ref[at : at + 8, :] = value[:, lanes]
+    tile_row = tile_ref[...].astype(F32)
+    data_ref[0:1, :] = col_ref[...].astype(F32)
+    data_ref[1:2, :] = (row_ref[...] * levels + lev_ref[...]).astype(F32)
+    data_ref[2:6, :] = weights_ref[...]
+    data_ref[6:7, :] = value_ref[...]
+    data_ref[7:8, :] = rinv_ref[...]
+    sent_ref[...] = pack(tiles, slots, tile_row, data_ref[...])
+
+
+def mask_body(unused_ref, tile_ref, alpha_ref, members_ref, land_ref, own_ref, masked_ref, info_ref):
+    tile_row = tile_ref[...].astype(F32)
+    unused, rank = ranks(tile_row)
+    info_ref[0:1, :] = tile_row
+    info_ref[1:2, :] = rank
     members, levels, rows, columns = members_ref.shape
     parts = columns // LANES
     size = rows * parts
-    count = members * levels
     land = land_ref[...].astype(F32)
-    for f in range(count):
+    for f in range(members * levels):
         field = land * members_ref[f // levels, f % levels].astype(F32)
         for k in range(rows // 8):
             for j in range(parts):
@@ -177,15 +208,15 @@
                 mask = land[k * 8 : k * 8 + 8, j * LANES : (j + 1) * LANES]
                 own_ref[at : at + 8, :] = mask * alpha_ref[at : at + 8, :]
                 masked_ref[at : at + 8, :] = field[k * 8 : k * 8 + 8, j * LANES : (j + 1) * LANES]
-    brim = STEPS * parts
-    odd = odd_tile()
-    first = odd * (size - brim)
-    last = (1 - odd) * (size - brim)
-    for source, start in ((own_ref, 0), (masked_ref, count * brim)):
-        for f in range(count):
-            to = slice(start + f * brim, start + (f + 1) * brim)
-            far_ref[to, :] = source[pl.ds(pl.multiple_of(f * size + first, 8), brim), :]
-            near_ref[to, :] = source[pl.ds(pl.multiple_of(f * size + last, 8), brim), :]
+
+
+def pass_body(in_ref, out_ref):
+    def run(sem):
+        copy = pltpu.make_async_copy(in_ref, out_ref, sem)
+        copy.start()
+        copy.wait()
+
+    pl.run_scoped(run, pltpu.SemaphoreType.DMA(()))
 
 
 def partial_body(rows, tiles, rate_x_ref, rate_y_ref, own_ref, far_ref, near_ref, members_ref, out_ref, work):
@@ -411,43 +442,20 @@
     size = members * levels * rows * columns // LANES
     brim = members * levels * STEPS * columns // LANES
 
-    def exchange(far, near):
-        return lax.ppermute(far, "tile", far_pairs), lax.ppermute(near, "tile", near_pairs)
+    def to_far(x):
+        return lax.ppermute(x, "tile", far_pairs)
+
+    def to_near(x):
+        return lax.ppermute(x, "tile", near_pairs)
 
     alpha_tiles = tiled(alpha)
-    own, masked, far, near = call(
-        prep_body,
-        (
-            jax.ShapeDtypeStruct((size, LANES), F32),
-            jax.ShapeDtypeStruct((size, LANES), F32),
-            jax.ShapeDtypeStruct((2 * brim, LANES), F32),
-            jax.ShapeDtypeStruct((2 * brim, LANES), F32),
-        ),
-        [pl.BlockSpec(memory_space=pltpu.HBM)] * 3,
-        [
-            pltpu.VMEM(alpha_tiles.shape, F32),
-            pltpu.VMEM(perturbs.shape, perturbs.dtype),
-            pltpu.VMEM(land_mask.shape, land_mask.dtype),
-            pltpu.SemaphoreType.DMA((3,)),
-        ],
-        name="prep",
-        mib=60,
-    )(alpha_tiles, perturbs, land_mask)
-    halo_far, halo_near = exchange(far, near)
-
     count = obs_row.shape[0]
-    tile_row = obs_tile.reshape(1, count)
     width = COMPS * slots
-    sent = call(
-        functools.partial(pack_body, tiles, slots, levels),
-        jax.ShapeDtypeStruct((tiles, width), F32),
-        [ANY] + vmem(7),
-        [pltpu.VMEM((COMPS, count), F32)],
-        flops=PACK_FLOPS,
-        name="pack",
-    )(
-        far,
-        tile_row,
+    sources = (
+        alpha_tiles,
+        perturbs,
+        land_mask,
+        obs_tile.reshape(1, count),
         obs_row.reshape(1, count),
         obs_col.reshape(1, count),
         obs_lev.reshape(1, count),
@@ -455,7 +463,34 @@
         obs_value.reshape(1, count),
         obs_rinv.reshape(1, count),
     )
+    far, near, sent = call(
+        functools.partial(prep_body, tiles, slots, levels),
+        (
+            jax.ShapeDtypeStruct((2 * brim, LANES), F32),
+            jax.ShapeDtypeStruct((2 * brim, LANES), F32),
+            jax.ShapeDtypeStruct((tiles, width), F32),
+        ),
+        [ANY] * len(sources),
+        [pltpu.VMEM(x.shape, x.dtype) for x in sources]
+        + [pltpu.VMEM((COMPS, count), F32), pltpu.SemaphoreType.DMA((len(sources),))],
+        name="prep",
+        mib=60,
+    )(*sources)
+    halo_far, halo_near = to_far(far), to_near(near)
+    sent = call(
+        pass_body, jax.ShapeDtypeStruct(sent.shape, F32), [ANY], flops=PACK_FLOPS, name="pass", mib=60
+    )(sent)
     routed = lax.all_to_all(sent, "tile", split_axis=0, concat_axis=0, tiled=True)
+    own, masked, info = call(
+        mask_body,
+        (
+            jax.ShapeDtypeStruct((size, LANES), F32),
+            jax.ShapeDtypeStruct((size, LANES), F32),
+            jax.ShapeDtypeStruct((2, count), F32),
+        ),
+        [ANY] + vmem(4),
+        name="mask",
+    )(sent, sources[3], alpha_tiles, perturbs, land_mask)
     count = mems * tiles
     work = pltpu.VMEM((rows + 2 * STEPS, 8, columns), F32)
     partial = call(
@@ -499,7 +534,8 @@
         [pltpu.VMEM((16 * rows, count), BF16), pltpu.VMEM((16 * rows, columns), F32)],
         name="spread",
     )(raw, comps, sums)
-    adjoint_far, adjoint_near = exchange(edge_far, edge_near)
+    adjoint_far = to_far(edge_far)
+    adjoint_near = to_near(edge_near)
     returned = lax.all_to_all(back, "tile", split_axis=0, concat_axis=0, tiled=True)
 
     grad, token = call(
@@ -526,7 +562,7 @@
         jax.ShapeDtypeStruct((1, obs_row.shape[0]), F32),
         [ANY] + vmem(2),
         name="unpack",
-    )(token, tile_row, returned)
+    )(token, info, returned)
     return untiled(grad, alpha.shape), hofx.reshape(-1)
 
 

time: 125 us -> 122 us (0.976)
  waiting for transfers between devices: 22.5 us -> 20.7 us
  local copies, waits for them, and re-layouts: 3.12 us -> 1.43 us
    ppermute x4, waiting for transfers between devices: 9.84 us -> 6.45 us  [the longest x2 6.44 us: to_far(): return lax.ppermute(x, 'tile', far_pairs)]
    unnamed x30 -> x14, local copies, waits for them, and re-layouts: 3.12 us -> 1.43 us
    all_to_all x1, waiting for transfers between devices: 3.89 us -> 5.54 us  [on_device(): lax.all_to_all(sent, 'tile', split_axis=0, concat_axis=0, tiled=True)]
    pallas_call x2 -> x3, Pallas kernels: 3.73 us -> 4.28 us  [the longest x1 2.76 us: on_device(): call(functools.partial(prep_body, tiles, slots, levels), (jax.ShapeDtypeS...]
  transfers between devices with their start and end apart: 6 -> 6, of which waited for: 3 -> 3; matrix products, arithmetic and copies ran while one was open for 0% -> 0% of each run, Pallas kernels for 9% -> 10%
where the time goes in v5:
time: 122 us
  starting transfers between devices  47.2 us (39%)
  blocking collectives  29.3 us (24%)
  Pallas kernels  22.1 us (18%)
  waiting for transfers between devices  20.7 us (17%)
  local copies, waits for them, and re-layouts  1.43 us (1%)
    ppermute x2, starting transfers between devices, to_far(): return lax.ppermute(x, 'tile', far_pairs)  18.8 us
    all_to_all x2, blocking collectives, gather(): lax.all_to_all(x, 'mem', split_axis=0, concat_axis=0, axis_index_groups=g...  14.7 us
    all_to_all x1, blocking collectives, on_device(): lax.all_to_all(copied, 'mem', split_axis=0, concat_axis=0, tiled=True)  14.6 us
    all_to_all x1, starting transfers between devices, on_device(): lax.all_to_all(sent, 'tile', split_axis=0, concat_axis=0, tiled=True)  13.7 us
    all_to_all x1, starting transfers between devices, on_device(): lax.all_to_all(back, 'tile', split_axis=0, concat_axis=0, tiled=True)  10.7 us
    all_to_all x1, waiting for transfers between devices, on_device(): lax.all_to_all(back, 'tile', split_axis=0, concat_axis=0, tiled=True)  8.72 us
    ppermute x2, waiting for transfers between devices, to_far(): return lax.ppermute(x, 'tile', far_pairs)  6.44 us
    all_to_all x1, waiting for transfers between devices, on_device(): lax.all_to_all(sent, 'tile', split_axis=0, concat_axis=0, tiled=True)  5.54 us
  transfers between devices with their start and end apart: 6, of which 3 were waited for; matrix products, arithmetic and copies ran while one was open for 0% of the time, Pallas kernels for 10%

profile of v5, /device:TPU:1, one launch (start us, length us, event | category | flops | bytes accessed | tf_op | source)
XLA Modules:
  0.0 121.6 jit_solution(12017502159005351419)
XLA Ops:
  0.6 2.8 %prep.1 = (f32[1024,128]{1,0:T(8,128)}, f32[1024,128]{1,0:T(8,128)}, f32[32,128]{1,0:T(8,128)}) custom-call(f32[1024,128]{1,0:T(8,128)} %bitcast.28, bf16[4,4,16,512]{3,2,1,0:T(8,128)(2,1)} %members_ref.1, s32[16,512]{1,0:T(8,128)} %land_ref.3, s32[1,256]{1,0:T(1,128)} %bitcast.34, s32[1,256]{1,0:T(1,128)} %bitcast.36, s32[1,256]{1,0:T(1,128)} %bitcast.37, ...), custom_call_target="tpu_custom_call" | custom-call | tf_op jit(solution)/shard_map/prep/pallas_call | solution.py:466
  3.4 10.2 %collective-permute-start = (f32[1024,128]{1,0:T(8,128)}, f32[1024,128]{1,0:T(8,128)S(1)}, u32[]{:S(2)}, u32[]{:S(2)}) collective-permute-start(f32[1024,128]{1,0:T(8,128)} %get-tuple-element.18), channel_id=1, source_target_pairs={{16,32},{48,64},{80,96},{112,128},{144,160},{176,192},{208,224},{2... | collective-permute-start | bytes 1572872 | tf_op jit(solution)/shard_map/ppermute | solution.py:446
  13.6 1.9 %collective-permute-start.1 = (f32[1024,128]{1,0:T(8,128)}, f32[1024,128]{1,0:T(8,128)S(1)}, u32[]{:S(2)}, u32[]{:S(2)}) collective-permute-start(f32[1024,128]{1,0:T(8,128)} %get-tuple-element.19), channel_id=1, source_target_pairs={{0,16},{32,48},{64,80},{96,112},{128,144},{160,176},{192,208},{224... | collective-permute-start | bytes 1572872 | tf_op jit(solution)/shard_map/ppermute | solution.py:449
  15.5 0.0 copy-start
  15.6 0.0 copy-start.1
  15.6 1.4 %pass.1.unused_ref = f32[32,128]{1,0:T(8,128)} custom-call(f32[32,128]{1,0:T(8,128)} %get-tuple-element.16.in_ref), custom_call_target="tpu_custom_call" | custom-call | flops 99999997952 | tf_op jit(solution)/shard_map/pass/pallas_call | solution.py:480
  16.9 13.7 %all-to-all-start = ((f32[32,1,128]{2,1,0:T(1,128)}), f32[32,1,128]{2,1,0:T(1,128)S(1)}, u32[]{:S(2)}, u32[]{:S(2)}) async-start(f32[32,1,128]{2,1,0:T(1,128)} %bitcast.32), calls=%async_computation | async-start | bytes 32768 | tf_op jit(solution)/shard_map/all_to_all | solution.py:483
  30.7 0.0 copy-done
  30.7 0.0 copy-done.1
  30.7 0.0 copy-done.2
  30.7 0.0 copy-done.4
  30.7 0.7 copy-done.3
  31.4 0.1 mask.1
  31.6 6.4 %collective-permute-done.far_ref = f32[1024,128]{1,0:T(8,128)S(1)} collective-permute-done((f32[1024,128]{1,0:T(8,128)}, f32[1024,128]{1,0:T(8,128)S(1)}, u32[]{:S(2)}, u32[]{:S(2)}) %collective-permute-start) | collective-permute-done | bytes 524320 | tf_op jit(solution)/shard_map/ppermute | solution.py:446
  38.0 0.0 collective-permute-done.1.near_ref
  38.0 0.7 copy-done.5
  38.7 0.0 copy-done.6
  38.7 5.0 %partial.1.unused_ref.field_ref = f32[128,512]{1,0:T(8,128)S(1)} custom-call(f32[4]{0:T(128)S(1)} %copy-done.5, f32[4]{0:T(128)S(1)} %copy-done.6, f32[1024,128]{1,0:T(8,128)S(1)} %get-tuple-element.20.own_ref, f32[1024,128]{1,0:T(8,128)S(1)} %collective-permute-done.far_ref, f32[1024,128]{1,0:T(8,128)S(1)} %collective-permute-done.1.near_ref, ...), custom_call_target="tpu_custom_call" | custom-call | flops 99999997952 | tf_op jit(solution)/shard_map/partial/pallas_call | solution.py:496
  43.7 5.5 %all-to-all-done = f32[32,1,128]{2,1,0:T(1,128)S(1)} async-done(((f32[32,1,128]{2,1,0:T(1,128)}), f32[32,1,128]{2,1,0:T(1,128)S(1)}, u32[]{:S(2)}, u32[]{:S(2)}) %all-to-all-start) | async-done | bytes 16416 | tf_op jit(solution)/shard_map/all_to_all | solution.py:483
  49.3 14.6 %all_to_all.37 = f32[16,32,128]{2,1,0:T(8,128)S(1)} all-to-all(f32[16,32,128]{2,1,0:T(8,128)S(1)} %copies.1), channel_id=1, replica_groups=mesh['tile'=32,'mem'=16] {'mem'}, dimensions={0} | all-to-all | bytes 524288 | tf_op jit(solution)/shard_map/all_to_all | solution.py:510
  63.9 3.4 %interpolate.1 = (f32[128,512]{1,0:T(8,128)S(1)}, f32[4,16,512]{2,1,0:T(8,128)S(1)}) custom-call(f32[512,128]{1,0:T(8,128)S(1)} %bitcast.26, f32[128,512]{1,0:T(8,128)S(1)} %partial.1.unused_ref.field_ref), custom_call_target="tpu_custom_call" | custom-call | tf_op jit(solution)/shard_map/interpolate/pallas_call | solution.py:512
  67.3 7.2 %all_to_all.38.in_ref = f32[4,16,512]{2,1,0:T(8,128)S(1)} all-to-all(f32[4,16,512]{2,1,0:T(8,128)S(1)} %get-tuple-element.22), channel_id=1, replica_groups={{0,1,2,3},{4,5,6,7},{8,9,10,11},{12,13,14,15},{16,17,18,19},{20,21,22,2..., dimensions={0} | all-to-all | bytes 262144 | tf_op jit(solution)/shard_map/all_to_all | solution.py:521
  74.5 7.6 %all_to_all.39.sums_ref = f32[4,16,512]{2,1,0:T(8,128)S(1)} all-to-all(f32[4,16,512]{2,1,0:T(8,128)S(1)} %add.1), channel_id=1, replica_groups={{0,4,8,12},{1,5,9,13},{2,6,10,14},{3,7,11,15},{16,20,24,28},{17,21,25,2..., dimensions={0} | all-to-all | bytes 262144 | tf_op jit(solution)/shard_map/all_to_all | solution.py:521
  82.0 3.2 %spread.1 = (f32[128,512]{1,0:T(8,128)S(1)}, f32[32,512]{1,0:T(8,128)S(1)}, f32[32,512]{1,0:T(8,128)S(1)}, f32[32,16]{1,0:T(8,128)}) custom-call(f32[512,128]{1,0:T(8,128)S(1)} %bitcast.27, f32[128,512]{1,0:T(8,128)S(1)} %get-tuple-element.21.comps_ref, f32[4,16,512]{2,1,0:T(8,128)S(1)} %all_to_all.39.sums_ref), custom_call_target="tpu_custom_call" | custom-call | tf_op jit(solution)/shard_map/spread/pallas_call | solution.py:525
  85.3 8.5 %collective-permute-start.2 = (f32[32,512]{1,0:T(8,128)S(1)}, f32[32,512]{1,0:T(8,128)S(1)}, u32[]{:S(2)}, u32[]{:S(2)}) collective-permute-start(f32[32,512]{1,0:T(8,128)S(1)} %get-tuple-element.24), channel_id=1, source_target_pairs={{16,32},{48,64},{80,96},{112,128},{144,160},{176,192},{208,224},{2... | collective-permute-start | bytes 196616 | tf_op jit(solution)/shard_map/ppermute | solution.py:446
  93.8 2.1 %collective-permute-start.3 = (f32[32,512]{1,0:T(8,128)S(1)}, f32[32,512]{1,0:T(8,128)S(1)}, u32[]{:S(2)}, u32[]{:S(2)}) collective-permute-start(f32[32,512]{1,0:T(8,128)S(1)} %get-tuple-element.25), channel_id=1, source_target_pairs={{0,16},{32,48},{64,80},{96,112},{128,144},{160,176},{192,208},{224... | collective-permute-start | bytes 196616 | tf_op jit(solution)/shard_map/ppermute | solution.py:449
  95.9 10.7 %all-to-all-start.4 = ((f32[32,1,16]{2,1,0:T(1,128)}), f32[32,1,16]{2,1,0:T(1,128)S(1)}, u32[]{:S(2)}, u32[]{:S(2)}) async-start(f32[32,1,16]{2,1,0:T(1,128)} %bitcast.19), calls=%async_computation.4 | async-start | bytes 32768 | tf_op jit(solution)/shard_map/all_to_all | solution.py:539
  106.6 0.0 collective-permute-done.2.adjoint_far_ref
  106.7 0.0 collective-permute-done.3.adjoint_near_ref
  106.7 5.4 %grad.1 = (f32[1024,128]{1,0:T(8,128)}, f32[8,128]{1,0:T(8,128)S(1)}) custom-call(f32[4]{0:T(128)S(1)} %copy-done.5, f32[4]{0:T(128)S(1)} %copy-done.6, f32[1024,128]{1,0:T(8,128)S(1)} %bitcast.30, s32[16,512]{1,0:T(8,128)S(1)} %copy-done.2, f32[1024,128]{1,0:T(8,128)S(1)} %get-tuple-element.17.members_ref, f32[1024,128]{1,0:T(8,128)S(1)} %collective-permute-done.far_ref, ...), custom_call_target="tpu_custom_call" | custom-call | flops 99999997952 | tf_op jit(solution)/shard_map/grad/pallas_call | solution.py:541
  112.1 8.7 %all-to-all-done.4 = f32[32,1,16]{2,1,0:T(1,128)S(1)} async-done(((f32[32,1,16]{2,1,0:T(1,128)}), f32[32,1,16]{2,1,0:T(1,128)S(1)}, u32[]{:S(2)}, u32[]{:S(2)}) %all-to-all-start.4) | async-done | bytes 2080 | tf_op jit(solution)/shard_map/all_to_all | solution.py:539
  120.8 0.8 unpack.1
  (7 shorter events, 0.0 us)
Async XLA Ops:
  3.4 34.6 %collective-permute-start = (f32[1024,128]{1,0:T(8,128)}, f32[1024,128]{1,0:T(8,128)S(1)}, u32[]{:S(2)}, u32[]{:S(2)}) collective-permute-start(f32[1024,128]{1,0:T(8,128)} %get-tuple-element.18), channel_id=1, source_target_pairs={{16,32},{48,64},{80,96},{112,128},{144,160},{176,192},{208,224},{2... | collective-permute-start | bytes 1572872 | tf_op jit(solution)/shard_map/ppermute | solution.py:446
  13.6 24.4 %collective-permute-start.1 = (f32[1024,128]{1,0:T(8,128)}, f32[1024,128]{1,0:T(8,128)S(1)}, u32[]{:S(2)}, u32[]{:S(2)}) collective-permute-start(f32[1024,128]{1,0:T(8,128)} %get-tuple-element.19), channel_id=1, source_target_pairs={{0,16},{32,48},{64,80},{96,112},{128,144},{160,176},{192,208},{224... | collective-permute-start | bytes 1572872 | tf_op jit(solution)/shard_map/ppermute | solution.py:449
  15.5 15.1 %copy-start = (f32[4,4,16,512]{3,2,1,0:T(8,128)S(1)}, f32[4,4,16,512]{3,2,1,0:T(8,128)}, u32[]{:S(2)}) copy-start(f32[4,4,16,512]{3,2,1,0:T(8,128)} %param.12) | copy-start | bytes 1572868
  15.6 15.1 %copy-start.1 = (bf16[4,4,16,512]{3,2,1,0:T(8,128)(2,1)S(1)}, bf16[4,4,16,512]{3,2,1,0:T(8,128)(2,1)}, u32[]{:S(2)}) copy-start(bf16[4,4,16,512]{3,2,1,0:T(8,128)(2,1)} %members_ref.1) | copy-start | bytes 786436
  16.9 13.7 %copy-start.2 = (s32[16,512]{1,0:T(8,128)S(1)}, s32[16,512]{1,0:T(8,128)}, u32[]{:S(2)}) copy-start(s32[16,512]{1,0:T(8,128)} %land_ref.3) | copy-start | bytes 98308
  16.9 13.7 %copy-start.4 = (s32[256,1]{0,1:T(1,128)S(1)}, s32[256,1]{0,1:T(1,128)}, u32[]{:S(2)}) copy-start(s32[256,1]{0,1:T(1,128)} %param.17) | copy-start | bytes 3076
  16.9 32.3 %all-to-all-start = ((f32[32,1,128]{2,1,0:T(1,128)}), f32[32,1,128]{2,1,0:T(1,128)S(1)}, u32[]{:S(2)}, u32[]{:S(2)}) async-start(f32[32,1,128]{2,1,0:T(1,128)} %bitcast.32), calls=%async_computation | async-start | bytes 32768 | tf_op jit(solution)/shard_map/all_to_all | solution.py:483
  30.7 0.7 copy-start.3
  38.0 0.7 copy-start.5
  38.0 0.7 copy-start.6
  85.3 21.4 %collective-permute-start.2 = (f32[32,512]{1,0:T(8,128)S(1)}, f32[32,512]{1,0:T(8,128)S(1)}, u32[]{:S(2)}, u32[]{:S(2)}) collective-permute-start(f32[32,512]{1,0:T(8,128)S(1)} %get-tuple-element.24), channel_id=1, source_target_pairs={{16,32},{48,64},{80,96},{112,128},{144,160},{176,192},{208,224},{2... | collective-permute-start | bytes 196616 | tf_op jit(solution)/shard_map/ppermute | solution.py:446
  93.8 12.8 %collective-permute-start.3 = (f32[32,512]{1,0:T(8,128)S(1)}, f32[32,512]{1,0:T(8,128)S(1)}, u32[]{:S(2)}, u32[]{:S(2)}) collective-permute-start(f32[32,512]{1,0:T(8,128)S(1)} %get-tuple-element.25), channel_id=1, source_target_pairs={{0,16},{32,48},{64,80},{96,112},{128,144},{160,176},{192,208},{224... | collective-permute-start | bytes 196616 | tf_op jit(solution)/shard_map/ppermute | solution.py:449
  95.9 24.9 %all-to-all-start.4 = ((f32[32,1,16]{2,1,0:T(1,128)}), f32[32,1,16]{2,1,0:T(1,128)S(1)}, u32[]{:S(2)}, u32[]{:S(2)}) async-start(f32[32,1,16]{2,1,0:T(1,128)} %bitcast.19), calls=%async_computation.4 | async-start | bytes 32768 | tf_op jit(solution)/shard_map/all_to_all | solution.py:539

commit v6 on v5

--- a/solution.py
+++ b/solution.py
@@ -14,7 +14,6 @@
 HIGHEST = lax.Precision.HIGHEST
 F32 = jnp.float32
 BF16 = jnp.bfloat16
-PACK_FLOPS = 10**11
 PARTIAL_FLOPS = 10**11
 GRAD_FLOPS = 10**11
 
@@ -144,11 +143,11 @@
 
 
 def prep_body(tiles, slots, levels, *refs):
-    sources, (far_ref, near_ref, sent_ref), buffers, (data_ref, sems) = (
+    sources, (far_ref, far_members_ref, near_ref, sent_ref), buffers, (data_ref, sems) = (
         refs[:10],
-        refs[10:13],
-        refs[13:23],
-        refs[23:],
+        refs[10:14],
+        refs[14:24],
+        refs[24:],
     )
     copies = [
         pltpu.make_async_copy(source, target, sems.at[k])
@@ -171,17 +170,17 @@
     for f in range(count):
         field = members_ref[f // levels, f % levels].astype(F32)
         first, last = field[:STEPS], field[rows - STEPS :]
-        for ref, mask, top, start in (
-            (far_ref, land_far, jnp.where(is_odd, last, first), odd * (size - brim)),
-            (near_ref, land_near, jnp.where(is_odd, first, last), (1 - odd) * (size - brim)),
+        for ref, other, mask, top, start in (
+            (far_ref, far_members_ref, land_far, jnp.where(is_odd, last, first), odd * (size - brim)),
+            (near_ref, near_ref, land_near, jnp.where(is_odd, first, last), (1 - odd) * (size - brim)),
         ):
             value = mask * top
             for j in range(parts):
                 lanes = slice(j * LANES, (j + 1) * LANES)
                 at = pl.multiple_of(f * size + start + j * 8, 8)
                 ref[f * brim + j * 8 : f * brim + j * 8 + 8, :] = mask[:, lanes] * alpha_ref[pl.ds(at, 8), :]
-                at = (count + f) * brim + j * 8
-                ref[at : at + 8, :] = value[:, lanes]
+                at = (f if other is far_members_ref else count + f) * brim + j * 8
+                other[at : at + 8, :] = value[:, lanes]
     tile_row = tile_ref[...].astype(F32)
     data_ref[0:1, :] = col_ref[...].astype(F32)
     data_ref[1:2, :] = (row_ref[...] * levels + lev_ref[...]).astype(F32)
@@ -208,15 +207,6 @@
                 mask = land[k * 8 : k * 8 + 8, j * LANES : (j + 1) * LANES]
                 own_ref[at : at + 8, :] = mask * alpha_ref[at : at + 8, :]
                 masked_ref[at : at + 8, :] = field[k * 8 : k * 8 + 8, j * LANES : (j + 1) * LANES]
-
-
-def pass_body(in_ref, out_ref):
-    def run(sem):
-        copy = pltpu.make_async_copy(in_ref, out_ref, sem)
-        copy.start()
-        copy.wait()
-
-    pl.run_scoped(run, pltpu.SemaphoreType.DMA(()))
 
 
 def partial_body(rows, tiles, rate_x_ref, rate_y_ref, own_ref, far_ref, near_ref, members_ref, out_ref, work):
@@ -290,8 +280,9 @@
         for j in range(parts):
             lanes = slice(j * LANES, (j + 1) * LANES)
             for r in range(STEPS):
+                at = at_fields(0, brim, group, r, j, parts)
+                work[far_at + r, :, lanes] = far_ref[at, :] * twice(adjoint_far_ref, r, lanes)
                 at = at_fields(16 * brim, brim, group, r, j, parts)
-                work[far_at + r, :, lanes] = far_ref[at, :] * twice(adjoint_far_ref, r, lanes)
                 work[near_at + r, :, lanes] = near_ref[at, :] * twice(adjoint_near_ref, r, lanes)
             for r in range(rows):
                 own = members_ref[at_fields(0, size, group, r, j, parts), :]
@@ -463,10 +454,11 @@
         obs_value.reshape(1, count),
         obs_rinv.reshape(1, count),
     )
-    far, near, sent = call(
+    far, far_members, near, sent = call(
         functools.partial(prep_body, tiles, slots, levels),
         (
-            jax.ShapeDtypeStruct((2 * brim, LANES), F32),
+            jax.ShapeDtypeStruct((brim, LANES), F32),
+            jax.ShapeDtypeStruct((brim, LANES), F32),
             jax.ShapeDtypeStruct((2 * brim, LANES), F32),
             jax.ShapeDtypeStruct((tiles, width), F32),
         ),
@@ -476,10 +468,7 @@
         name="prep",
         mib=60,
     )(*sources)
-    halo_far, halo_near = to_far(far), to_near(near)
-    sent = call(
-        pass_body, jax.ShapeDtypeStruct(sent.shape, F32), [ANY], flops=PACK_FLOPS, name="pass", mib=60
-    )(sent)
+    halo_far, halo_near, members_far = to_far(far), to_near(near), to_far(far_members)
     routed = lax.all_to_all(sent, "tile", split_axis=0, concat_axis=0, tiled=True)
     own, masked, info = call(
         mask_body,
@@ -551,7 +540,7 @@
         alpha_tiles,
         land_mask,
         masked,
-        halo_far,
+        members_far,
         halo_near,
         adjoint,
         adjoint_far,

time: 122 us -> 116 us (0.951)
  blocking collectives: 29.3 us -> 22.2 us
  starting transfers between devices: 47.2 us -> 52.8 us
  waiting for transfers between devices: 20.7 us -> 16.3 us
    all_to_all x2 -> x1, blocking collectives: 14.7 us -> 7.21 us  [gather(): lax.all_to_all(x, 'mem', split_axis=0, concat_axis=0, axis_index_groups=g...]
    ppermute x2, starting transfers between devices: 4.02 us -> 10.7 us  [to_near(): return lax.ppermute(x, 'tile', near_pairs)]
    ppermute x2 -> x3, waiting for transfers between devices: 6.44 us -> 0.01 us  [to_far(): return lax.ppermute(x, 'tile', far_pairs)]
    all_to_all x0 -> x1, starting transfers between devices: none -> 3.46 us  [gather(): lax.all_to_all(x, 'mem', split_axis=0, concat_axis=0, axis_index_groups=g...]
    ppermute x2 -> x3, starting transfers between devices: 18.8 us -> 16 us  [to_far(): return lax.ppermute(x, 'tile', far_pairs)]
    all_to_all x1, waiting for transfers between devices: 5.54 us -> 7.54 us  [on_device(): lax.all_to_all(sent, 'tile', split_axis=0, concat_axis=0, tiled=True)]
    pallas_call x1 -> x0, Pallas kernels: 1.38 us -> none  [on_device(): call(pass_body, jax.ShapeDtypeStruct(sent.shape, F32), [ANY], flops=PACK_...]
    all_to_all x1, starting transfers between devices: 10.7 us -> 9.44 us  [on_device(): lax.all_to_all(back, 'tile', split_axis=0, concat_axis=0, tiled=True)]
  transfers between devices with their start and end apart: 6 -> 8, of which waited for: 3 -> 2; matrix products, arithmetic and copies ran while one was open for 0% -> 0% of each run, Pallas kernels for 10% -> 12%
where the time goes in v6:
time: 116 us; the launch traced here: 115 us
  starting transfers between devices  52.8 us (46%)
  blocking collectives  22.2 us (19%)
  Pallas kernels  21.4 us (18%)
  waiting for transfers between devices  16.3 us (14%)
  local copies, waits for them, and re-layouts  1.42 us (1%)
    ppermute x3, starting transfers between devices, to_far(): return lax.ppermute(x, 'tile', far_pairs)  16 us
    all_to_all x1, blocking collectives, on_device(): lax.all_to_all(copied, 'mem', split_axis=0, concat_axis=0, tiled=True)  15 us
    all_to_all x1, starting transfers between devices, on_device(): lax.all_to_all(sent, 'tile', split_axis=0, concat_axis=0, tiled=True)  13.2 us
    ppermute x2, starting transfers between devices, to_near(): return lax.ppermute(x, 'tile', near_pairs)  10.7 us
    all_to_all x1, starting transfers between devices, on_device(): lax.all_to_all(back, 'tile', split_axis=0, concat_axis=0, tiled=True)  9.44 us
    all_to_all x1, waiting for transfers between devices, on_device(): lax.all_to_all(back, 'tile', split_axis=0, concat_axis=0, tiled=True)  8.75 us
    all_to_all x1, waiting for transfers between devices, on_device(): lax.all_to_all(sent, 'tile', split_axis=0, concat_axis=0, tiled=True)  7.54 us
    all_to_all x1, blocking collectives, gather(): lax.all_to_all(x, 'mem', split_axis=0, concat_axis=0, axis_index_groups=g...  7.21 us
  transfers between devices with their start and end apart: 8, of which 2 were waited for; matrix products, arithmetic and copies ran while one was open for 0% of the time, Pallas kernels for 12%

profile of v6, /device:TPU:1, one launch (start us, length us, event | category | flops | bytes accessed | tf_op | source)
XLA Modules:
  0.0 115.0 jit_solution(9528844876723452052)
XLA Ops:
  0.7 2.8 %prep.1 = (f32[512,128]{1,0:T(8,128)}, f32[512,128]{1,0:T(8,128)}, f32[1024,128]{1,0:T(8,128)}, f32[32,128]{1,0:T(8,128)}) custom-call(f32[1024,128]{1,0:T(8,128)} %bitcast.28, bf16[4,4,16,512]{3,2,1,0:T(8,128)(2,1)} %members_ref.1, s32[16,512]{1,0:T(8,128)} %land_ref.3, s32[1,256]{1,0:T(1,128)} %bitcast.34, s32[1,256]{1,0:T(1,128)} %bitcast.36, ...), custom_call_target="tpu_custom_call" | custom-call | tf_op jit(solution)/shard_map/prep/pallas_call | solution.py:457
  3.5 0.0 copy-start.2
  3.5 8.8 %collective-permute-start.1 = (f32[1024,128]{1,0:T(8,128)}, f32[1024,128]{1,0:T(8,128)S(1)}, u32[]{:S(2)}, u32[]{:S(2)}) collective-permute-start(f32[1024,128]{1,0:T(8,128)} %get-tuple-element.20), channel_id=1, source_target_pairs={{0,16},{32,48},{64,80},{96,112},{128,144},{160,176},{192,208},{224... | collective-permute-start | bytes 1572872 | tf_op jit(solution)/shard_map/ppermute | solution.py:440
  12.3 3.3 %collective-permute-start.2 = (f32[512,128]{1,0:T(8,128)}, f32[512,128]{1,0:T(8,128)S(1)}, u32[]{:S(2)}, u32[]{:S(2)}) collective-permute-start(f32[512,128]{1,0:T(8,128)} %get-tuple-element.22), channel_id=1, source_target_pairs={{16,32},{48,64},{80,96},{112,128},{144,160},{176,192},{208,224},{2... | collective-permute-start | bytes 786440 | tf_op jit(solution)/shard_map/ppermute | solution.py:437
  15.6 0.0 copy-start.4
  15.6 13.2 %all-to-all-start = ((f32[32,1,128]{2,1,0:T(1,128)}), f32[32,1,128]{2,1,0:T(1,128)S(1)}, u32[]{:S(2)}, u32[]{:S(2)}) async-start(f32[32,1,128]{2,1,0:T(1,128)} %bitcast.31), calls=%async_computation | async-start | bytes 32768 | tf_op jit(solution)/shard_map/all_to_all | solution.py:472
  28.9 0.7 copy-done.3
  29.6 0.1 mask.1
  29.8 0.0 collective-permute-done.2.far_ref
  29.8 0.0 collective-permute-done.1.near_ref
  29.8 0.0 copy-start.5
  29.8 0.0 copy-start.6
  29.8 0.6 copy-done.5
  30.5 0.0 copy-done.6
  30.5 5.0 %partial.1.unused_ref.field_ref = f32[128,512]{1,0:T(8,128)S(1)} custom-call(f32[4]{0:T(128)S(1)} %copy-done.5, f32[4]{0:T(128)S(1)} %copy-done.6, f32[1024,128]{1,0:T(8,128)S(1)} %get-tuple-element.21.own_ref, f32[512,128]{1,0:T(8,128)S(1)} %collective-permute-done.2.far_ref, f32[1024,128]{1,0:T(8,128)S(1)} %collective-permute-done.1.near_ref, ...), custom_call_target="tpu_custom_call" | custom-call | flops 99999997952 | tf_op jit(solution)/shard_map/partial/pallas_call | solution.py:485
  35.5 7.5 %all-to-all-done = f32[32,1,128]{2,1,0:T(1,128)S(1)} async-done(((f32[32,1,128]{2,1,0:T(1,128)}), f32[32,1,128]{2,1,0:T(1,128)S(1)}, u32[]{:S(2)}, u32[]{:S(2)}) %all-to-all-start) | async-done | bytes 16416 | tf_op jit(solution)/shard_map/all_to_all | solution.py:472
  43.1 15.0 %all_to_all.37 = f32[16,32,128]{2,1,0:T(8,128)S(1)} all-to-all(f32[16,32,128]{2,1,0:T(8,128)S(1)} %copies.1), channel_id=1, replica_groups=mesh['tile'=32,'mem'=16] {'mem'}, dimensions={0} | all-to-all | bytes 524288 | tf_op jit(solution)/shard_map/all_to_all | solution.py:499
  58.0 4.0 %interpolate.1 = (f32[128,512]{1,0:T(8,128)S(1)}, f32[4,16,512]{2,1,0:T(8,128)}) custom-call(f32[512,128]{1,0:T(8,128)S(1)} %bitcast.26, f32[128,512]{1,0:T(8,128)S(1)} %partial.1.unused_ref.field_ref), custom_call_target="tpu_custom_call" | custom-call | tf_op jit(solution)/shard_map/interpolate/pallas_call | solution.py:501
  62.0 3.5 %all-to-all-start.2 = ((f32[4,16,512]{2,1,0:T(8,128)}), f32[4,16,512]{2,1,0:T(8,128)S(1)}, u32[]{:S(2)}, u32[]{:S(2)}) async-start(f32[4,16,512]{2,1,0:T(8,128)} %get-tuple-element.24), calls=%async_computation.2 | async-start | bytes 262144 | tf_op jit(solution)/shard_map/all_to_all | solution.py:510
  65.5 5.5 %collective-permute-start = (f32[512,128]{1,0:T(8,128)S(1)}, f32[512,128]{1,0:T(8,128)S(1)}, u32[]{:S(2)}, u32[]{:S(2)}) collective-permute-start(f32[512,128]{1,0:T(8,128)S(1)} %copy-done.7), channel_id=1, source_target_pairs={{16,32},{48,64},{80,96},{112,128},{144,160},{176,192},{208,224},{2... | collective-permute-start | bytes 786440 | tf_op jit(solution)/shard_map/ppermute | solution.py:437
  71.0 0.0 all-to-all-done.2.in_ref
  71.0 7.2 %all_to_all.38.sums_ref = f32[4,16,512]{2,1,0:T(8,128)S(1)} all-to-all(f32[4,16,512]{2,1,0:T(8,128)S(1)} %add.1), channel_id=1, replica_groups={{0,4,8,12},{1,5,9,13},{2,6,10,14},{3,7,11,15},{16,20,24,28},{17,21,25,2..., dimensions={0} | all-to-all | bytes 262144 | tf_op jit(solution)/shard_map/all_to_all | solution.py:510
  78.2 3.2 %spread.1 = (f32[128,512]{1,0:T(8,128)S(1)}, f32[32,512]{1,0:T(8,128)S(1)}, f32[32,512]{1,0:T(8,128)S(1)}, f32[32,16]{1,0:T(8,128)}) custom-call(f32[512,128]{1,0:T(8,128)S(1)} %bitcast.27, f32[128,512]{1,0:T(8,128)S(1)} %get-tuple-element.23.comps_ref, f32[4,16,512]{2,1,0:T(8,128)S(1)} %all_to_all.38.sums_ref), custom_call_target="tpu_custom_call" | custom-call | tf_op jit(solution)/shard_map/spread/pallas_call | solution.py:514
  81.5 7.2 %collective-permute-start.3 = (f32[32,512]{1,0:T(8,128)S(1)}, f32[32,512]{1,0:T(8,128)S(1)}, u32[]{:S(2)}, u32[]{:S(2)}) collective-permute-start(f32[32,512]{1,0:T(8,128)S(1)} %get-tuple-element.26), channel_id=1, source_target_pairs={{16,32},{48,64},{80,96},{112,128},{144,160},{176,192},{208,224},{2... | collective-permute-start | bytes 196616 | tf_op jit(solution)/shard_map/ppermute | solution.py:437
  88.7 1.9 %collective-permute-start.4 = (f32[32,512]{1,0:T(8,128)S(1)}, f32[32,512]{1,0:T(8,128)S(1)}, u32[]{:S(2)}, u32[]{:S(2)}) collective-permute-start(f32[32,512]{1,0:T(8,128)S(1)} %get-tuple-element.27), channel_id=1, source_target_pairs={{0,16},{32,48},{64,80},{96,112},{128,144},{160,176},{192,208},{224... | collective-permute-start | bytes 196616 | tf_op jit(solution)/shard_map/ppermute | solution.py:440
  90.6 9.4 %all-to-all-start.4 = ((f32[32,1,16]{2,1,0:T(1,128)}), f32[32,1,16]{2,1,0:T(1,128)S(1)}, u32[]{:S(2)}, u32[]{:S(2)}) async-start(f32[32,1,16]{2,1,0:T(1,128)} %bitcast.19), calls=%async_computation.4 | async-start | bytes 32768 | tf_op jit(solution)/shard_map/all_to_all | solution.py:528
  100.0 0.0 collective-permute-done.far_ref
  100.0 0.0 collective-permute-done.3.adjoint_far_ref
  100.1 0.0 collective-permute-done.4.adjoint_near_ref
  100.1 5.4 %grad.1 = (f32[1024,128]{1,0:T(8,128)}, f32[8,128]{1,0:T(8,128)S(1)}) custom-call(f32[4]{0:T(128)S(1)} %copy-done.5, f32[4]{0:T(128)S(1)} %copy-done.6, f32[1024,128]{1,0:T(8,128)S(1)} %bitcast.30, s32[16,512]{1,0:T(8,128)S(1)} %copy-done.2, f32[1024,128]{1,0:T(8,128)S(1)} %get-tuple-element.18.members_ref, f32[512,128]{1,0:T(8,128)S(1)} %collective-permute-done.far_ref, ...), custom_call_target="tpu_custom_call" | custom-call | flops 99999997952 | tf_op jit(solution)/shard_map/grad/pallas_call | solution.py:530
  105.4 8.7 %all-to-all-done.4 = f32[32,1,16]{2,1,0:T(1,128)S(1)} async-done(((f32[32,1,16]{2,1,0:T(1,128)}), f32[32,1,16]{2,1,0:T(1,128)S(1)}, u32[]{:S(2)}, u32[]{:S(2)}) %all-to-all-start.4) | async-done | bytes 2080 | tf_op jit(solution)/shard_map/all_to_all | solution.py:528
  114.2 0.8 unpack.1
  (11 shorter events, 0.1 us)
Async XLA Ops:
  0.6 28.2 %copy-start = (f32[4,4,16,512]{3,2,1,0:T(8,128)S(1)}, f32[4,4,16,512]{3,2,1,0:T(8,128)}, u32[]{:S(2)}) copy-start(f32[4,4,16,512]{3,2,1,0:T(8,128)} %param.12) | copy-start | bytes 1572868
  0.6 28.2 %copy-start.1 = (bf16[4,4,16,512]{3,2,1,0:T(8,128)(2,1)S(1)}, bf16[4,4,16,512]{3,2,1,0:T(8,128)(2,1)}, u32[]{:S(2)}) copy-start(bf16[4,4,16,512]{3,2,1,0:T(8,128)(2,1)} %members_ref.1) | copy-start | bytes 786436
  3.5 25.4 %copy-start.2 = (s32[16,512]{1,0:T(8,128)S(1)}, s32[16,512]{1,0:T(8,128)}, u32[]{:S(2)}) copy-start(s32[16,512]{1,0:T(8,128)} %land_ref.3) | copy-start | bytes 98308
  3.5 26.3 %collective-permute-start.1 = (f32[1024,128]{1,0:T(8,128)}, f32[1024,128]{1,0:T(8,128)S(1)}, u32[]{:S(2)}, u32[]{:S(2)}) collective-permute-start(f32[1024,128]{1,0:T(8,128)} %get-tuple-element.20), channel_id=1, source_target_pairs={{0,16},{32,48},{64,80},{96,112},{128,144},{160,176},{192,208},{224... | collective-permute-start | bytes 1572872 | tf_op jit(solution)/shard_map/ppermute | solution.py:440
  12.3 17.5 %collective-permute-start.2 = (f32[512,128]{1,0:T(8,128)}, f32[512,128]{1,0:T(8,128)S(1)}, u32[]{:S(2)}, u32[]{:S(2)}) collective-permute-start(f32[512,128]{1,0:T(8,128)} %get-tuple-element.22), channel_id=1, source_target_pairs={{16,32},{48,64},{80,96},{112,128},{144,160},{176,192},{208,224},{2... | collective-permute-start | bytes 786440 | tf_op jit(solution)/shard_map/ppermute | solution.py:437
  15.6 13.2 %copy-start.4 = (s32[256,1]{0,1:T(1,128)S(1)}, s32[256,1]{0,1:T(1,128)}, u32[]{:S(2)}) copy-start(s32[256,1]{0,1:T(1,128)} %param.17) | copy-start | bytes 3076
  15.6 27.4 %all-to-all-start = ((f32[32,1,128]{2,1,0:T(1,128)}), f32[32,1,128]{2,1,0:T(1,128)S(1)}, u32[]{:S(2)}, u32[]{:S(2)}) async-start(f32[32,1,128]{2,1,0:T(1,128)} %bitcast.31), calls=%async_computation | async-start | bytes 32768 | tf_op jit(solution)/shard_map/all_to_all | solution.py:472
  28.9 0.7 copy-start.3
  29.8 0.7 copy-start.5
  29.8 0.7 copy-start.6
  62.0 3.5 %copy-start.7 = (f32[512,128]{1,0:T(8,128)S(1)}, f32[512,128]{1,0:T(8,128)}, u32[]{:S(2)}) copy-start(f32[512,128]{1,0:T(8,128)} %get-tuple-element.19) | copy-start | bytes 786436
  62.0 8.9 %all-to-all-start.2 = ((f32[4,16,512]{2,1,0:T(8,128)}), f32[4,16,512]{2,1,0:T(8,128)S(1)}, u32[]{:S(2)}, u32[]{:S(2)}) async-start(f32[4,16,512]{2,1,0:T(8,128)} %get-tuple-element.24), calls=%async_computation.2 | async-start | bytes 262144 | tf_op jit(solution)/shard_map/all_to_all | solution.py:510
  65.5 34.5 %collective-permute-start = (f32[512,128]{1,0:T(8,128)S(1)}, f32[512,128]{1,0:T(8,128)S(1)}, u32[]{:S(2)}, u32[]{:S(2)}) collective-permute-start(f32[512,128]{1,0:T(8,128)S(1)} %copy-done.7), channel_id=1, source_target_pairs={{16,32},{48,64},{80,96},{112,128},{144,160},{176,192},{208,224},{2... | collective-permute-start | bytes 786440 | tf_op jit(solution)/shard_map/ppermute | solution.py:437
  81.5 18.6 %collective-permute-start.3 = (f32[32,512]{1,0:T(8,128)S(1)}, f32[32,512]{1,0:T(8,128)S(1)}, u32[]{:S(2)}, u32[]{:S(2)}) collective-permute-start(f32[32,512]{1,0:T(8,128)S(1)} %get-tuple-element.26), channel_id=1, source_target_pairs={{16,32},{48,64},{80,96},{112,128},{144,160},{176,192},{208,224},{2... | collective-permute-start | bytes 196616 | tf_op jit(solution)/shard_map/ppermute | solution.py:437
  88.7 11.4 %collective-permute-start.4 = (f32[32,512]{1,0:T(8,128)S(1)}, f32[32,512]{1,0:T(8,128)S(1)}, u32[]{:S(2)}, u32[]{:S(2)}) collective-permute-start(f32[32,512]{1,0:T(8,128)S(1)} %get-tuple-element.27), channel_id=1, source_target_pairs={{0,16},{32,48},{64,80},{96,112},{128,144},{160,176},{192,208},{224... | collective-permute-start | bytes 196616 | tf_op jit(solution)/shard_map/ppermute | solution.py:440
  90.6 23.6 %all-to-all-start.4 = ((f32[32,1,16]{2,1,0:T(1,128)}), f32[32,1,16]{2,1,0:T(1,128)S(1)}, u32[]{:S(2)}, u32[]{:S(2)}) async-start(f32[32,1,16]{2,1,0:T(1,128)} %bitcast.19), calls=%async_computation.4 | async-start | bytes 32768 | tf_op jit(solution)/shard_map/all_to_all | solution.py:528

commit v7 on v6

--- a/solution.py
+++ b/solution.py
@@ -14,6 +14,7 @@
 HIGHEST = lax.Precision.HIGHEST
 F32 = jnp.float32
 BF16 = jnp.bfloat16
+I16 = jnp.int16
 PARTIAL_FLOPS = 10**11
 GRAD_FLOPS = 10**11
 
@@ -324,8 +325,8 @@
     pieces[: 8 * rows, :] = top
     pieces[8 * rows :, :] = (field - top.astype(F32)).astype(BF16)
     for s in range(slots):
-        column = comps_ref[s : s + 1, :].astype(jnp.int32)
-        hot = jnp.where(iota((columns, count), 0) == column, 1.0, 0.0).astype(BF16)
+        column = comps_ref[s : s + 1, :].astype(jnp.int32).astype(I16)
+        hot = jnp.where(iota((columns, count), 0).astype(I16) == column, BF16(1.0), BF16(0.0))
         found = jnp.dot(pieces[...], hot, preferred_element_type=F32)
         row, lower, upper = corner_terms(s, slots, comps_ref, None)
         total = jnp.zeros((8, count), F32)
@@ -354,8 +355,16 @@
         out_ref[k] = total
 
 
+def spread_scratch(rows, count, columns):
+    return [
+        pltpu.VMEM((16 * rows, count), BF16),
+        pltpu.VMEM((count, columns), BF16),
+        pltpu.VMEM((16 * rows, columns), F32),
+    ]
+
+
 def spread_body(
-    rows, slots, tiles, factor, raw_ref, comps_ref, sums_ref, own_ref, far_ref, near_ref, back_ref, left, total
+    rows, slots, tiles, factor, raw_ref, comps_ref, sums_ref, own_ref, far_ref, near_ref, back_ref, left, hot, total
 ):
     columns = own_ref.shape[1]
     count = comps_ref.shape[1]
@@ -376,18 +385,23 @@
     dep = rinv * (hofx - value)
     for s in range(slots):
         row, lower, upper = corner_terms(s, slots, comps_ref, dep[s : s + 1, :])
-        previous = None
+        previous, terms = None, []
         for g in range(rows):
             at = row == float(g)
             rest = 0.0 if previous is None else jnp.where(previous, upper, 0.0)
-            term = jnp.where(at, lower, rest)
-            top = term.astype(BF16)
-            left[g * 8 : g * 8 + 8, :] = top
-            left[8 * (rows + g) : 8 * (rows + g) + 8, :] = (term - top.astype(F32)).astype(BF16)
+            terms.append(jnp.where(at, lower, rest))
             previous = at
-        column = raw_ref[:, s : s + 1].astype(jnp.int32)
-        hot = jnp.where(iota((count, columns), 1) == column, 1.0, 0.0).astype(BF16)
-        part = jnp.dot(left[...], hot, preferred_element_type=F32)
+            if g % 2 == 1:
+                pair = jnp.concatenate(terms[-2:], axis=0)
+                top = pair.astype(BF16)
+                left[g * 8 - 8 : g * 8 + 8, :] = top
+                left[8 * (rows + g) - 8 : 8 * (rows + g) + 8, :] = (pair - top.astype(F32)).astype(BF16)
+        column = jnp.broadcast_to(raw_ref[:, s : s + 1].astype(jnp.int32), (count, LANES)).astype(I16)
+        lane16 = iota((count, LANES), 1).astype(I16)
+        for j in range(columns // LANES):
+            lanes = slice(j * LANES, (j + 1) * LANES)
+            hot[:, lanes] = jnp.where(lane16 + I16(j * LANES) == column, BF16(1.0), BF16(0.0))
+        part = jnp.dot(left[...], hot[...], preferred_element_type=F32)
         if s == 0:
             total[...] = part
         else:
@@ -520,7 +534,7 @@
             jax.ShapeDtypeStruct((tiles, slots), F32),
         ),
         vmem(3),
-        [pltpu.VMEM((16 * rows, count), BF16), pltpu.VMEM((16 * rows, columns), F32)],
+        spread_scratch(rows, count, columns),
         name="spread",
     )(raw, comps, sums)
     adjoint_far = to_far(edge_far)

time: 116 us -> 114 us (0.983)
  no operation moved by 1% of the time
where the time goes in v7:
time: 114 us
  starting transfers between devices  52.6 us (46%)
  blocking collectives  22.2 us (19%)
  Pallas kernels  20.4 us (18%)
  waiting for transfers between devices  16.3 us (14%)
  local copies, waits for them, and re-layouts  1.42 us (1%)
    ppermute x3, starting transfers between devices, to_far(): return lax.ppermute(x, 'tile', far_pairs)  15.8 us
    all_to_all x1, blocking collectives, on_device(): lax.all_to_all(copied, 'mem', split_axis=0, concat_axis=0, tiled=True)  15 us
    all_to_all x1, starting transfers between devices, on_device(): lax.all_to_all(sent, 'tile', split_axis=0, concat_axis=0, tiled=True)  13.2 us
    ppermute x2, starting transfers between devices, to_near(): return lax.ppermute(x, 'tile', near_pairs)  10.7 us
    all_to_all x1, starting transfers between devices, on_device(): lax.all_to_all(back, 'tile', split_axis=0, concat_axis=0, tiled=True)  9.47 us
    all_to_all x1, waiting for transfers between devices, on_device(): lax.all_to_all(back, 'tile', split_axis=0, concat_axis=0, tiled=True)  8.74 us
    all_to_all x1, waiting for transfers between devices, on_device(): lax.all_to_all(sent, 'tile', split_axis=0, concat_axis=0, tiled=True)  7.54 us
    all_to_all x1, blocking collectives, gather(): lax.all_to_all(x, 'mem', split_axis=0, concat_axis=0, axis_index_groups=g...  7.21 us
  transfers between devices with their start and end apart: 8, of which 2 were waited for; matrix products, arithmetic and copies ran while one was open for 0% of the time, Pallas kernels for 12%

profile of v7, /device:TPU:1, one launch (start us, length us, event | category | flops | bytes accessed | tf_op | source)
XLA Modules:
  0.0 113.8 jit_solution(12561275402475884025)
XLA Ops:
  0.7 2.8 %prep.1 = (f32[512,128]{1,0:T(8,128)}, f32[512,128]{1,0:T(8,128)}, f32[1024,128]{1,0:T(8,128)}, f32[32,128]{1,0:T(8,128)}) custom-call(f32[1024,128]{1,0:T(8,128)} %bitcast.28, bf16[4,4,16,512]{3,2,1,0:T(8,128)(2,1)} %members_ref.1, s32[16,512]{1,0:T(8,128)} %land_ref.3, s32[1,256]{1,0:T(1,128)} %bitcast.34, s32[1,256]{1,0:T(1,128)} %bitcast.36, ...), custom_call_target="tpu_custom_call" | custom-call | tf_op jit(solution)/shard_map/prep/pallas_call | solution.py:471
  3.5 0.0 copy-start.2
  3.5 8.8 %collective-permute-start.1 = (f32[1024,128]{1,0:T(8,128)}, f32[1024,128]{1,0:T(8,128)S(1)}, u32[]{:S(2)}, u32[]{:S(2)}) collective-permute-start(f32[1024,128]{1,0:T(8,128)} %get-tuple-element.20), channel_id=1, source_target_pairs={{0,16},{32,48},{64,80},{96,112},{128,144},{160,176},{192,208},{224... | collective-permute-start | bytes 1572872 | tf_op jit(solution)/shard_map/ppermute | solution.py:454
  12.3 3.3 %collective-permute-start.2 = (f32[512,128]{1,0:T(8,128)}, f32[512,128]{1,0:T(8,128)S(1)}, u32[]{:S(2)}, u32[]{:S(2)}) collective-permute-start(f32[512,128]{1,0:T(8,128)} %get-tuple-element.22), channel_id=1, source_target_pairs={{16,32},{48,64},{80,96},{112,128},{144,160},{176,192},{208,224},{2... | collective-permute-start | bytes 786440 | tf_op jit(solution)/shard_map/ppermute | solution.py:451
  15.6 0.0 copy-start.4
  15.6 13.2 %all-to-all-start = ((f32[32,1,128]{2,1,0:T(1,128)}), f32[32,1,128]{2,1,0:T(1,128)S(1)}, u32[]{:S(2)}, u32[]{:S(2)}) async-start(f32[32,1,128]{2,1,0:T(1,128)} %bitcast.31), calls=%async_computation | async-start | bytes 32768 | tf_op jit(solution)/shard_map/all_to_all | solution.py:486
  28.9 0.7 copy-done.3
  29.6 0.1 mask.1
  29.8 0.0 collective-permute-done.2.far_ref
  29.8 0.0 collective-permute-done.1.near_ref
  29.8 0.0 copy-start.5
  29.8 0.0 copy-start.6
  29.8 0.6 copy-done.5
  30.5 0.0 copy-done.6
  30.5 5.0 %partial.1.unused_ref.field_ref = f32[128,512]{1,0:T(8,128)S(1)} custom-call(f32[4]{0:T(128)S(1)} %copy-done.5, f32[4]{0:T(128)S(1)} %copy-done.6, f32[1024,128]{1,0:T(8,128)S(1)} %get-tuple-element.21.own_ref, f32[512,128]{1,0:T(8,128)S(1)} %collective-permute-done.2.far_ref, f32[1024,128]{1,0:T(8,128)S(1)} %collective-permute-done.1.near_ref, ...), custom_call_target="tpu_custom_call" | custom-call | flops 99999997952 | tf_op jit(solution)/shard_map/partial/pallas_call | solution.py:499
  35.5 7.5 %all-to-all-done = f32[32,1,128]{2,1,0:T(1,128)S(1)} async-done(((f32[32,1,128]{2,1,0:T(1,128)}), f32[32,1,128]{2,1,0:T(1,128)S(1)}, u32[]{:S(2)}, u32[]{:S(2)}) %all-to-all-start) | async-done | bytes 16416 | tf_op jit(solution)/shard_map/all_to_all | solution.py:486
  43.1 15.0 %all_to_all.37 = f32[16,32,128]{2,1,0:T(8,128)S(1)} all-to-all(f32[16,32,128]{2,1,0:T(8,128)S(1)} %copies.1), channel_id=1, replica_groups=mesh['tile'=32,'mem'=16] {'mem'}, dimensions={0} | all-to-all | bytes 524288 | tf_op jit(solution)/shard_map/all_to_all | solution.py:513
  58.0 3.2 %interpolate.1 = (f32[128,512]{1,0:T(8,128)S(1)}, f32[4,16,512]{2,1,0:T(8,128)}) custom-call(f32[512,128]{1,0:T(8,128)S(1)} %bitcast.26, f32[128,512]{1,0:T(8,128)S(1)} %partial.1.unused_ref.field_ref), custom_call_target="tpu_custom_call" | custom-call | tf_op jit(solution)/shard_map/interpolate/pallas_call | solution.py:515
  61.2 3.5 %all-to-all-start.2 = ((f32[4,16,512]{2,1,0:T(8,128)}), f32[4,16,512]{2,1,0:T(8,128)S(1)}, u32[]{:S(2)}, u32[]{:S(2)}) async-start(f32[4,16,512]{2,1,0:T(8,128)} %get-tuple-element.24), calls=%async_computation.2 | async-start | bytes 262144 | tf_op jit(solution)/shard_map/all_to_all | solution.py:524
  64.7 5.5 %collective-permute-start = (f32[512,128]{1,0:T(8,128)S(1)}, f32[512,128]{1,0:T(8,128)S(1)}, u32[]{:S(2)}, u32[]{:S(2)}) collective-permute-start(f32[512,128]{1,0:T(8,128)S(1)} %copy-done.7), channel_id=1, source_target_pairs={{16,32},{48,64},{80,96},{112,128},{144,160},{176,192},{208,224},{2... | collective-permute-start | bytes 786440 | tf_op jit(solution)/shard_map/ppermute | solution.py:451
  70.1 0.0 all-to-all-done.2.in_ref
  70.1 7.2 %all_to_all.38.sums_ref = f32[4,16,512]{2,1,0:T(8,128)S(1)} all-to-all(f32[4,16,512]{2,1,0:T(8,128)S(1)} %add.1), channel_id=1, replica_groups={{0,4,8,12},{1,5,9,13},{2,6,10,14},{3,7,11,15},{16,20,24,28},{17,21,25,2..., dimensions={0} | all-to-all | bytes 262144 | tf_op jit(solution)/shard_map/all_to_all | solution.py:524
  77.4 3.1 %spread.1 = (f32[128,512]{1,0:T(8,128)S(1)}, f32[32,512]{1,0:T(8,128)S(1)}, f32[32,512]{1,0:T(8,128)S(1)}, f32[32,16]{1,0:T(8,128)}) custom-call(f32[512,128]{1,0:T(8,128)S(1)} %bitcast.27, f32[128,512]{1,0:T(8,128)S(1)} %get-tuple-element.23.comps_ref, f32[4,16,512]{2,1,0:T(8,128)S(1)} %all_to_all.38.sums_ref), custom_call_target="tpu_custom_call" | custom-call | tf_op jit(solution)/shard_map/spread/pallas_call | solution.py:528
  80.5 7.0 %collective-permute-start.3 = (f32[32,512]{1,0:T(8,128)S(1)}, f32[32,512]{1,0:T(8,128)S(1)}, u32[]{:S(2)}, u32[]{:S(2)}) collective-permute-start(f32[32,512]{1,0:T(8,128)S(1)} %get-tuple-element.26), channel_id=1, source_target_pairs={{16,32},{48,64},{80,96},{112,128},{144,160},{176,192},{208,224},{2... | collective-permute-start | bytes 196616 | tf_op jit(solution)/shard_map/ppermute | solution.py:451
  87.5 1.9 %collective-permute-start.4 = (f32[32,512]{1,0:T(8,128)S(1)}, f32[32,512]{1,0:T(8,128)S(1)}, u32[]{:S(2)}, u32[]{:S(2)}) collective-permute-start(f32[32,512]{1,0:T(8,128)S(1)} %get-tuple-element.27), channel_id=1, source_target_pairs={{0,16},{32,48},{64,80},{96,112},{128,144},{160,176},{192,208},{224... | collective-permute-start | bytes 196616 | tf_op jit(solution)/shard_map/ppermute | solution.py:454
  89.4 9.5 %all-to-all-start.4 = ((f32[32,1,16]{2,1,0:T(1,128)}), f32[32,1,16]{2,1,0:T(1,128)S(1)}, u32[]{:S(2)}, u32[]{:S(2)}) async-start(f32[32,1,16]{2,1,0:T(1,128)} %bitcast.19), calls=%async_computation.4 | async-start | bytes 32768 | tf_op jit(solution)/shard_map/all_to_all | solution.py:542
  98.9 0.0 collective-permute-done.far_ref
  98.9 0.0 collective-permute-done.3.adjoint_far_ref
  98.9 0.0 collective-permute-done.4.adjoint_near_ref
  98.9 5.4 %grad.1 = (f32[1024,128]{1,0:T(8,128)}, f32[8,128]{1,0:T(8,128)S(1)}) custom-call(f32[4]{0:T(128)S(1)} %copy-done.5, f32[4]{0:T(128)S(1)} %copy-done.6, f32[1024,128]{1,0:T(8,128)S(1)} %bitcast.30, s32[16,512]{1,0:T(8,128)S(1)} %copy-done.2, f32[1024,128]{1,0:T(8,128)S(1)} %get-tuple-element.18.members_ref, f32[512,128]{1,0:T(8,128)S(1)} %collective-permute-done.far_ref, ...), custom_call_target="tpu_custom_call" | custom-call | flops 99999997952 | tf_op jit(solution)/shard_map/grad/pallas_call | solution.py:544
  104.3 8.7 %all-to-all-done.4 = f32[32,1,16]{2,1,0:T(1,128)S(1)} async-done(((f32[32,1,16]{2,1,0:T(1,128)}), f32[32,1,16]{2,1,0:T(1,128)S(1)}, u32[]{:S(2)}, u32[]{:S(2)}) %all-to-all-start.4) | async-done | bytes 2080 | tf_op jit(solution)/shard_map/all_to_all | solution.py:542
  113.0 0.8 unpack.1
  (11 shorter events, 0.1 us)
Async XLA Ops:
  0.6 28.2 %copy-start = (f32[4,4,16,512]{3,2,1,0:T(8,128)S(1)}, f32[4,4,16,512]{3,2,1,0:T(8,128)}, u32[]{:S(2)}) copy-start(f32[4,4,16,512]{3,2,1,0:T(8,128)} %param.12) | copy-start | bytes 1572868
  0.6 28.2 %copy-start.1 = (bf16[4,4,16,512]{3,2,1,0:T(8,128)(2,1)S(1)}, bf16[4,4,16,512]{3,2,1,0:T(8,128)(2,1)}, u32[]{:S(2)}) copy-start(bf16[4,4,16,512]{3,2,1,0:T(8,128)(2,1)} %members_ref.1) | copy-start | bytes 786436
  3.5 25.4 %copy-start.2 = (s32[16,512]{1,0:T(8,128)S(1)}, s32[16,512]{1,0:T(8,128)}, u32[]{:S(2)}) copy-start(s32[16,512]{1,0:T(8,128)} %land_ref.3) | copy-start | bytes 98308
  3.5 26.3 %collective-permute-start.1 = (f32[1024,128]{1,0:T(8,128)}, f32[1024,128]{1,0:T(8,128)S(1)}, u32[]{:S(2)}, u32[]{:S(2)}) collective-permute-start(f32[1024,128]{1,0:T(8,128)} %get-tuple-element.20), channel_id=1, source_target_pairs={{0,16},{32,48},{64,80},{96,112},{128,144},{160,176},{192,208},{224... | collective-permute-start | bytes 1572872 | tf_op jit(solution)/shard_map/ppermute | solution.py:454
  12.3 17.5 %collective-permute-start.2 = (f32[512,128]{1,0:T(8,128)}, f32[512,128]{1,0:T(8,128)S(1)}, u32[]{:S(2)}, u32[]{:S(2)}) collective-permute-start(f32[512,128]{1,0:T(8,128)} %get-tuple-element.22), channel_id=1, source_target_pairs={{16,32},{48,64},{80,96},{112,128},{144,160},{176,192},{208,224},{2... | collective-permute-start | bytes 786440 | tf_op jit(solution)/shard_map/ppermute | solution.py:451
  15.6 13.2 %copy-start.4 = (s32[256,1]{0,1:T(1,128)S(1)}, s32[256,1]{0,1:T(1,128)}, u32[]{:S(2)}) copy-start(s32[256,1]{0,1:T(1,128)} %param.17) | copy-start | bytes 3076
  15.6 27.4 %all-to-all-start = ((f32[32,1,128]{2,1,0:T(1,128)}), f32[32,1,128]{2,1,0:T(1,128)S(1)}, u32[]{:S(2)}, u32[]{:S(2)}) async-start(f32[32,1,128]{2,1,0:T(1,128)} %bitcast.31), calls=%async_computation | async-start | bytes 32768 | tf_op jit(solution)/shard_map/all_to_all | solution.py:486
  28.9 0.7 copy-start.3
  29.8 0.7 copy-start.5
  29.8 0.7 copy-start.6
  61.2 3.5 %copy-start.7 = (f32[512,128]{1,0:T(8,128)S(1)}, f32[512,128]{1,0:T(8,128)}, u32[]{:S(2)}) copy-start(f32[512,128]{1,0:T(8,128)} %get-tuple-element.19) | copy-start | bytes 786436
  61.2 8.9 %all-to-all-start.2 = ((f32[4,16,512]{2,1,0:T(8,128)}), f32[4,16,512]{2,1,0:T(8,128)S(1)}, u32[]{:S(2)}, u32[]{:S(2)}) async-start(f32[4,16,512]{2,1,0:T(8,128)} %get-tuple-element.24), calls=%async_computation.2 | async-start | bytes 262144 | tf_op jit(solution)/shard_map/all_to_all | solution.py:524
  64.7 34.2 %collective-permute-start = (f32[512,128]{1,0:T(8,128)S(1)}, f32[512,128]{1,0:T(8,128)S(1)}, u32[]{:S(2)}, u32[]{:S(2)}) collective-permute-start(f32[512,128]{1,0:T(8,128)S(1)} %copy-done.7), channel_id=1, source_target_pairs={{16,32},{48,64},{80,96},{112,128},{144,160},{176,192},{208,224},{2... | collective-permute-start | bytes 786440 | tf_op jit(solution)/shard_map/ppermute | solution.py:451
  80.5 18.4 %collective-permute-start.3 = (f32[32,512]{1,0:T(8,128)S(1)}, f32[32,512]{1,0:T(8,128)S(1)}, u32[]{:S(2)}, u32[]{:S(2)}) collective-permute-start(f32[32,512]{1,0:T(8,128)S(1)} %get-tuple-element.26), channel_id=1, source_target_pairs={{16,32},{48,64},{80,96},{112,128},{144,160},{176,192},{208,224},{2... | collective-permute-start | bytes 196616 | tf_op jit(solution)/shard_map/ppermute | solution.py:451
  87.5 11.4 %collective-permute-start.4 = (f32[32,512]{1,0:T(8,128)S(1)}, f32[32,512]{1,0:T(8,128)S(1)}, u32[]{:S(2)}, u32[]{:S(2)}) collective-permute-start(f32[32,512]{1,0:T(8,128)S(1)} %get-tuple-element.27), channel_id=1, source_target_pairs={{0,16},{32,48},{64,80},{96,112},{128,144},{160,176},{192,208},{224... | collective-permute-start | bytes 196616 | tf_op jit(solution)/shard_map/ppermute | solution.py:454
  89.4 23.6 %all-to-all-start.4 = ((f32[32,1,16]{2,1,0:T(1,128)}), f32[32,1,16]{2,1,0:T(1,128)S(1)}, u32[]{:S(2)}, u32[]{:S(2)}) async-start(f32[32,1,16]{2,1,0:T(1,128)} %bitcast.19), calls=%async_computation.4 | async-start | bytes 32768 | tf_op jit(solution)/shard_map/all_to_all | solution.py:542

commit v8 on v7

--- a/solution.py
+++ b/solution.py
@@ -191,7 +191,7 @@
     sent_ref[...] = pack(tiles, slots, tile_row, data_ref[...])
 
 
-def mask_body(unused_ref, tile_ref, alpha_ref, members_ref, land_ref, own_ref, masked_ref, info_ref):
+def mask_body(tile_ref, alpha_ref, members_ref, land_ref, own_ref, masked_ref, info_ref):
     tile_row = tile_ref[...].astype(F32)
     unused, rank = ranks(tile_row)
     info_ref[0:1, :] = tile_row
@@ -491,9 +491,9 @@
             jax.ShapeDtypeStruct((size, LANES), F32),
             jax.ShapeDtypeStruct((2, count), F32),
         ),
-        [ANY] + vmem(4),
+        vmem(4),
         name="mask",
-    )(sent, sources[3], alpha_tiles, perturbs, land_mask)
+    )(sources[3], alpha_tiles, perturbs, land_mask)
     count = mems * tiles
     work = pltpu.VMEM((rows + 2 * STEPS, 8, columns), F32)
     partial = call(

time: 114 us -> 115 us (level)
  transfers between devices with their start and end apart: 8 -> 8, of which waited for: 2 -> 3; matrix products, arithmetic and copies ran while one was open for 0% -> 0% of each run, Pallas kernels for 12% -> 12%
where the time goes in v8:
time: 115 us; the launch traced here: 114 us
  starting transfers between devices  52.6 us (46%)
  blocking collectives  22.2 us (19%)
  Pallas kernels  20.6 us (18%)
  waiting for transfers between devices  17 us (15%)
    ppermute x3, starting transfers between devices, to_far(): return lax.ppermute(x, 'tile', far_pairs)  15.8 us
    all_to_all x1, blocking collectives, on_device(): lax.all_to_all(copied, 'mem', split_axis=0, concat_axis=0, tiled=True)  15 us
    all_to_all x1, starting transfers between devices, on_device(): lax.all_to_all(sent, 'tile', split_axis=0, concat_axis=0, tiled=True)  13.2 us
    ppermute x2, starting transfers between devices, to_near(): return lax.ppermute(x, 'tile', near_pairs)  10.7 us
    all_to_all x1, starting transfers between devices, on_device(): lax.all_to_all(back, 'tile', split_axis=0, concat_axis=0, tiled=True)  9.48 us
    all_to_all x1, waiting for transfers between devices, on_device(): lax.all_to_all(back, 'tile', split_axis=0, concat_axis=0, tiled=True)  8.74 us
    all_to_all x1, waiting for transfers between devices, on_device(): lax.all_to_all(sent, 'tile', split_axis=0, concat_axis=0, tiled=True)  7.6 us
    all_to_all x1, blocking collectives, gather(): lax.all_to_all(x, 'mem', split_axis=0, concat_axis=0, axis_index_groups=g...  7.21 us
  transfers between devices with their start and end apart: 8, of which 3 were waited for; matrix products, arithmetic and copies ran while one was open for 0% of the time, Pallas kernels for 12%

profile of v8, /device:TPU:1, one launch (start us, length us, event | category | flops | bytes accessed | tf_op | source)
XLA Modules:
  0.0 114.0 jit_solution(10194805883799695274)
XLA Ops:
  0.6 0.0 copy-start
  0.6 0.0 copy-start.1
  0.7 2.8 %prep.1 = (f32[512,128]{1,0:T(8,128)}, f32[512,128]{1,0:T(8,128)}, f32[1024,128]{1,0:T(8,128)}, f32[32,128]{1,0:T(8,128)}) custom-call(f32[1024,128]{1,0:T(8,128)} %bitcast.28, bf16[4,4,16,512]{3,2,1,0:T(8,128)(2,1)} %refs_1_.1, s32[16,512]{1,0:T(8,128)} %land_ref.3, s32[1,256]{1,0:T(1,128)} %bitcast.33, s32[1,256]{1,0:T(1,128)} %bitcast.36, ...), custom_call_target="tpu_custom_call" | custom-call | tf_op jit(solution)/shard_map/prep/pallas_call | solution.py:471
  3.5 0.0 copy-start.2
  3.5 8.8 %collective-permute-start.1 = (f32[1024,128]{1,0:T(8,128)}, f32[1024,128]{1,0:T(8,128)S(1)}, u32[]{:S(2)}, u32[]{:S(2)}) collective-permute-start(f32[1024,128]{1,0:T(8,128)} %get-tuple-element.19), channel_id=1, source_target_pairs={{0,16},{32,48},{64,80},{96,112},{128,144},{160,176},{192,208},{224... | collective-permute-start | bytes 1572872 | tf_op jit(solution)/shard_map/ppermute | solution.py:454
  12.3 3.3 %collective-permute-start.2 = (f32[512,128]{1,0:T(8,128)}, f32[512,128]{1,0:T(8,128)S(1)}, u32[]{:S(2)}, u32[]{:S(2)}) collective-permute-start(f32[512,128]{1,0:T(8,128)} %get-tuple-element.21), channel_id=1, source_target_pairs={{16,32},{48,64},{80,96},{112,128},{144,160},{176,192},{208,224},{2... | collective-permute-start | bytes 786440 | tf_op jit(solution)/shard_map/ppermute | solution.py:451
  15.6 0.0 copy-start.3
  15.6 13.2 %all-to-all-start = ((f32[32,1,128]{2,1,0:T(1,128)}), f32[32,1,128]{2,1,0:T(1,128)S(1)}, u32[]{:S(2)}, u32[]{:S(2)}) async-start(f32[32,1,128]{2,1,0:T(1,128)} %bitcast.35), calls=%async_computation | async-start | bytes 32768 | tf_op jit(solution)/shard_map/all_to_all | solution.py:486
  28.9 0.1 mask.1
  29.0 0.6 collective-permute-done.2.far_ref
  29.7 0.0 collective-permute-done.1.near_ref
  29.7 0.7 copy-done.4
  30.3 0.0 copy-done.5
  30.3 5.1 %partial.1.unused_ref.field_ref = f32[128,512]{1,0:T(8,128)S(1)} custom-call(f32[4]{0:T(128)S(1)} %copy-done.4, f32[4]{0:T(128)S(1)} %copy-done.5, f32[1024,128]{1,0:T(8,128)S(1)} %get-tuple-element.20.own_ref, f32[512,128]{1,0:T(8,128)S(1)} %collective-permute-done.2.far_ref, f32[1024,128]{1,0:T(8,128)S(1)} %collective-permute-done.1.near_ref, ...), custom_call_target="tpu_custom_call" | custom-call | flops 99999997952 | tf_op jit(solution)/shard_map/partial/pallas_call | solution.py:499
  35.4 7.6 %all-to-all-done = f32[32,1,128]{2,1,0:T(1,128)S(1)} async-done(((f32[32,1,128]{2,1,0:T(1,128)}), f32[32,1,128]{2,1,0:T(1,128)S(1)}, u32[]{:S(2)}, u32[]{:S(2)}) %all-to-all-start) | async-done | bytes 16416 | tf_op jit(solution)/shard_map/all_to_all | solution.py:486
  43.0 15.0 %all_to_all.37 = f32[16,32,128]{2,1,0:T(8,128)S(1)} all-to-all(f32[16,32,128]{2,1,0:T(8,128)S(1)} %copies.1), channel_id=1, replica_groups=mesh['tile'=32,'mem'=16] {'mem'}, dimensions={0} | all-to-all | bytes 524288 | tf_op jit(solution)/shard_map/all_to_all | solution.py:513
  58.0 3.2 %interpolate.1 = (f32[128,512]{1,0:T(8,128)S(1)}, f32[4,16,512]{2,1,0:T(8,128)}) custom-call(f32[512,128]{1,0:T(8,128)S(1)} %bitcast.26, f32[128,512]{1,0:T(8,128)S(1)} %partial.1.unused_ref.field_ref), custom_call_target="tpu_custom_call" | custom-call | tf_op jit(solution)/shard_map/interpolate/pallas_call | solution.py:515
  61.2 3.5 %all-to-all-start.2 = ((f32[4,16,512]{2,1,0:T(8,128)}), f32[4,16,512]{2,1,0:T(8,128)S(1)}, u32[]{:S(2)}, u32[]{:S(2)}) async-start(f32[4,16,512]{2,1,0:T(8,128)} %get-tuple-element.24), calls=%async_computation.2 | async-start | bytes 262144 | tf_op jit(solution)/shard_map/all_to_all | solution.py:524
  64.6 0.0 copy-done.6
  64.7 5.4 %collective-permute-start = (f32[512,128]{1,0:T(8,128)S(1)}, f32[512,128]{1,0:T(8,128)S(1)}, u32[]{:S(2)}, u32[]{:S(2)}) collective-permute-start(f32[512,128]{1,0:T(8,128)S(1)} %copy-done.6), channel_id=1, source_target_pairs={{16,32},{48,64},{80,96},{112,128},{144,160},{176,192},{208,224},{2... | collective-permute-start | bytes 786440 | tf_op jit(solution)/shard_map/ppermute | solution.py:451
  70.1 0.0 all-to-all-done.2.in_ref
  70.1 7.2 %all_to_all.38.sums_ref = f32[4,16,512]{2,1,0:T(8,128)S(1)} all-to-all(f32[4,16,512]{2,1,0:T(8,128)S(1)} %add.1), channel_id=1, replica_groups={{0,4,8,12},{1,5,9,13},{2,6,10,14},{3,7,11,15},{16,20,24,28},{17,21,25,2..., dimensions={0} | all-to-all | bytes 262144 | tf_op jit(solution)/shard_map/all_to_all | solution.py:524
  77.3 3.2 %spread.1 = (f32[128,512]{1,0:T(8,128)S(1)}, f32[32,512]{1,0:T(8,128)S(1)}, f32[32,512]{1,0:T(8,128)S(1)}, f32[32,16]{1,0:T(8,128)}) custom-call(f32[512,128]{1,0:T(8,128)S(1)} %bitcast.27, f32[128,512]{1,0:T(8,128)S(1)} %get-tuple-element.23.comps_ref, f32[4,16,512]{2,1,0:T(8,128)S(1)} %all_to_all.38.sums_ref), custom_call_target="tpu_custom_call" | custom-call | tf_op jit(solution)/shard_map/spread/pallas_call | solution.py:528
  80.6 7.0 %collective-permute-start.3 = (f32[32,512]{1,0:T(8,128)S(1)}, f32[32,512]{1,0:T(8,128)S(1)}, u32[]{:S(2)}, u32[]{:S(2)}) collective-permute-start(f32[32,512]{1,0:T(8,128)S(1)} %get-tuple-element.26), channel_id=1, source_target_pairs={{16,32},{48,64},{80,96},{112,128},{144,160},{176,192},{208,224},{2... | collective-permute-start | bytes 196616 | tf_op jit(solution)/shard_map/ppermute | solution.py:451
  87.6 1.9 %collective-permute-start.4 = (f32[32,512]{1,0:T(8,128)S(1)}, f32[32,512]{1,0:T(8,128)S(1)}, u32[]{:S(2)}, u32[]{:S(2)}) collective-permute-start(f32[32,512]{1,0:T(8,128)S(1)} %get-tuple-element.27), channel_id=1, source_target_pairs={{0,16},{32,48},{64,80},{96,112},{128,144},{160,176},{192,208},{224... | collective-permute-start | bytes 196616 | tf_op jit(solution)/shard_map/ppermute | solution.py:454
  89.5 9.5 %all-to-all-start.4 = ((f32[32,1,16]{2,1,0:T(1,128)}), f32[32,1,16]{2,1,0:T(1,128)S(1)}, u32[]{:S(2)}, u32[]{:S(2)}) async-start(f32[32,1,16]{2,1,0:T(1,128)} %bitcast.19), calls=%async_computation.4 | async-start | bytes 32768 | tf_op jit(solution)/shard_map/all_to_all | solution.py:542
  99.0 0.0 collective-permute-done.far_ref
  99.0 0.0 collective-permute-done.3.adjoint_far_ref
  99.0 0.0 collective-permute-done.4.adjoint_near_ref
  99.0 5.4 %grad.1 = (f32[1024,128]{1,0:T(8,128)}, f32[8,128]{1,0:T(8,128)S(1)}) custom-call(f32[4]{0:T(128)S(1)} %copy-done.4, f32[4]{0:T(128)S(1)} %copy-done.5, f32[1024,128]{1,0:T(8,128)S(1)} %bitcast.30, s32[16,512]{1,0:T(8,128)S(1)} %copy-done.2, f32[1024,128]{1,0:T(8,128)S(1)} %get-tuple-element.17.members_ref, f32[512,128]{1,0:T(8,128)S(1)} %collective-permute-done.far_ref, ...), custom_call_target="tpu_custom_call" | custom-call | flops 99999997952 | tf_op jit(solution)/shard_map/grad/pallas_call | solution.py:544
  104.4 8.7 %all-to-all-done.4 = f32[32,1,16]{2,1,0:T(1,128)S(1)} async-done(((f32[32,1,16]{2,1,0:T(1,128)}), f32[32,1,16]{2,1,0:T(1,128)S(1)}, u32[]{:S(2)}, u32[]{:S(2)}) %all-to-all-start.4) | async-done | bytes 2080 | tf_op jit(solution)/shard_map/all_to_all | solution.py:542
  113.2 0.8 unpack.1
  (9 shorter events, 0.0 us)
Async XLA Ops:
  0.6 28.2 %copy-start = (f32[4,4,16,512]{3,2,1,0:T(8,128)S(1)}, f32[4,4,16,512]{3,2,1,0:T(8,128)}, u32[]{:S(2)}) copy-start(f32[4,4,16,512]{3,2,1,0:T(8,128)} %param.12) | copy-start | bytes 1572868
  0.6 28.2 %copy-start.1 = (bf16[4,4,16,512]{3,2,1,0:T(8,128)(2,1)S(1)}, bf16[4,4,16,512]{3,2,1,0:T(8,128)(2,1)}, u32[]{:S(2)}) copy-start(bf16[4,4,16,512]{3,2,1,0:T(8,128)(2,1)} %refs_1_.1) | copy-start | bytes 786436
  3.5 25.4 %copy-start.2 = (s32[16,512]{1,0:T(8,128)S(1)}, s32[16,512]{1,0:T(8,128)}, u32[]{:S(2)}) copy-start(s32[16,512]{1,0:T(8,128)} %land_ref.3) | copy-start | bytes 98308
  3.5 26.2 %collective-permute-start.1 = (f32[1024,128]{1,0:T(8,128)}, f32[1024,128]{1,0:T(8,128)S(1)}, u32[]{:S(2)}, u32[]{:S(2)}) collective-permute-start(f32[1024,128]{1,0:T(8,128)} %get-tuple-element.19), channel_id=1, source_target_pairs={{0,16},{32,48},{64,80},{96,112},{128,144},{160,176},{192,208},{224... | collective-permute-start | bytes 1572872 | tf_op jit(solution)/shard_map/ppermute | solution.py:454
  12.3 17.4 %collective-permute-start.2 = (f32[512,128]{1,0:T(8,128)}, f32[512,128]{1,0:T(8,128)S(1)}, u32[]{:S(2)}, u32[]{:S(2)}) collective-permute-start(f32[512,128]{1,0:T(8,128)} %get-tuple-element.21), channel_id=1, source_target_pairs={{16,32},{48,64},{80,96},{112,128},{144,160},{176,192},{208,224},{2... | collective-permute-start | bytes 786440 | tf_op jit(solution)/shard_map/ppermute | solution.py:451
  15.6 13.2 %copy-start.3 = (s32[256,1]{0,1:T(1,128)S(1)}, s32[256,1]{0,1:T(1,128)}, u32[]{:S(2)}) copy-start(s32[256,1]{0,1:T(1,128)} %param.17) | copy-start | bytes 3076
  15.6 27.4 %all-to-all-start = ((f32[32,1,128]{2,1,0:T(1,128)}), f32[32,1,128]{2,1,0:T(1,128)S(1)}, u32[]{:S(2)}, u32[]{:S(2)}) async-start(f32[32,1,128]{2,1,0:T(1,128)} %bitcast.35), calls=%async_computation | async-start | bytes 32768 | tf_op jit(solution)/shard_map/all_to_all | solution.py:486
  29.7 0.7 copy-start.4
  29.7 0.7 copy-start.5
  61.2 3.5 %copy-start.6 = (f32[512,128]{1,0:T(8,128)S(1)}, f32[512,128]{1,0:T(8,128)}, u32[]{:S(2)}) copy-start(f32[512,128]{1,0:T(8,128)} %get-tuple-element.18) | copy-start | bytes 786436
  61.2 8.9 %all-to-all-start.2 = ((f32[4,16,512]{2,1,0:T(8,128)}), f32[4,16,512]{2,1,0:T(8,128)S(1)}, u32[]{:S(2)}, u32[]{:S(2)}) async-start(f32[4,16,512]{2,1,0:T(8,128)} %get-tuple-element.24), calls=%async_computation.2 | async-start | bytes 262144 | tf_op jit(solution)/shard_map/all_to_all | solution.py:524
  64.7 34.4 %collective-permute-start = (f32[512,128]{1,0:T(8,128)S(1)}, f32[512,128]{1,0:T(8,128)S(1)}, u32[]{:S(2)}, u32[]{:S(2)}) collective-permute-start(f32[512,128]{1,0:T(8,128)S(1)} %copy-done.6), channel_id=1, source_target_pairs={{16,32},{48,64},{80,96},{112,128},{144,160},{176,192},{208,224},{2... | collective-permute-start | bytes 786440 | tf_op jit(solution)/shard_map/ppermute | solution.py:451
  80.6 18.4 %collective-permute-start.3 = (f32[32,512]{1,0:T(8,128)S(1)}, f32[32,512]{1,0:T(8,128)S(1)}, u32[]{:S(2)}, u32[]{:S(2)}) collective-permute-start(f32[32,512]{1,0:T(8,128)S(1)} %get-tuple-element.26), channel_id=1, source_target_pairs={{16,32},{48,64},{80,96},{112,128},{144,160},{176,192},{208,224},{2... | collective-permute-start | bytes 196616 | tf_op jit(solution)/shard_map/ppermute | solution.py:451
  87.6 11.4 %collective-permute-start.4 = (f32[32,512]{1,0:T(8,128)S(1)}, f32[32,512]{1,0:T(8,128)S(1)}, u32[]{:S(2)}, u32[]{:S(2)}) collective-permute-start(f32[32,512]{1,0:T(8,128)S(1)} %get-tuple-element.27), channel_id=1, source_target_pairs={{0,16},{32,48},{64,80},{96,112},{128,144},{160,176},{192,208},{224... | collective-permute-start | bytes 196616 | tf_op jit(solution)/shard_map/ppermute | solution.py:454
  89.5 23.7 %all-to-all-start.4 = ((f32[32,1,16]{2,1,0:T(1,128)}), f32[32,1,16]{2,1,0:T(1,128)S(1)}, u32[]{:S(2)}, u32[]{:S(2)}) async-start(f32[32,1,16]{2,1,0:T(1,128)} %bitcast.19), calls=%async_computation.4 | async-start | bytes 32768 | tf_op jit(solution)/shard_map/all_to_all | solution.py:542
